TPU v7x, 32 devices: a whole 2x2x4 slice. The times are simulated.
32 devices in a mesh: dict: 4 (over y, x), dp: 8 (over z, core).
Axes of the slice: x: 2, y: 2, z: 4, core: 2. Of those that a mesh axis runs over, the one named last changes fastest.
Arguments:
- activations: bfloat16 [2048, 3584], P('dp', 'dict'), may hold values from -6 to 6
- dictionary: bfloat16 [32768, 3584], P(('dict', 'dp')), may hold values from -0.09375 to 0.09375
- enc_bias: bfloat16 [32768], P(('dict', 'dp')), may hold values from -1.5 to 0
- dec_bias: float32 [3584], replicated, may hold values from -3 to 3
- block_codes: int32 [16, 4, 8], P('dp'), may hold values from -1 to 255, as said below
Outputs:
- error: bfloat16 [2048, 3584], P('dp', 'dict')
- grad_dict: float32 [32768, 3584], P(('dict', 'dp'))
- grad_enc_bias: float32 [32768], P(('dict', 'dp'))
Inputs may be any that keep to these rules, and one draw needn't show every extreme that they name: `block_codes`: entry [b, s, m] is either -1 (an empty slot) or a latent block of shard s, that is one of the blocks s * 64 upward. Block k is held by the dp index (k % 64) // 8. Every token block names exactly 32 blocks in all and at most 8 in one shard, reached in every draw; within one shard its blocks are held by distinct dp indices. All token blocks of one dp index that name a block held by the same dp index of the same shard name the same block.
All inputs are finite; a program needn't handle non-finite values.
Results may differ from a plain program's by a relative error of at most 0.012.
The roundings to bfloat16 on the way count: a program that leaves them out, or rounds other values in their place, can miss the bound.
Values may be sent and summed in bfloat16 or wider, within the bound.
No kernel may reach another device: no remote copies, remote signals or barrier semaphores. Data moves between devices by JAX's collectives and lax.ppermute only.
A program may use at most 128 MiB of HBM per device.

v0:
```python
import jax
import jax.numpy as jnp
from jax import lax
from jax.sharding import PartitionSpec as P

DICT_SPAN = 128
SAMPLE_SPAN = 128


def flat_dot(left, right):
    return lax.dot_general(
        left, right, (((1,), (1,)), ((), ())), preferred_element_type=jnp.float32
    )


def shards(activations, dictionary, enc_bias, dec_bias, block_codes):
    replica_total = lax.axis_size("dp")
    shard_index = lax.axis_index("dict")
    model_width = dictionary.shape[1]
    own_blocks = dictionary.shape[0] // DICT_SPAN
    shard_blocks = own_blocks * replica_total
    sample_matrix = activations.shape[0]
    gathered = lax.all_gather(activations, "dict", axis=1, tiled=True)
    my_codes = lax.dynamic_index_in_dim(block_codes, shard_index, axis=1, keepdims=False)
    filled = my_codes >= 0
    local_id = my_codes - shard_index * shard_blocks
    owning = jnp.where(filled, local_id // own_blocks, -1)
    inside = jnp.where(filled, local_id % own_blocks, -1)
    peer_ids = jnp.arange(replica_total, dtype=jnp.int32)
    matches = owning[:, :, None] == peer_ids
    selected_entries = jnp.any(matches, axis=1)
    wanted = jnp.max(jnp.where(matches, inside[:, :, None], -1), axis=(0, 1))
    asked = lax.all_to_all(wanted, "dp", split_axis=0, concat_axis=0, tiled=True)
    own_w = dictionary.reshape(own_blocks, DICT_SPAN, model_width)
    own_b = enc_bias.reshape(own_blocks, DICT_SPAN)
    picked = jnp.maximum(asked, 0)
    answered = asked >= 0
    send_w = jnp.where(answered[:, None, None], own_w[picked], jnp.zeros((), jnp.bfloat16))
    send_b = jnp.where(answered[:, None], own_b[picked], jnp.zeros((), jnp.bfloat16))
    got_w, got_b = (
        lax.all_to_all(send_w, "dp", split_axis=0, concat_axis=0, tiled=True),
        lax.all_to_all(send_b, "dp", split_axis=0, concat_axis=0, tiled=True),
    )
    slot_rows = replica_total * DICT_SPAN
    fetched = got_w.reshape(slot_rows, model_width)
    bias_flat = got_b.reshape(slot_rows).astype(jnp.float32)
    mean_removed = (gathered.astype(jnp.float32) - dec_bias).astype(jnp.bfloat16)
    preact = flat_dot(mean_removed, fetched) + bias_flat
    encoder_input_tiles = preact.reshape(sample_matrix, replica_total, DICT_SPAN)
    nonzero_indicator = jnp.repeat(selected_entries, SAMPLE_SPAN, axis=0)[:, :, None]
    hidden_activity = jnp.where(
        nonzero_indicator, jnp.maximum(encoder_input_tiles, 0.0), 0.0
    ).astype(jnp.bfloat16)
    partial_product = jnp.dot(
        hidden_activity.reshape(sample_matrix, slot_rows),
        fetched,
        preferred_element_type=jnp.float32,
    )
    summed = lax.psum(partial_product, "dict")
    error_full = (summed + dec_bias - gathered.astype(jnp.float32)).astype(jnp.bfloat16)
    share = model_width // lax.axis_size("dict")
    error_out = lax.dynamic_slice_in_dim(error_full, shard_index * share, share, 1)
    returned_entries = flat_dot(error_full, fetched)
    derivative_factor = jnp.where(
        nonzero_indicator & (encoder_input_tiles > 0),
        returned_entries.reshape(sample_matrix, replica_total, DICT_SPAN),
        0.0,
    ).astype(jnp.bfloat16)
    bias_terms = jnp.sum(derivative_factor.astype(jnp.float32), axis=0).astype(jnp.bfloat16)

    def block_grad(paired):
        latent_one, slope_one = paired
        first_term = lax.dot_general(
            latent_one, error_full, (((0,), (0,)), ((), ())), preferred_element_type=jnp.float32
        )
        second_term = lax.dot_general(
            slope_one, mean_removed, (((0,), (0,)), ((), ())), preferred_element_type=jnp.float32
        )
        return (first_term + second_term).astype(jnp.bfloat16)

    weight_terms = lax.map(
        block_grad, (jnp.swapaxes(hidden_activity, 0, 1), jnp.swapaxes(derivative_factor, 0, 1))
    )
    back_w, back_b = (
        lax.all_to_all(weight_terms, "dp", split_axis=0, concat_axis=0, tiled=True),
        lax.all_to_all(bias_terms, "dp", split_axis=0, concat_axis=0, tiled=True),
    )
    onehot = (asked[:, None] == jnp.arange(own_blocks, dtype=jnp.int32)).astype(jnp.bfloat16)
    grad_w = jnp.einsum("rk,rld->kld", onehot, back_w, preferred_element_type=jnp.float32)
    grad_b = jnp.einsum("rk,rl->kl", onehot, back_b, preferred_element_type=jnp.float32)
    return (
        error_out,
        grad_w.reshape(own_blocks * DICT_SPAN, model_width),
        grad_b.reshape(own_blocks * DICT_SPAN),
    )


def solution(mesh):
    in_specs = (
        P("dp", "dict"),
        P(("dict", "dp"), None),
        P(("dict", "dp")),
        P(),
        P("dp", None, None),
    )
    out_specs = (P("dp", "dict"), P(("dict", "dp"), None), P(("dict", "dp")))
    return jax.shard_map(shards, mesh=mesh, in_specs=in_specs, out_specs=out_specs, check_vma=False)
```

profile of v0, /device:TPU:0, one launch (start us, length us, event | category | flops | bytes accessed | tf_op | source)
XLA Modules:
  0.0 566.5 jit_solution(8718488875575083242)
XLA Ops:
  8.8 11.7 %all_to_all.40 = s32[8,1,1]{2,1,0:T(1,128)S(1)} all-to-all(s32[8,1,1]{2,1,0:T(1,128)S(1)} %copy.28), channel_id=1, replica_groups=mesh['dict'=4,'dp'=8] {'dp'}, dimensions={0} | all-to-all | bytes 64 | tf_op jit(solution)/shard_map/all_to_all | solution.py:33
  20.8 7.2 %gather_fusion = bf16[8,128,3584]{2,1,0:T(8,128)(2,1)} fusion(bf16[8,128,3584]{2,1,0:T(8,128)(2,1)} %bitcast.89, s32[1024]{0:T(1024)S(1)} %pad_clamp_fusion), kind=kCustom, calls=%fused_computation | custom fusion | bytes 14680096 | tf_op jit(solution)/shard_map/gather | solution.py:38
  29.2 3.3 all-to-all-start.2
  32.8 6.7 %broadcast_select_fusion = bf16[8,128,3584]{2,1,0:T(8,128)(2,1)} fusion(bf16[8,128,3584]{2,1,0:T(8,128)(2,1)} %gather_fusion, pred[8]{0:T(512)(128)(4,1)S(1)} %compare_reduce_fusion), kind=kLoop, calls=%fused_computation.15 | loop fusion | flops 3670016 | bytes 14680072 | tf_op jit(solution)/shard_map/jit(_where)/select_n | solution.py:38
  39.5 5.2 all-to-all-start.1
  45.6 36.4 %all-gather.2.cloned.1.call-done = bf16[256,3584]{1,0:T(8,128)(2,1)} async-done(((bf16[256,896]{1,0:T(8,128)(2,1)}), bf16[256,3584]{1,0:T(8,128)(2,1)}) %all-gather.2.cloned.1.call-update) | async-done | bytes 1835024 | tf_op jit(solution)/shard_map/all_gather | solution.py:23
  82.0 1.8 fusion.12
  83.8 122.4 %all-to-all-done.1 = bf16[8,128,3584]{2,1,0:T(8,128)(2,1)} async-done(((bf16[8,128,3584]{2,1,0:T(8,128)(2,1)}), bf16[8,128,3584]{2,1,0:T(8,128)(2,1)}, u32[]{:S(2)}, u32[]{:S(2)}) %all-to-all-start.1) | async-done | bytes 7340064 | tf_op jit(solution)/shard_map/all_to_all | solution.py:41
  206.2 5.2 convolution_add_fusion.1
  211.4 7.1 %convolution_bitcast_fusion = f32[256,3584]{1,0:T(8,128)} fusion(bf16[8,128,3584]{2,1,0:T(8,128)(2,1)} %all-to-all-done.1, pred[256,8]{0,1:T(8,128)(4,1)S(1)} %broadcast_bitcast_fusion, f32[256,1024]{1,0:T(8,128)S(1)} %convolution_add_fusion.1), kind=kOutput, calls=%fused_computation.16 | convolution fusion | flops 1879834624 | bytes 12060672 | tf_op jit(solution)/shard_map/dot_general | solution.py:54
  218.9 94.7 %all-reduce.2.cloned.1.call-done = f32[256,3584]{1,0:T(8,128)} async-done(((f32[256,3584]{1,0:T(8,128)}), f32[256,3584]{1,0:T(8,128)}) %all-reduce.2.cloned.1.call-update) | async-done | bytes 3670032 | tf_op jit(solution)/shard_map/psum | solution.py:59
  313.5 3.1 fusion.13
  316.6 6.1 %fusion.34 = (bf16[8,128]{1,0:T(8,128)(2,1)S(1)}, bf16[256,8,128]{2,0,1:T(8,128)(2,1)}) fusion(bf16[8,128,3584]{2,1,0:T(8,128)(2,1)} %all-to-all-done.1, bf16[256,3584]{1,0:T(8,128)(2,1)S(1)} %fusion.13, pred[256,8]{0,1:T(8,128)(4,1)S(1)} %broadcast_bitcast_fusion, f32[256,1024]{1,0:T(8,128)S(1)} %convolution_add_fusion.1), kind=kOutput, calls=%fused_computation.63 | convolution fusion | flops 1880357888 | bytes 10752000 | tf_op jit(solution)/shard_map/dot_general | solution.py:11
  323.3 4.6 all-to-all-start.4
  327.9 29.6 %while.11 = (s32[]{:T(128)}, bf16[8,128,3584]{2,1,0:T(8,128)(2,1)}, bf16[8,256,128]{2,1,0:T(8,128)(2,1)S(1)}, bf16[256,3584]{1,0:T(8,128)(2,1)S(1)}, bf16[8,256,128]{2,1,0:T(8,128)(2,1)}, /*index=5*/bf16[256,3584]{1,0:T(8,128)(2,1)}) while((s32[]{:T(128)}, bf16[8,128,3584]{2,1,0:T(8,128)(2,1)}, bf16[8,256,128]{2,1,0:T(8,128)(2,1)S(1)}, ...), condition=%wide.region_4.5_spmd.clone, body=%wide.region_3.4_spmd.sunk.clone | while | flops 470679552 | bytes 15729773 | solution.py:81
  329.4 2.2 fusion.58
  333.1 2.2 fusion.58
  335.7 1.1 copy-done.3
  336.8 2.2 fusion.58
  339.4 1.1 copy-done.3
  340.5 2.2 fusion.58
  344.2 2.2 fusion.58
  346.8 1.1 copy-done.3
  347.9 2.2 fusion.58
  350.5 1.1 copy-done.3
  351.6 2.2 fusion.58
  354.2 1.1 copy-done.3
  355.3 2.2 fusion.58
  357.5 5.1 all-to-all-start.3
  364.1 160.0 %all-to-all-done.3 = bf16[8,128,3584]{2,1,0:T(8,128)(2,1)} async-done(((bf16[8,128,3584]{2,1,0:T(8,128)(2,1)}), bf16[8,128,3584]{2,1,0:T(8,128)(2,1)}, u32[]{:S(2)}, u32[]{:S(2)}) %all-to-all-start.3) | async-done | bytes 7340064 | tf_op jit(solution)/shard_map/all_to_all | solution.py:85
  524.1 16.2 %fusion.10 = f32[8,128,3584]{2,0,1:T(8,128)} fusion(bf16[8,128,3584]{2,1,0:T(8,128)(2,1)} %all-to-all-done.3, s32[8]{0:T(128)S(1)} %get-tuple-element.36), kind=kOutput, calls=%fused_computation.13 | convolution fusion | flops 58720320 | bytes 22020128 | tf_op jit(solution)/shard_map/rk,rld->kld/dot_general | solution.py:89
  540.3 19.4 %copy.33 = f32[8,128,3584]{2,1,0:T(8,128)} copy(f32[8,128,3584]{2,0,1:T(8,128)} %fusion.10) | data formatting | bytes 29360128 | tf_op jit(solution)/shard_map/rk,rld->kld/dot_general | solution.py:89
  (53 shorter events, 13.5 us)
Async XLA Ops:
  7.2 20.8 %copy-start = (bf16[1024]{0:T(1024)(128)(2,1)S(1)}, bf16[1024]{0:T(1024)(128)(2,1)}, u32[]{:S(2)}) copy-start(bf16[1024]{0:T(1024)(128)(2,1)} %param.9) | copy-start | bytes 6148
  29.2 10.2 %all-to-all-start.2 = ((bf16[8,1,128]{2,1,0:T(2,128)(2,1)}), bf16[8,1,128]{2,1,0:T(2,128)(2,1)S(1)}, u32[]{:S(2)}, u32[]{:S(2)}) async-start(bf16[8,1,128]{2,1,0:T(2,128)(2,1)} %copy.29), calls=%async_computation.2 | async-start | bytes 8192 | tf_op jit(solution)/shard_map/all_to_all | solution.py:42
  39.5 42.5 %copy-start.4 = (f32[3584]{0:T(1024)S(1)}, f32[3584]{0:T(1024)}, u32[]{:S(2)}) copy-start(f32[3584]{0:T(1024)} %param.10) | copy-start | bytes 43012
  39.5 166.7 %all-to-all-start.1 = ((bf16[8,128,3584]{2,1,0:T(8,128)(2,1)}), bf16[8,128,3584]{2,1,0:T(8,128)(2,1)}, u32[]{:S(2)}, u32[]{:S(2)}) async-start(bf16[8,128,3584]{2,1,0:T(8,128)(2,1)} %broadcast_select_fusion), calls=%async_computation.1 | async-start | bytes 14680064 | tf_op jit(solution)/shard_map/all_to_all | solution.py:41
  44.6 37.3 %all-gather.2.cloned.1.call-start = ((), (), s32[]{:S(2)}) async-start(), calls=%async_computation.5 | async-start | bytes 2293760 | tf_op jit(solution)/shard_map/all_gather | solution.py:23
  45.4 268.2 %all-reduce.2.cloned.1.call-start = ((), (), s32[]{:S(2)}) async-start(), calls=%async_computation.6 | async-start | bytes 7340032 | tf_op jit(solution)/shard_map/psum | solution.py:59
  83.8 127.6 %copy-start.2 = (bf16[256,3584]{1,0:T(8,128)(2,1)}, bf16[256,3584]{1,0:T(8,128)(2,1)S(1)}, u32[]{:S(2)}) copy-start(bf16[256,3584]{1,0:T(8,128)(2,1)S(1)} %fusion.12) | copy-start | bytes 5505028
  323.3 34.2 %all-to-all-start.4 = ((bf16[8,1,128]{2,1,0:T(2,128)(2,1)}), bf16[8,1,128]{2,1,0:T(2,128)(2,1)S(1)}, u32[]{:S(2)}, u32[]{:S(2)}) async-start(bf16[8,1,128]{2,1,0:T(2,128)(2,1)} %copy.34), calls=%async_computation.4 | async-start | bytes 8192 | tf_op jit(solution)/shard_map/all_to_all | solution.py:86
  327.9 1.5 copy-start.3
  331.6 1.5 copy-start.3
  335.3 1.5 copy-start.3
  339.0 1.5 copy-start.3
  342.7 1.5 copy-start.3
  346.4 1.5 copy-start.3
  350.1 1.5 copy-start.3
  353.8 1.5 copy-start.3
  357.5 166.6 %all-to-all-start.3 = ((bf16[8,128,3584]{2,1,0:T(8,128)(2,1)}), bf16[8,128,3584]{2,1,0:T(8,128)(2,1)}, u32[]{:S(2)}, u32[]{:S(2)}) async-start(bf16[8,128,3584]{2,1,0:T(8,128)(2,1)} %get-tuple-element.35), calls=%async_computation.3 | async-start | bytes 14680064 | tf_op jit(solution)/shard_map/all_to_all | solution.py:85
  540.3 19.4 %copy-start.1 = (bf16[1024]{0:T(1024)(128)(2,1)S(1)}, bf16[1024]{0:T(1024)(128)(2,1)}, u32[]{:S(2)}) copy-start(bf16[1024]{0:T(1024)(128)(2,1)} %param.9) | copy-start | bytes 6148
Sparse Core Ops, SparseCore 0:
  47.3 34.6 all-gather.1
  218.6 94.8 all-reduce.1
where the time goes:
time: 568 us; the launch traced here: 567 us
  waiting for transfers between devices  414 us (73%)
  matrix products  56.3 us (10%)
  local copies, waits for them, and re-layouts  37.8 us (7%)
  starting transfers between devices  18.2 us (3%)
  other arithmetic  14.2 us (2%)
  between operations  14.1 us (2%)
  blocking collectives  11.7 us (2%)
    all_to_all x1, waiting for transfers between devices, shards(): lax.all_to_all(weight_terms, 'dp', split_axis=0, concat_axis=0, tiled=True)  160 us
    all_to_all x1, waiting for transfers between devices, shards(): lax.all_to_all(send_w, 'dp', split_axis=0, concat_axis=0, tiled=True)  122 us
    psum x1, waiting for transfers between devices, shards(): summed = lax.psum(partial_product, 'dict')  94.7 us
    all_gather x1, waiting for transfers between devices, shards(): gathered = lax.all_gather(activations, 'dict', axis=1, tiled=True)  36.4 us
    dot_general x1, local copies, waits for them, and re-layouts, shards(): jnp.einsum('rk,rld->kld', onehot, back_w, preferred_element_type=jnp.floa...  19.4 us
    dot_general x8, matrix products, block_grad(): lax.dot_general(slope_one, mean_removed, (((0,), (0,)), ((), ())), prefer...  17.6 us
    dot_general x1, matrix products, shards(): jnp.einsum('rk,rld->kld', onehot, back_w, preferred_element_type=jnp.floa...  16.2 us
    all_to_all x1, blocking collectives, shards(): lax.all_to_all(wanted, 'dp', split_axis=0, concat_axis=0, tiled=True)  11.7 us
  transfers between devices with their start and end apart: 6, of which 4 were waited for; matrix products, arithmetic and copies ran while one was open for 6% of the time, Pallas kernels for 0%

commit v1 on v0

v1 whole, which is shorter than its diff:
```python
import functools

import jax
import jax.numpy as jnp
from jax import lax
from jax.experimental import pallas as pl
from jax.experimental.pallas import tpu as pltpu
from jax.sharding import PartitionSpec as P

SPAN = 128
EXTRA = 16
VMEM_LIMIT = 48 * 1024 * 1024
BF = jnp.bfloat16
F32 = jnp.float32


def bits_of(slot):
    return [1 << b for b in range(slot.bit_length()) if slot >> b & 1]


def hop_bit(slot, half):
    bits = bits_of(slot)
    return bits[-1] if half == 0 else bits[0]


def over_dict(x, bit):
    n = lax.axis_size("dict")
    return lax.ppermute(x, "dict", [(i, i ^ bit) for i in range(n)])


def to_sibling(x):
    n = lax.axis_size("dp")
    return lax.ppermute(x, "dp", [(i, i ^ 1) for i in range(n)])


def along_ring(x):
    n = lax.axis_size("dp")
    return lax.ppermute(x, "dp", [(i, (i + 2) % n) for i in range(n)])


def gather_slots(own):
    n = lax.axis_size("dict")
    half = own.shape[0] // 2
    slots = {0: [own]}

    def rows(slot, h):
        pieces = slots[slot]
        if len(pieces) == 2:
            return pieces[h]
        return pieces[0][h * half : (h + 1) * half]

    for count in range(1, n.bit_length()):
        for slot in range(1, n):
            if slot.bit_count() != count:
                continue
            if count == 1:
                slots[slot] = [over_dict(own, slot)]
            else:
                slots[slot] = [
                    over_dict(rows(slot ^ hop_bit(slot, h), h), hop_bit(slot, h)) for h in (0, 1)
                ]
    return [slots[j] for j in range(n)]


def scatter_sum(parts):
    n = lax.axis_size("dict")
    acc = [list(p) for p in parts]
    for count in range(n.bit_length() - 1, 0, -1):
        moved = []
        for slot in range(1, n):
            if slot.bit_count() != count:
                continue
            for h in (0, 1):
                bit = hop_bit(slot, h)
                moved.append((slot ^ bit, h, over_dict(acc[slot][h].astype(BF), bit)))
        for slot, h, got in moved:
            acc[slot][h] = acc[slot][h].astype(F32) + got.astype(F32)
    return jnp.concatenate(acc[0], axis=0)


def nt_dot(a, b):
    return lax.dot_general(a, b, (((1,), (1,)), ((), ())), preferred_element_type=F32)


def fill_weights(w_refs, w_cat, fw):
    ns = len(w_refs) // 2
    for part in range(2):
        for j in range(ns):
            w_cat[part * SPAN : (part + 1) * SPAN, j * fw : (j + 1) * fw] = w_refs[part * ns + j][0]


def fill_rows(refs, layout, dst, fw, dec=None):
    for ref, (slot, row, count) in zip(refs, layout):
        cols = slice(slot * fw, (slot + 1) * fw)
        value = ref[...]
        if dec is not None:
            value = (value.astype(F32) - dec[:, cols]).astype(BF)
        dst[row : row + count, cols] = value


def fwd_kernel(layout, ns, fw, out_layout, meta, *refs):
    nx = len(layout)
    x_refs, refs = refs[:nx], refs[nx:]
    w_refs, refs = refs[: 2 * ns], refs[2 * ns :]
    dec, bias = refs[:2]
    lat_out = refs[2]
    outs = refs[3 : 3 + len(out_layout)]
    xc, wc = refs[3 + len(out_layout) :]
    fill_weights(w_refs, wc, fw)
    fill_rows(x_refs, layout, xc, fw, dec)
    preact = nt_dot(xc[...], wc[...]) + bias[...]
    tokens = preact.shape[0]
    for tb in range(tokens // SPAN):
        for part in range(2):
            cell = (slice(tb * SPAN, (tb + 1) * SPAN), slice(part * SPAN, (part + 1) * SPAN))
            named = jnp.full((SPAN, SPAN), meta[2 + 2 * tb + part], jnp.int32) > 0
            lat_out[cell] = jnp.where(named, jnp.maximum(preact[cell], 0.0), 0.0).astype(BF)
    lat = lat_out[...]
    for j in range(ns):
        recon = jnp.dot(lat, wc[:, j * fw : (j + 1) * fw], preferred_element_type=F32)
        for out, (slot, row, count) in zip(outs, out_layout):
            if slot == j:
                out[...] = recon[row : row + count].astype(out.dtype)


def bwd_kernel(x_layout, e_layout, ns, fw, meta, *refs):
    nx, ne = len(x_layout), len(e_layout)
    x_refs, refs = refs[:nx], refs[nx:]
    e_refs, refs = refs[:ne], refs[ne:]
    w_refs, refs = refs[: 2 * ns], refs[2 * ns :]
    dec, lat_ref, own_out, sib_out, xc, ec, wc = refs
    fill_weights(w_refs, wc, fw)
    fill_rows(e_refs, e_layout, ec, fw)
    fill_rows(x_refs, x_layout, xc, fw, dec)
    lat = lat_ref[...]
    back = nt_dot(ec[...], wc[...])
    slope = jnp.where(lat > 0, back, 0.0).astype(BF)
    bias = jnp.sum(slope.astype(F32), axis=0, keepdims=True).astype(BF)
    lat_t, slope_t = lat.T, slope.T
    for part, out in enumerate((own_out, sib_out)):
        out[SPAN:, :SPAN] = jnp.broadcast_to(bias[:, part * SPAN : (part + 1) * SPAN], (EXTRA, SPAN))
    for j in range(ns):
        cols = slice(j * fw, (j + 1) * fw)
        grad = jnp.dot(lat_t, ec[:, cols], preferred_element_type=F32) + jnp.dot(
            slope_t, xc[:, cols], preferred_element_type=F32
        )
        own_out[:SPAN, cols] = grad[:SPAN].astype(BF)
        sib_out[:SPAN, cols] = grad[SPAN:].astype(BF)


def sum_kernel(terms, meta, *refs):
    w_refs, b_refs = refs[:terms], refs[terms : 2 * terms]
    w_out, b_out = refs[2 * terms :]
    j, k = pl.program_id(0), pl.program_id(1)
    w_out[...] = jnp.zeros_like(w_out)
    for i in range(terms):

        @pl.when(meta[i] == k)
        def _(i=i):
            w_out[0] += w_refs[i][...].astype(F32)

    @pl.when((j == 0) & (k == 0))
    def _():
        b_out[...] = jnp.zeros_like(b_out)

    @pl.when(j == 0)
    def _():
        for i in range(terms):

            @pl.when(meta[i] == k)
            def _(i=i):
                b_out[pl.ds(k, 1)] += b_refs[i][0:1].astype(F32)[None]


def shards(activations, dictionary, enc_bias, dec_bias, block_codes):
    nd, npar = lax.axis_size("dict"), lax.axis_size("dp")
    nz = npar // 2
    s, d = lax.axis_index("dict"), lax.axis_index("dp")
    tokens, share = activations.shape
    width = dictionary.shape[1]
    own_blocks = dictionary.shape[0] // SPAN
    shard_blocks = own_blocks * npar
    ntb = block_codes.shape[0]
    aligned = share % SPAN == 0
    ns, fw = (nd, share) if aligned else (1, width)

    mine = lax.dynamic_index_in_dim(block_codes, s, axis=1, keepdims=False)
    codes = lax.all_gather(mine, "dp", axis=0, tiled=False)
    filled = codes >= 0
    local = codes - s * shard_blocks
    owner = jnp.where(filled, local // own_blocks, -1)
    inner = jnp.where(filled, local % own_blocks, -1)

    def pick(holder):
        match = owner == holder
        return jnp.max(jnp.where(match, inner, -1), axis=(1, 2)), jnp.any(match, axis=2).astype(jnp.int32)

    own_pick, own_named = pick(d)
    sib_pick, sib_named = pick(d ^ 1)

    order = s ^ jnp.arange(nd, dtype=jnp.int32)
    dec_rel = dec_bias.reshape(nd, share)[order].reshape(1, width)
    table = dictionary
    if not aligned:
        table = table.reshape(-1, nd, share)[:, order].reshape(-1, width)
    own_w = table.reshape(own_blocks, SPAN, width)
    sib_w = to_sibling(own_w)
    own_b = enc_bias.reshape(own_blocks, SPAN)
    sib_b = to_sibling(own_b)
    place = order if aligned else jnp.zeros((1,), jnp.int32)

    def meta_of(t):
        g = (d + 2 * (nz - t)) % npar
        safe = jnp.maximum(jnp.stack([own_pick[g], sib_pick[g]]), 0)
        named = jnp.stack([own_named[g], sib_named[g]], axis=1).reshape(-1)
        bias = jnp.concatenate([own_b[safe[0]], sib_b[safe[1]]]).astype(F32).reshape(1, 2 * SPAN)
        return jnp.concatenate([safe, named, place]), bias

    base = 2 + 2 * ntb

    def w_specs():
        return [
            pl.BlockSpec((1, SPAN, fw), lambda i, m, part=part, j=j: (m[part], 0, m[base + j]))
            for part in range(2)
            for j in range(ns)
        ]

    def whole(shape):
        return pl.BlockSpec(shape, lambda i, m: (0,) * len(shape))

    def flatten(slots):
        if not aligned:
            slots = [[jnp.concatenate(q, axis=0) if len(q) > 1 else q[0]] for q in slots]
            return [jnp.concatenate([q[0] for q in slots], axis=1)], [(0, 0, tokens)]
        pieces, layout = [], []
        for j, slot in enumerate(slots):
            row = 0
            for piece in slot:
                pieces.append(piece)
                layout.append((j, row, piece.shape[0]))
                row += piece.shape[0]
        return pieces, layout

    half = tokens // 2

    def forward(slots, meta, bias):
        pieces, layout = flatten(slots)
        if aligned:
            out_layout = [(j, h * half, half) for j in range(ns) for h in (0, 1)]
            dtypes = []
            for j in range(ns):
                for h in (0, 1):
                    fed = any(k & j == j and k.bit_count() == j.bit_count() + 1 and k ^ hop_bit(k, h) == j for k in range(1, nd))
                    dtypes.append(F32 if fed else BF)
        else:
            out_layout, dtypes = [(0, 0, tokens)], [F32]
        res = pl.pallas_call(
            functools.partial(fwd_kernel, layout, ns, fw, out_layout),
            grid_spec=pltpu.PrefetchScalarGridSpec(
                num_scalar_prefetch=1,
                grid=(1,),
                in_specs=[whole(p.shape) for p in pieces]
                + w_specs()
                + [whole((1, width)), whole((1, 2 * SPAN))],
                out_specs=[whole((tokens, 2 * SPAN))] + [whole((c, fw)) for _, _, c in out_layout],
                scratch_shapes=[pltpu.VMEM((tokens, width), BF), pltpu.VMEM((2 * SPAN, width), BF)],
            ),
            out_shape=[jax.ShapeDtypeStruct((tokens, 2 * SPAN), BF)]
            + [jax.ShapeDtypeStruct((c, fw), t) for (_, _, c), t in zip(out_layout, dtypes)],
            compiler_params=pltpu.CompilerParams(vmem_limit_bytes=VMEM_LIMIT),
            cost_estimate=pl.CostEstimate(
                flops=8 * tokens * SPAN * width, bytes_accessed=8 * tokens * width, transcendentals=0
            ),
        )(meta, *pieces, *([own_w] * ns), *([sib_w] * ns), dec_rel, bias)
        lat, outs = res[0], res[1:]
        if aligned:
            return lat, [[outs[2 * j], outs[2 * j + 1]] for j in range(nd)]
        full = outs[0].reshape(2, half, nd, share)
        return lat, [[full[h, :, j] for h in (0, 1)] for j in range(nd)]

    def backward(x_slots, e_slots, lat, meta):
        xp, xl = flatten(x_slots)
        ep, el = flatten(e_slots)
        rows = SPAN + EXTRA
        return pl.pallas_call(
            functools.partial(bwd_kernel, xl, el, ns, fw),
            grid_spec=pltpu.PrefetchScalarGridSpec(
                num_scalar_prefetch=1,
                grid=(1,),
                in_specs=[whole(p.shape) for p in xp + ep]
                + w_specs()
                + [whole((1, width)), whole((tokens, 2 * SPAN))],
                out_specs=[whole((rows, width))] * 2,
                scratch_shapes=[
                    pltpu.VMEM((tokens, width), BF),
                    pltpu.VMEM((tokens, width), BF),
                    pltpu.VMEM((2 * SPAN, width), BF),
                ],
            ),
            out_shape=[jax.ShapeDtypeStruct((rows, width), BF)] * 2,
            compiler_params=pltpu.CompilerParams(vmem_limit_bytes=VMEM_LIMIT),
            cost_estimate=pl.CostEstimate(
                flops=12 * tokens * SPAN * width, bytes_accessed=10 * tokens * width, transcendentals=0
            ),
        )(meta, *xp, *ep, *([own_w] * ns), *([sib_w] * ns), dec_rel, lat)

    metas = [meta_of(t) for t in range(nz)]
    own_x = [activations]
    for t in range(1, nz):
        own_x.append(along_ring(own_x[-1]))
    x_slots, lats, parts = [], [], []
    for t in range(nz):
        x_slots.append(gather_slots(own_x[t]))
        lat, part = forward(x_slots[t], *metas[t])
        lats.append(lat)
        parts.append(part)
    carry = None
    for t in list(range(1, nz)) + [0]:
        total = scatter_sum(parts[t])
        if carry is not None:
            total = total + along_ring(carry.astype(BF)).astype(F32)
        carry = total
    dec_own = lax.dynamic_slice_in_dim(dec_bias, s * share, share)
    error = (carry + dec_own - activations.astype(F32)).astype(BF)

    own_e = error
    own_terms, sib_terms = [], []
    for t in range(nz):
        if t:
            own_e = along_ring(own_e)
        mine_t, theirs = backward(x_slots[t], gather_slots(own_e), lats[t], metas[t][0])
        own_terms.append(mine_t)
        sib_terms.append(to_sibling(theirs))

    here = [(d + 2 * (nz - t)) % npar for t in range(nz)]
    which = jnp.stack([own_pick[g] for g in here] + [own_pick[g ^ 1] for g in here])
    terms = own_terms + sib_terms
    nt = len(terms)
    meta = jnp.concatenate([which, place])
    grad_w, grad_b = pl.pallas_call(
        functools.partial(sum_kernel, nt),
        grid_spec=pltpu.PrefetchScalarGridSpec(
            num_scalar_prefetch=1,
            grid=(ns, own_blocks),
            in_specs=[pl.BlockSpec((SPAN, fw), lambda j, k, m: (0, j))] * nt
            + [pl.BlockSpec((EXTRA, SPAN), lambda j, k, m: (SPAN // EXTRA, 0))] * nt,
            out_specs=[
                pl.BlockSpec((1, SPAN, fw), lambda j, k, m: (k, 0, m[nt + j])),
                pl.BlockSpec((own_blocks, 1, SPAN), lambda j, k, m: (0, 0, 0)),
            ],
        ),
        out_shape=[
            jax.ShapeDtypeStruct((own_blocks, SPAN, width), F32),
            jax.ShapeDtypeStruct((own_blocks, 1, SPAN), F32),
        ],
        compiler_params=pltpu.CompilerParams(vmem_limit_bytes=VMEM_LIMIT),
        cost_estimate=pl.CostEstimate(
            flops=nt * SPAN * width,
            bytes_accessed=2 * nt * SPAN * width + 4 * own_blocks * SPAN * width,
            transcendentals=0,
        ),
    )(meta, *terms, *terms)
    grad_w = grad_w.reshape(own_blocks * SPAN, width)
    if not aligned:
        grad_w = grad_w.reshape(-1, nd, share)[:, order].reshape(-1, width)
    return error, grad_w, grad_b.reshape(own_blocks * SPAN)


def solution(mesh):
    in_specs = (
        P("dp", "dict"),
        P(("dict", "dp"), None),
        P(("dict", "dp")),
        P(),
        P("dp", None, None),
    )
    out_specs = (P("dp", "dict"), P(("dict", "dp"), None), P(("dict", "dp")))
    return jax.shard_map(shards, mesh=mesh, in_specs=in_specs, out_specs=out_specs, check_vma=False)
```

time: 568 us -> 329 us (0.58)
  waiting for transfers between devices: 414 us -> 133 us
  Pallas kernels: 0 us -> 62.1 us
  matrix products: 56.3 us -> 0 us
  starting transfers between devices: 18.2 us -> 71.9 us
  local copies, waits for them, and re-layouts: 37.8 us -> 18.4 us
    all_to_all x4 -> x0, waiting for transfers between devices: 282 us -> none  [the longest x1 160 us: shards(): lax.all_to_all(weight_terms, 'dp', split_axis=0, concat_axis=0, tiled=True)]
    ppermute x0 -> x71, waiting for transfers between devices: none -> 133 us  [the longest x9 70.5 us: along_ring(): return lax.ppermute(x, 'dp', [(i, (i + 2) % n) for i in range(n)])]
    psum x1 -> x0, waiting for transfers between devices: 94.7 us -> none  [shards(): summed = lax.psum(partial_product, 'dict')]
    ppermute x0 -> x71, starting transfers between devices: none -> 71.9 us  [the longest x56 67.5 us: over_dict(): return lax.ppermute(x, 'dict', [(i, i ^ bit) for i in range(n)])]
    pallas_call x0 -> x9, Pallas kernels: none -> 62.1 us  [the longest x4 24.8 us: backward(): pl.pallas_call(functools.partial(bwd_kernel, xl, el, ns, fw), grid_spec=p...]
    dot_general x21 -> x0, matrix products: 56.3 us -> none  [the longest x8 17.6 us: block_grad(): lax.dot_general(slope_one, mean_removed, (((0,), (0,)), ((), ())), prefer...]
    all_gather x1 -> x0, waiting for transfers between devices: 36.4 us -> none  [shards(): gathered = lax.all_gather(activations, 'dict', axis=1, tiled=True)]
    dot_general x1 -> x0, local copies, waits for them, and re-layouts: 19.4 us -> none  [shards(): jnp.einsum('rk,rld->kld', onehot, back_w, preferred_element_type=jnp.floa...]
  transfers between devices with their start and end apart: 6 -> 71, of which waited for: 4 -> 22; matrix products, arithmetic and copies ran while one was open for 6% -> 7% of each run, Pallas kernels for 0% -> 13%
where the time goes in v1:
time: 329 us; the launch traced here: 328 us
  waiting for transfers between devices  133 us (40%)
  starting transfers between devices  71.9 us (22%)
  Pallas kernels  62.1 us (19%)
  local copies, waits for them, and re-layouts  18.4 us (6%)
  between operations  17.1 us (5%)
  blocking collectives  14.6 us (4%)
  other arithmetic  10.4 us (3%)
    ppermute x9, waiting for transfers between devices, along_ring(): return lax.ppermute(x, 'dp', [(i, (i + 2) % n) for i in range(n)])  70.5 us
    ppermute x56, starting transfers between devices, over_dict(): return lax.ppermute(x, 'dict', [(i, i ^ bit) for i in range(n)])  67.5 us
    ppermute x56, waiting for transfers between devices, over_dict(): return lax.ppermute(x, 'dict', [(i, i ^ bit) for i in range(n)])  62.8 us
    pallas_call x4, Pallas kernels, backward(): pl.pallas_call(functools.partial(bwd_kernel, xl, el, ns, fw), grid_spec=p...  24.8 us
    pallas_call x1, Pallas kernels, shards(): pl.pallas_call(functools.partial(sum_kernel, nt), grid_spec=pltpu.Prefetc...  19.2 us
    pallas_call x4, Pallas kernels, forward(): pl.pallas_call(functools.partial(fwd_kernel, layout, ns, fw, out_layout),...  18.1 us
    all_gather x1, blocking collectives, shards(): codes = lax.all_gather(mine, 'dp', axis=0, tiled=False)  14.6 us
  transfers between devices with their start and end apart: 71, of which 22 were waited for; matrix products, arithmetic and copies ran while one was open for 7% of the time, Pallas kernels for 13%

profile of v1, /device:TPU:0, one launch (start us, length us, event | category | flops | bytes accessed | tf_op | source)
XLA Modules:
  0.0 327.6 jit_solution(11452057114018384409)
XLA Ops:
  1.2 2.6 collective-permute-start.12
  6.8 14.6 %all-gather = s32[16,1,8]{2,1,0:T(1,128)S(1)} all-gather(s32[2,1,8]{2,1,0:T(1,128)S(1)} %constant_dynamic-slice_fusion.16), channel_id=2, replica_groups=mesh['dict'=4,'dp'=8] {'dp'}, dimensions={0}, use_global_device_ids=true | all-gather | bytes 576 | tf_op jit(solution)/shard_map/all_gather | solution.py:188
  29.6 12.3 %collective-permute-done.13.refs_0_ = bf16[256,896]{1,0:T(8,128)(2,1)} collective-permute-done((bf16[256,896]{1,0:T(8,128)(2,1)}, bf16[256,896]{1,0:T(8,128)(2,1)}, u32[]{:S(2)}, u32[]{:S(2)}) %collective-permute-start.13) | collective-permute-done | bytes 458784 | tf_op jit(solution)/shard_map/ppermute | solution.py:38
  49.8 6.1 %collective-permute-done.14.refs_0_ = bf16[256,896]{1,0:T(8,128)(2,1)} collective-permute-done((bf16[256,896]{1,0:T(8,128)(2,1)}, bf16[256,896]{1,0:T(8,128)(2,1)}, u32[]{:S(2)}, u32[]{:S(2)}) %collective-permute-start.14) | collective-permute-done | bytes 458784 | tf_op jit(solution)/shard_map/ppermute | solution.py:38
  83.2 3.3 %collective-permute-done.38.refs_4_ = bf16[128,896]{1,0:T(8,128)(2,1)S(1)} collective-permute-done((bf16[128,896]{1,0:T(8,128)(2,1)S(1)}, bf16[128,896]{1,0:T(8,128)(2,1)S(1)}, u32[]{:S(2)}, u32[]{:S(2)}) %collective-permute-start.38) | collective-permute-done | bytes 229408 | tf_op jit(solution)/shard_map/ppermute | solution.py:28
  87.6 3.7 %collective-permute-done.28.refs_4_ = bf16[128,896]{1,0:T(8,128)(2,1)S(1)} collective-permute-done((bf16[128,896]{1,0:T(8,128)(2,1)S(1)}, bf16[128,896]{1,0:T(8,128)(2,1)S(1)}, u32[]{:S(2)}, u32[]{:S(2)}) %collective-permute-start.28) | collective-permute-done | bytes 229408 | tf_op jit(solution)/shard_map/ppermute | solution.py:28
  92.5 4.5 %shard_map.79 = (bf16[256,256]{1,0:T(8,128)(2,1)S(1)}, f32[128,896]{1,0:T(8,128)S(1)}, f32[128,896]{1,0:T(8,128)S(1)}, f32[128,896]{1,0:T(8,128)S(1)}, bf16[128,...) custom-call(s32[10]{0:T(128)S(1)} %get-tuple-element.126.meta, ...), custom_call_target="tpu_custom_call" | custom-call | flops 939524096 | bytes 7340032 | tf_op jit(solution)/shard_map/pallas_call | solution.py:257
  98.6 4.6 %shard_map.78 = (bf16[256,256]{1,0:T(8,128)(2,1)S(1)}, f32[128,896]{1,0:T(8,128)S(1)}, f32[128,896]{1,0:T(8,128)S(1)}, f32[128,896]{1,0:T(8,128)S(1)}, bf16[128,...) custom-call(s32[10]{0:T(128)S(1)} %get-tuple-element.128.meta, ...), custom_call_target="tpu_custom_call" | custom-call | flops 939524096 | bytes 7340032 | tf_op jit(solution)/shard_map/pallas_call | solution.py:257
  105.5 4.6 %shard_map.77 = (bf16[256,256]{1,0:T(8,128)(2,1)S(1)}, f32[128,896]{1,0:T(8,128)S(1)}, f32[128,896]{1,0:T(8,128)S(1)}, f32[128,896]{1,0:T(8,128)S(1)}, bf16[128,...) custom-call(s32[10]{0:T(128)S(1)} %get-tuple-element.127.meta, ...), custom_call_target="tpu_custom_call" | custom-call | flops 939524096 | bytes 7340032 | tf_op jit(solution)/shard_map/pallas_call | solution.py:257
  112.0 4.4 %shard_map.76 = (bf16[256,256]{1,0:T(8,128)(2,1)S(1)}, f32[128,896]{1,0:T(8,128)S(1)}, f32[128,896]{1,0:T(8,128)S(1)}, f32[128,896]{1,0:T(8,128)S(1)}, bf16[128,...) custom-call(s32[10]{0:T(128)S(1)} %add_add_fusion.meta, ...), custom_call_target="tpu_custom_call" | custom-call | flops 939524096 | bytes 7340032 | tf_op jit(solution)/shard_map/pallas_call | solution.py:257
  120.8 6.3 %collective-permute-done.33 = bf16[128,896]{1,0:T(8,128)(2,1)S(1)} collective-permute-done((bf16[128,896]{1,0:T(8,128)(2,1)S(1)}, bf16[128,896]{1,0:T(8,128)(2,1)S(1)}, u32[]{:S(2)}, u32[]{:S(2)}) %collective-permute-start.33) | collective-permute-done | bytes 229408 | tf_op jit(solution)/shard_map/ppermute | solution.py:28
  128.4 4.8 %collective-permute-done.19 = bf16[128,896]{1,0:T(8,128)(2,1)S(1)} collective-permute-done((bf16[128,896]{1,0:T(8,128)(2,1)S(1)}, bf16[128,896]{1,0:T(8,128)(2,1)S(1)}, u32[]{:S(2)}, u32[]{:S(2)}) %collective-permute-start.19) | collective-permute-done | bytes 229408 | tf_op jit(solution)/shard_map/ppermute | solution.py:28
  134.3 6.2 %collective-permute-done.23 = bf16[128,896]{1,0:T(8,128)(2,1)S(1)} collective-permute-done((bf16[128,896]{1,0:T(8,128)(2,1)S(1)}, bf16[128,896]{1,0:T(8,128)(2,1)S(1)}, u32[]{:S(2)}, u32[]{:S(2)}) %collective-permute-start.23) | collective-permute-done | bytes 229408 | tf_op jit(solution)/shard_map/ppermute | solution.py:28
  141.9 6.3 %collective-permute-done.6 = bf16[128,896]{1,0:T(8,128)(2,1)S(1)} collective-permute-done((bf16[128,896]{1,0:T(8,128)(2,1)S(1)}, bf16[128,896]{1,0:T(8,128)(2,1)S(1)}, u32[]{:S(2)}, u32[]{:S(2)}) %collective-permute-start.6) | collective-permute-done | bytes 229408 | tf_op jit(solution)/shard_map/ppermute | solution.py:28
  148.9 7.8 %collective-permute-done.10 = bf16[128,896]{1,0:T(8,128)(2,1)S(1)} collective-permute-done((bf16[128,896]{1,0:T(8,128)(2,1)S(1)}, bf16[128,896]{1,0:T(8,128)(2,1)S(1)}, u32[]{:S(2)}, u32[]{:S(2)}) %collective-permute-start.10) | collective-permute-done | bytes 229408 | tf_op jit(solution)/shard_map/ppermute | solution.py:28
  158.0 5.4 %collective-permute-done.40 = bf16[128,896]{1,0:T(8,128)(2,1)S(1)} collective-permute-done((bf16[128,896]{1,0:T(8,128)(2,1)S(1)}, bf16[128,896]{1,0:T(8,128)(2,1)S(1)}, u32[]{:S(2)}, u32[]{:S(2)}) %collective-permute-start.40) | collective-permute-done | bytes 229408 | tf_op jit(solution)/shard_map/ppermute | solution.py:28
  165.8 3.7 %collective-permute-done.44 = bf16[128,896]{1,0:T(8,128)(2,1)S(1)} collective-permute-done((bf16[128,896]{1,0:T(8,128)(2,1)S(1)}, bf16[128,896]{1,0:T(8,128)(2,1)S(1)}, u32[]{:S(2)}, u32[]{:S(2)}) %collective-permute-start.44) | collective-permute-done | bytes 229408 | tf_op jit(solution)/shard_map/ppermute | solution.py:28
  172.0 4.7 %collective-permute-done.30 = bf16[128,896]{1,0:T(8,128)(2,1)S(1)} collective-permute-done((bf16[128,896]{1,0:T(8,128)(2,1)S(1)}, bf16[128,896]{1,0:T(8,128)(2,1)S(1)}, u32[]{:S(2)}, u32[]{:S(2)}) %collective-permute-start.30) | collective-permute-done | bytes 229408 | tf_op jit(solution)/shard_map/ppermute | solution.py:28
  178.9 15.2 %collective-permute-done.45 = bf16[256,896]{1,0:T(8,128)(2,1)S(1)} collective-permute-done((bf16[256,896]{1,0:T(8,128)(2,1)S(1)}, bf16[256,896]{1,0:T(8,128)(2,1)S(1)}, u32[]{:S(2)}, u32[]{:S(2)}) %collective-permute-start.45) | collective-permute-done | bytes 458784 | tf_op jit(solution)/shard_map/ppermute | solution.py:38
  194.1 3.2 collective-permute-start.20
  205.5 7.5 %collective-permute-done.46 = bf16[256,896]{1,0:T(8,128)(2,1)S(1)} collective-permute-done((bf16[256,896]{1,0:T(8,128)(2,1)S(1)}, bf16[256,896]{1,0:T(8,128)(2,1)S(1)}, u32[]{:S(2)}, u32[]{:S(2)}) %collective-permute-start.46) | collective-permute-done | bytes 458784 | tf_op jit(solution)/shard_map/ppermute | solution.py:38
  213.4 13.0 %collective-permute-done.47 = bf16[256,896]{1,0:T(8,128)(2,1)S(1)} collective-permute-done((bf16[256,896]{1,0:T(8,128)(2,1)S(1)}, bf16[256,896]{1,0:T(8,128)(2,1)S(1)}, u32[]{:S(2)}, u32[]{:S(2)}) %collective-permute-start.47) | collective-permute-done | bytes 458784 | tf_op jit(solution)/shard_map/ppermute | solution.py:38
  226.7 10.3 %collective-permute-done.52.refs_5_ = bf16[256,896]{1,0:T(8,128)(2,1)S(1)} collective-permute-done((bf16[256,896]{1,0:T(8,128)(2,1)S(1)}, bf16[256,896]{1,0:T(8,128)(2,1)S(1)}, u32[]{:S(2)}, u32[]{:S(2)}) %collective-permute-start.52) | collective-permute-done | bytes 458784 | tf_op jit(solution)/shard_map/ppermute | solution.py:38
  236.9 2.6 collective-permute-start.49
  241.2 6.1 %collective-permute-done.57.refs_5_ = bf16[256,896]{1,0:T(8,128)(2,1)S(1)} collective-permute-done((bf16[256,896]{1,0:T(8,128)(2,1)S(1)}, bf16[256,896]{1,0:T(8,128)(2,1)S(1)}, u32[]{:S(2)}, u32[]{:S(2)}) %collective-permute-start.57) | collective-permute-done | bytes 458784 | tf_op jit(solution)/shard_map/ppermute | solution.py:38
  252.7 3.2 collective-permute-done.51.refs_9_
  272.7 6.1 %shard_map.80 = (bf16[144,3584]{1,0:T(8,128)(2,1)S(1)}, bf16[144,3584]{1,0:T(8,128)(2,1)}) custom-call(s32[10]{0:T(128)S(1)} %add_add_fusion.meta, bf16[256,896]{1,0:T(8,128)(2,1)S(1)} %copy-done.2, bf16[256,896]{1,0:T(8,128)(2,1)S(1)} %collective-permute-done.refs_1_, bf16[256,896]{1,0:T(8,128)(2,1)S(1)} %collective-permute-done.1.refs_2_, ...), custom_call_target="tpu_custom_call" | custom-call | flops 1409286144 | bytes 9175040 | tf_op jit(solution)/shard_map/pallas_call | solution.py:285
  279.4 6.2 %shard_map.81 = (bf16[144,3584]{1,0:T(8,128)(2,1)S(1)}, bf16[144,3584]{1,0:T(8,128)(2,1)}) custom-call(s32[10]{0:T(128)S(1)} %get-tuple-element.126.meta, bf16[256,896]{1,0:T(8,128)(2,1)} %collective-permute-done.12.refs_0_, bf16[256,896]{1,0:T(8,128)(2,1)S(1)} %copy-done.16, bf16[256,896]{1,0:T(8,128)(2,1)S(1)} %copy-done.8, ...), custom_call_target="tpu_custom_call" | custom-call | flops 1409286144 | bytes 9175040 | tf_op jit(solution)/shard_map/pallas_call | solution.py:285
  285.9 6.3 %shard_map.82 = (bf16[144,3584]{1,0:T(8,128)(2,1)S(1)}, bf16[144,3584]{1,0:T(8,128)(2,1)}) custom-call(s32[10]{0:T(128)S(1)} %get-tuple-element.128.meta, bf16[256,896]{1,0:T(8,128)(2,1)} %collective-permute-done.13.refs_0_, bf16[256,896]{1,0:T(8,128)(2,1)S(1)} %copy-done.14, bf16[256,896]{1,0:T(8,128)(2,1)S(1)} %copy-done.12, ...), custom_call_target="tpu_custom_call" | custom-call | flops 1409286144 | bytes 9175040 | tf_op jit(solution)/shard_map/pallas_call | solution.py:285
  293.4 6.3 %shard_map.83 = (bf16[144,3584]{1,0:T(8,128)(2,1)S(1)}, bf16[144,3584]{1,0:T(8,128)(2,1)}) custom-call(s32[10]{0:T(128)S(1)} %get-tuple-element.127.meta, bf16[256,896]{1,0:T(8,128)(2,1)} %collective-permute-done.14.refs_0_, bf16[256,896]{1,0:T(8,128)(2,1)} %collective-permute-done.15.refs_1_, bf16[256,896]{1,0:T(8,128)(2,1)S(1)} %copy-done.10, ...), custom_call_target="tpu_custom_call" | custom-call | flops 1409286144 | bytes 9175040 | tf_op jit(solution)/shard_map/pallas_call | solution.py:285
  300.9 5.1 %concatenate.80.meta = s32[12]{0:T(128)S(1)} concatenate(s32[1]{0:T(128)} %get-tuple-element.123, s32[1]{0:T(128)} %get-tuple-element.120, s32[1]{0:T(128)} %get-tuple-element.121, s32[1]{0:T(128)} %get-tuple-element.122, s32[1]{0:T(128)} %get-tuple-element.119, s32[1]{0:T(128)} %get-tuple-element.118, s32[1]{0:T(128)} %get-tuple-element.117, s32[1]{0:T(128)} %get-tuple-element.116, ...), dimensions={0} | concatenate | bytes 96 | tf_op jit(solution)/shard_map/concatenate | solution.py:339
  308.5 19.2 %shard_map.84 = (f32[8,128,3584]{2,1,0:T(8,128)}, f32[8,1,128]{2,1,0:T(1,128)}) custom-call(s32[12]{0:T(128)S(1)} %concatenate.80.meta, bf16[144,3584]{1,0:T(8,128)(2,1)S(1)} %get-tuple-element.82.refs_0_.refs_8_, bf16[144,3584]{1,0:T(8,128)(2,1)S(1)} %get-tuple-element.84.refs_1_.refs_9_, bf16[144,3584]{1,0:T(8,128)(2,1)S(1)} %copy-done.4, ...), custom_call_target="tpu_custom_call" | custom-call | flops 3670016 | bytes 22020096 | tf_op jit(solution)/shard_map/pallas_call | solution.py:340
  (245 shorter events, 94.5 us)
Async XLA Ops:
  0.6 91.2 %collective-permute-start.4 = (bf16[8,128,3584]{2,1,0:T(8,128)(2,1)}, bf16[8,128,3584]{2,1,0:T(8,128)(2,1)}, u32[]{:S(2)}, u32[]{:S(2)}) collective-permute-start(bf16[8,128,3584]{2,1,0:T(8,128)(2,1)} %bitcast.43), channel_id=1, source_target_pairs={{0,1},{1,0},{2,3},{3,2},{4,5},{5,4},{6,7},{7,6},{8,9},{9,8},{10,11... | collective-permute-start | bytes 22020104 | tf_op jit(solution)/shard_map/ppermute | solution.py:33
  1.2 25.8 %collective-permute-start.12 = (bf16[256,896]{1,0:T(8,128)(2,1)}, bf16[256,896]{1,0:T(8,128)(2,1)}, u32[]{:S(2)}, u32[]{:S(2)}) collective-permute-start(bf16[256,896]{1,0:T(8,128)(2,1)} %refs_0_.3), channel_id=1, source_target_pairs={{0,2},{1,3},{2,4},{3,5},{4,6},{5,7},{6,0},{7,1},{8,10},{9,11},{10,... | collective-permute-start | bytes 1376264 | tf_op jit(solution)/shard_map/ppermute | solution.py:38
  3.8 39.4 %collective-permute-start.1 = (bf16[256,896]{1,0:T(8,128)(2,1)}, bf16[256,896]{1,0:T(8,128)(2,1)S(1)}, u32[]{:S(2)}, u32[]{:S(2)}) collective-permute-start(bf16[256,896]{1,0:T(8,128)(2,1)} %refs_0_.3), channel_id=1, source_target_pairs={{0,16},{8,24},{16,0},{24,8},{1,17},{9,25},{17,1},{25,9},{2,18},{10... | collective-permute-start | bytes 1376264 | tf_op jit(solution)/shard_map/ppermute | solution.py:28
  5.3 41.9 %collective-permute-start = (bf16[256,896]{1,0:T(8,128)(2,1)}, bf16[256,896]{1,0:T(8,128)(2,1)S(1)}, u32[]{:S(2)}, u32[]{:S(2)}) collective-permute-start(bf16[256,896]{1,0:T(8,128)(2,1)} %refs_0_.3), channel_id=1, source_target_pairs={{0,8},{8,0},{16,24},{24,16},{1,9},{9,1},{17,25},{25,17},{2,10},{10... | collective-permute-start | bytes 1376264 | tf_op jit(solution)/shard_map/ppermute | solution.py:28
  6.8 21.1 %collective-permute-start.5 = (bf16[8,128]{1,0:T(8,128)(2,1)}, bf16[8,128]{1,0:T(8,128)(2,1)S(1)}, u32[]{:S(2)}, u32[]{:S(2)}) collective-permute-start(bf16[8,128]{1,0:T(8,128)(2,1)} %bitcast.79), channel_id=1, source_target_pairs={{0,1},{1,0},{2,3},{3,2},{4,5},{5,4},{6,7},{7,6},{8,9},{9,8},{10,11... | collective-permute-start | bytes 6152 | tf_op jit(solution)/shard_map/ppermute | solution.py:33
  27.0 14.9 %collective-permute-start.13 = (bf16[256,896]{1,0:T(8,128)(2,1)}, bf16[256,896]{1,0:T(8,128)(2,1)}, u32[]{:S(2)}, u32[]{:S(2)}) collective-permute-start(bf16[256,896]{1,0:T(8,128)(2,1)} %collective-permute-done.12.refs_0_), channel_id=1, source_target_pairs={{0,2},{1,3},{2,4},{3,5},{4,6},{5,7},{6,0},{7,1},{8,10},{9,11},{10,... | collective-permute-start | bytes 1376264 | tf_op jit(solution)/shard_map/ppermute | solution.py:38
  28.0 20.7 %collective-permute-start.36 = (bf16[256,896]{1,0:T(8,128)(2,1)}, bf16[256,896]{1,0:T(8,128)(2,1)S(1)}, u32[]{:S(2)}, u32[]{:S(2)}) collective-permute-start(bf16[256,896]{1,0:T(8,128)(2,1)} %collective-permute-done.12.refs_0_), channel_id=1, source_target_pairs={{0,16},{8,24},{16,0},{24,8},{1,17},{9,25},{17,1},{25,9},{2,18},{10... | collective-permute-start | bytes 1376264 | tf_op jit(solution)/shard_map/ppermute | solution.py:28
  47.2 30.6 %collective-permute-start.26 = (bf16[256,896]{1,0:T(8,128)(2,1)}, bf16[256,896]{1,0:T(8,128)(2,1)S(1)}, u32[]{:S(2)}, u32[]{:S(2)}) collective-permute-start(bf16[256,896]{1,0:T(8,128)(2,1)} %collective-permute-done.13.refs_0_), channel_id=1, source_target_pairs={{0,16},{8,24},{16,0},{24,8},{1,17},{9,25},{17,1},{25,9},{2,18},{10... | collective-permute-start | bytes 1376264 | tf_op jit(solution)/shard_map/ppermute | solution.py:28
  48.7 29.7 %collective-permute-start.25 = (bf16[256,896]{1,0:T(8,128)(2,1)}, bf16[256,896]{1,0:T(8,128)(2,1)S(1)}, u32[]{:S(2)}, u32[]{:S(2)}) collective-permute-start(bf16[256,896]{1,0:T(8,128)(2,1)} %collective-permute-done.13.refs_0_), channel_id=1, source_target_pairs={{0,8},{8,0},{16,24},{24,16},{1,9},{9,1},{17,25},{25,17},{2,10},{10... | collective-permute-start | bytes 1376264 | tf_op jit(solution)/shard_map/ppermute | solution.py:28
  55.9 23.3 %collective-permute-start.16 = (bf16[256,896]{1,0:T(8,128)(2,1)}, bf16[256,896]{1,0:T(8,128)(2,1)S(1)}, u32[]{:S(2)}, u32[]{:S(2)}) collective-permute-start(bf16[256,896]{1,0:T(8,128)(2,1)} %collective-permute-done.14.refs_0_), channel_id=1, source_target_pairs={{0,16},{8,24},{16,0},{24,8},{1,17},{9,25},{17,1},{25,9},{2,18},{10... | collective-permute-start | bytes 1376264 | tf_op jit(solution)/shard_map/ppermute | solution.py:28
  57.6 23.1 %collective-permute-start.15 = (bf16[256,896]{1,0:T(8,128)(2,1)}, bf16[256,896]{1,0:T(8,128)(2,1)}, u32[]{:S(2)}, u32[]{:S(2)}) collective-permute-start(bf16[256,896]{1,0:T(8,128)(2,1)} %collective-permute-done.14.refs_0_), channel_id=1, source_target_pairs={{0,8},{8,0},{16,24},{24,16},{1,9},{9,1},{17,25},{25,17},{2,10},{10... | collective-permute-start | bytes 1376264 | tf_op jit(solution)/shard_map/ppermute | solution.py:28
  80.8 16.3 %collective-permute-start.27 = (bf16[128,896]{1,0:T(8,128)(2,1)S(1)}, bf16[128,896]{1,0:T(8,128)(2,1)S(1)}, u32[]{:S(2)}, u32[]{:S(2)}) collective-permute-start(bf16[128,896]{1,0:T(8,128)(2,1)S(1)} %slice.102), channel_id=1, source_target_pairs={{0,16},{8,24},{16,0},{24,8},{1,17},{9,25},{17,1},{25,9},{2,18},{10... | collective-permute-start | bytes 688136 | tf_op jit(solution)/shard_map/ppermute | solution.py:28
  86.4 16.7 %collective-permute-start.18 = (bf16[128,896]{1,0:T(8,128)(2,1)S(1)}, bf16[128,896]{1,0:T(8,128)(2,1)S(1)}, u32[]{:S(2)}, u32[]{:S(2)}) collective-permute-start(bf16[128,896]{1,0:T(8,128)(2,1)S(1)} %slice.101), channel_id=1, source_target_pairs={{0,8},{8,0},{16,24},{24,16},{1,9},{9,1},{17,25},{25,17},{2,10},{10... | collective-permute-start | bytes 688136 | tf_op jit(solution)/shard_map/ppermute | solution.py:28
  87.0 16.8 %collective-permute-start.17 = (bf16[128,896]{1,0:T(8,128)(2,1)S(1)}, bf16[128,896]{1,0:T(8,128)(2,1)S(1)}, u32[]{:S(2)}, u32[]{:S(2)}) collective-permute-start(bf16[128,896]{1,0:T(8,128)(2,1)S(1)} %slice.100), channel_id=1, source_target_pairs={{0,16},{8,24},{16,0},{24,8},{1,17},{9,25},{17,1},{25,9},{2,18},{10... | collective-permute-start | bytes 688136 | tf_op jit(solution)/shard_map/ppermute | solution.py:28
  91.3 18.7 %collective-permute-start.3 = (bf16[128,896]{1,0:T(8,128)(2,1)S(1)}, bf16[128,896]{1,0:T(8,128)(2,1)S(1)}, u32[]{:S(2)}, u32[]{:S(2)}) collective-permute-start(bf16[128,896]{1,0:T(8,128)(2,1)S(1)} %slice.99), channel_id=1, source_target_pairs={{0,8},{8,0},{16,24},{24,16},{1,9},{9,1},{17,25},{25,17},{2,10},{10... | collective-permute-start | bytes 688136 | tf_op jit(solution)/shard_map/ppermute | solution.py:28
  91.9 18.6 %collective-permute-start.2 = (bf16[128,896]{1,0:T(8,128)(2,1)S(1)}, bf16[128,896]{1,0:T(8,128)(2,1)S(1)}, u32[]{:S(2)}, u32[]{:S(2)}) collective-permute-start(bf16[128,896]{1,0:T(8,128)(2,1)S(1)} %slice.98), channel_id=1, source_target_pairs={{0,16},{8,24},{16,0},{24,8},{1,17},{9,25},{17,1},{25,9},{2,18},{10... | collective-permute-start | bytes 688136 | tf_op jit(solution)/shard_map/ppermute | solution.py:28
  97.1 19.4 %collective-permute-start.39 = (bf16[128,896]{1,0:T(8,128)(2,1)S(1)}, bf16[128,896]{1,0:T(8,128)(2,1)}, u32[]{:S(2)}, u32[]{:S(2)}) collective-permute-start(bf16[128,896]{1,0:T(8,128)(2,1)S(1)} %get-tuple-element.75), channel_id=1, source_target_pairs={{0,16},{8,24},{16,0},{24,8},{1,17},{9,25},{17,1},{25,9},{2,18},{10... | collective-permute-start | bytes 688136 | tf_op jit(solution)/shard_map/ppermute | solution.py:28
  103.2 54.1 %collective-permute-start.41 = (bf16[128,896]{1,0:T(8,128)(2,1)S(1)}, bf16[128,896]{1,0:T(8,128)(2,1)}, u32[]{:S(2)}, u32[]{:S(2)}) collective-permute-start(bf16[128,896]{1,0:T(8,128)(2,1)S(1)} %get-tuple-element.76), channel_id=1, source_target_pairs={{0,16},{8,24},{16,0},{24,8},{1,17},{9,25},{17,1},{25,9},{2,18},{10... | collective-permute-start | bytes 688136 | tf_op jit(solution)/shard_map/ppermute | solution.py:28
  103.8 61.9 %collective-permute-start.42 = (bf16[128,896]{1,0:T(8,128)(2,1)S(1)}, bf16[128,896]{1,0:T(8,128)(2,1)}, u32[]{:S(2)}, u32[]{:S(2)}) collective-permute-start(bf16[128,896]{1,0:T(8,128)(2,1)S(1)} %get-tuple-element.78), channel_id=1, source_target_pairs={{0,8},{8,0},{16,24},{24,16},{1,9},{9,1},{17,25},{25,17},{2,10},{10... | collective-permute-start | bytes 688136 | tf_op jit(solution)/shard_map/ppermute | solution.py:28
  116.4 54.3 %collective-permute-start.31 = (bf16[128,896]{1,0:T(8,128)(2,1)S(1)}, bf16[128,896]{1,0:T(8,128)(2,1)S(1)}, u32[]{:S(2)}, u32[]{:S(2)}) collective-permute-start(bf16[128,896]{1,0:T(8,128)(2,1)S(1)} %get-tuple-element.68), channel_id=1, source_target_pairs={{0,16},{8,24},{16,0},{24,8},{1,17},{9,25},{17,1},{25,9},{2,18},{10... | collective-permute-start | bytes 688136 | tf_op jit(solution)/shard_map/ppermute | solution.py:28
  118.6 58.2 %collective-permute-start.32 = (bf16[128,896]{1,0:T(8,128)(2,1)S(1)}, bf16[128,896]{1,0:T(8,128)(2,1)S(1)}, u32[]{:S(2)}, u32[]{:S(2)}) collective-permute-start(bf16[128,896]{1,0:T(8,128)(2,1)S(1)} %get-tuple-element.70), channel_id=1, source_target_pairs={{0,8},{8,0},{16,24},{24,16},{1,9},{9,1},{17,25},{25,17},{2,10},{10... | collective-permute-start | bytes 688136 | tf_op jit(solution)/shard_map/ppermute | solution.py:28
  157.3 40.2 %collective-permute-start.21 = (bf16[128,896]{1,0:T(8,128)(2,1)S(1)}, bf16[128,896]{1,0:T(8,128)(2,1)S(1)}, u32[]{:S(2)}, u32[]{:S(2)}) collective-permute-start(bf16[128,896]{1,0:T(8,128)(2,1)S(1)} %get-tuple-element.60), channel_id=1, source_target_pairs={{0,16},{8,24},{16,0},{24,8},{1,17},{9,25},{17,1},{25,9},{2,18},{10... | collective-permute-start | bytes 688136 | tf_op jit(solution)/shard_map/ppermute | solution.py:28
  165.7 35.8 %collective-permute-start.22 = (bf16[128,896]{1,0:T(8,128)(2,1)S(1)}, bf16[128,896]{1,0:T(8,128)(2,1)S(1)}, u32[]{:S(2)}, u32[]{:S(2)}) collective-permute-start(bf16[128,896]{1,0:T(8,128)(2,1)S(1)} %get-tuple-element.62), channel_id=1, source_target_pairs={{0,8},{8,0},{16,24},{24,16},{1,9},{9,1},{17,25},{25,17},{2,10},{10... | collective-permute-start | bytes 688136 | tf_op jit(solution)/shard_map/ppermute | solution.py:28
  176.7 17.4 %collective-permute-start.45 = (bf16[256,896]{1,0:T(8,128)(2,1)S(1)}, bf16[256,896]{1,0:T(8,128)(2,1)S(1)}, u32[]{:S(2)}, u32[]{:S(2)}) collective-permute-start(bf16[256,896]{1,0:T(8,128)(2,1)S(1)} %pad_maximum_fusion), channel_id=1, source_target_pairs={{0,2},{1,3},{2,4},{3,5},{4,6},{5,7},{6,0},{7,1},{8,10},{9,11},{10,... | collective-permute-start | bytes 1376264 | tf_op jit(solution)/shard_map/ppermute | solution.py:38
  176.8 36.4 %collective-permute-start.8 = (bf16[128,896]{1,0:T(8,128)(2,1)S(1)}, bf16[128,896]{1,0:T(8,128)(2,1)S(1)}, u32[]{:S(2)}, u32[]{:S(2)}) collective-permute-start(bf16[128,896]{1,0:T(8,128)(2,1)S(1)} %get-tuple-element.52), channel_id=1, source_target_pairs={{0,16},{8,24},{16,0},{24,8},{1,17},{9,25},{17,1},{25,9},{2,18},{10... | collective-permute-start | bytes 688136 | tf_op jit(solution)/shard_map/ppermute | solution.py:28
  177.7 35.6 %collective-permute-start.9 = (bf16[128,896]{1,0:T(8,128)(2,1)S(1)}, bf16[128,896]{1,0:T(8,128)(2,1)S(1)}, u32[]{:S(2)}, u32[]{:S(2)}) collective-permute-start(bf16[128,896]{1,0:T(8,128)(2,1)S(1)} %get-tuple-element.54), channel_id=1, source_target_pairs={{0,8},{8,0},{16,24},{24,16},{1,9},{9,1},{17,25},{25,17},{2,10},{10... | collective-permute-start | bytes 688136 | tf_op jit(solution)/shard_map/ppermute | solution.py:28
  260.1 18.7 %collective-permute-start.63 = (bf16[256,896]{1,0:T(8,128)(2,1)S(1)}, bf16[256,896]{1,0:T(8,128)(2,1)S(1)}, u32[]{:S(2)}, u32[]{:S(2)}) collective-permute-start(bf16[256,896]{1,0:T(8,128)(2,1)S(1)} %collective-permute-done.62.refs_5_), channel_id=1, source_target_pairs={{0,8},{8,0},{16,24},{24,16},{1,9},{9,1},{17,25},{25,17},{2,10},{10... | collective-permute-start | bytes 1376264 | tf_op jit(solution)/shard_map/ppermute | solution.py:28
  261.9 17.0 %collective-permute-start.56 = (bf16[128,896]{1,0:T(8,128)(2,1)S(1)}, bf16[128,896]{1,0:T(8,128)(2,1)S(1)}, u32[]{:S(2)}, u32[]{:S(2)}) collective-permute-start(bf16[128,896]{1,0:T(8,128)(2,1)S(1)} %slice.109), channel_id=1, source_target_pairs={{0,8},{8,0},{16,24},{24,16},{1,9},{9,1},{17,25},{25,17},{2,10},{10... | collective-permute-start | bytes 688136 | tf_op jit(solution)/shard_map/ppermute | solution.py:28
  269.0 16.7 %collective-permute-start.61 = (bf16[128,896]{1,0:T(8,128)(2,1)S(1)}, bf16[128,896]{1,0:T(8,128)(2,1)S(1)}, u32[]{:S(2)}, u32[]{:S(2)}) collective-permute-start(bf16[128,896]{1,0:T(8,128)(2,1)S(1)} %slice.111), channel_id=1, source_target_pairs={{0,8},{8,0},{16,24},{24,16},{1,9},{9,1},{17,25},{25,17},{2,10},{10... | collective-permute-start | bytes 688136 | tf_op jit(solution)/shard_map/ppermute | solution.py:28
  270.6 15.2 %collective-permute-start.60 = (bf16[128,896]{1,0:T(8,128)(2,1)S(1)}, bf16[128,896]{1,0:T(8,128)(2,1)S(1)}, u32[]{:S(2)}, u32[]{:S(2)}) collective-permute-start(bf16[128,896]{1,0:T(8,128)(2,1)S(1)} %slice.110), channel_id=1, source_target_pairs={{0,16},{8,24},{16,0},{24,8},{1,17},{9,25},{17,1},{25,9},{2,18},{10... | collective-permute-start | bytes 688136 | tf_op jit(solution)/shard_map/ppermute | solution.py:28
  278.8 27.2 %collective-permute-start.67 = (bf16[144,3584]{1,0:T(8,128)(2,1)}, bf16[144,3584]{1,0:T(8,128)(2,1)S(1)}, u32[]{:S(2)}, u32[]{:S(2)}) collective-permute-start(bf16[144,3584]{1,0:T(8,128)(2,1)} %get-tuple-element.89), channel_id=1, source_target_pairs={{0,1},{1,0},{2,3},{3,2},{4,5},{5,4},{6,7},{7,6},{8,9},{9,8},{10,11... | collective-permute-start | bytes 3096584 | tf_op jit(solution)/shard_map/ppermute | solution.py:33
  285.6 20.3 %collective-permute-start.68 = (bf16[144,3584]{1,0:T(8,128)(2,1)}, bf16[144,3584]{1,0:T(8,128)(2,1)}, u32[]{:S(2)}, u32[]{:S(2)}) collective-permute-start(bf16[144,3584]{1,0:T(8,128)(2,1)} %get-tuple-element.90), channel_id=1, source_target_pairs={{0,1},{1,0},{2,3},{3,2},{4,5},{5,4},{6,7},{7,6},{8,9},{9,8},{10,11... | collective-permute-start | bytes 3096584 | tf_op jit(solution)/shard_map/ppermute | solution.py:33
  (61 other events, 690.9 us)

commit v2 on v1

--- a/solution.py
+++ b/solution.py
@@ -9,18 +9,28 @@
 
 SPAN = 128
 EXTRA = 16
-VMEM_LIMIT = 48 * 1024 * 1024
+VMEM_LIMIT = 30 * 1024 * 1024
 BF = jnp.bfloat16
 F32 = jnp.float32
 
 
-def bits_of(slot):
-    return [1 << b for b in range(slot.bit_length()) if slot >> b & 1]
-
-
 def hop_bit(slot, half):
-    bits = bits_of(slot)
-    return bits[-1] if half == 0 else bits[0]
+    return 1 << (slot.bit_length() - 1) if half == 0 else slot & -slot
+
+
+class Steps:
+    def __init__(self):
+        self.done = []
+
+    def send(self, items, after=()):
+        held = list(after) + (self.done[-2] if len(self.done) > 1 else [])
+        out = []
+        for x, bit in items:
+            if held:
+                x = lax.optimization_barrier((x, *held))[0]
+            out.append(over_dict(x, bit))
+        self.done.append(out)
+        return out
 
 
 def over_dict(x, bit):
@@ -38,44 +48,64 @@
     return lax.ppermute(x, "dp", [(i, (i + 2) % n) for i in range(n)])
 
 
-def gather_slots(own):
+def gather_level(slots, count, mode):
     n = lax.axis_size("dict")
-    half = own.shape[0] // 2
-    slots = {0: [own]}
-
-    def rows(slot, h):
-        pieces = slots[slot]
-        if len(pieces) == 2:
-            return pieces[h]
-        return pieces[0][h * half : (h + 1) * half]
-
-    for count in range(1, n.bit_length()):
-        for slot in range(1, n):
-            if slot.bit_count() != count:
-                continue
-            if count == 1:
-                slots[slot] = [over_dict(own, slot)]
-            else:
-                slots[slot] = [
-                    over_dict(rows(slot ^ hop_bit(slot, h), h), hop_bit(slot, h)) for h in (0, 1)
-                ]
-    return [slots[j] for j in range(n)]
-
-
-def scatter_sum(parts):
-    n = lax.axis_size("dict")
-    acc = [list(p) for p in parts]
-    for count in range(n.bit_length() - 1, 0, -1):
-        moved = []
-        for slot in range(1, n):
-            if slot.bit_count() != count:
-                continue
+    items, keys = [], []
+    for slot in range(1, n):
+        if slot.bit_count() != count:
+            continue
+        if count == 1 or mode < 2:
+            bit = hop_bit(slot, mode % 2)
+            source = slots[slot ^ bit]
+            items.append((source[0] if len(source) == 1 else jnp.concatenate(source, axis=0), bit))
+            keys.append((slot, 0))
+        else:
             for h in (0, 1):
                 bit = hop_bit(slot, h)
-                moved.append((slot ^ bit, h, over_dict(acc[slot][h].astype(BF), bit)))
-        for slot, h, got in moved:
-            acc[slot][h] = acc[slot][h].astype(F32) + got.astype(F32)
-    return jnp.concatenate(acc[0], axis=0)
+                source = slots[slot ^ bit]
+                if len(source) == 1:
+                    half = source[0].shape[0] // 2
+                    items.append((source[0][h * half : (h + 1) * half], bit))
+                else:
+                    items.append((source[h], bit))
+                keys.append((slot, h))
+    return items, keys
+
+
+def gather_store(slots, keys, got):
+    for (slot, _), x in zip(keys, got):
+        slots.setdefault(slot, []).append(x)
+
+
+def scatter_level(acc, count):
+    n = lax.axis_size("dict")
+    items, keys = [], []
+    for slot in range(1, n):
+        if slot.bit_count() != count:
+            continue
+        if len(acc[slot]) == 1:
+            bit = slot
+            items.append((acc[slot][0].astype(BF), bit))
+            keys.append((0, None))
+        else:
+            for h in (0, 1):
+                bit = hop_bit(slot, h)
+                items.append((acc[slot][h].astype(BF), bit))
+                keys.append((slot ^ bit, h))
+    return items, keys
+
+
+def scatter_store(acc, keys, got):
+    for (slot, h), x in zip(keys, got):
+        x = x.astype(F32)
+        if h is None:
+            acc[slot] = [acc[slot][0] + x]
+        elif len(acc[slot]) == 2:
+            acc[slot][h] = acc[slot][h] + x
+        else:
+            half = x.shape[0]
+            grow = ((0, half), (0, 0)) if h == 0 else ((half, 0), (0, 0))
+            acc[slot] = [acc[slot][0] + jnp.pad(x, grow)]
 
 
 def nt_dot(a, b):
@@ -102,19 +132,19 @@
     nx = len(layout)
     x_refs, refs = refs[:nx], refs[nx:]
     w_refs, refs = refs[: 2 * ns], refs[2 * ns :]
-    dec, bias = refs[:2]
-    lat_out = refs[2]
-    outs = refs[3 : 3 + len(out_layout)]
-    xc, wc = refs[3 + len(out_layout) :]
+    dec, own_bias, sib_bias, lat_out = refs[:4]
+    outs = refs[4 : 4 + len(out_layout)]
+    xc, wc = refs[4 + len(out_layout) :]
     fill_weights(w_refs, wc, fw)
     fill_rows(x_refs, layout, xc, fw, dec)
-    preact = nt_dot(xc[...], wc[...]) + bias[...]
+    preact = nt_dot(xc[...], wc[...])
+    biases = (own_bias[0].astype(F32), sib_bias[0].astype(F32))
     tokens = preact.shape[0]
     for tb in range(tokens // SPAN):
         for part in range(2):
             cell = (slice(tb * SPAN, (tb + 1) * SPAN), slice(part * SPAN, (part + 1) * SPAN))
             named = jnp.full((SPAN, SPAN), meta[2 + 2 * tb + part], jnp.int32) > 0
-            lat_out[cell] = jnp.where(named, jnp.maximum(preact[cell], 0.0), 0.0).astype(BF)
+            lat_out[cell] = jnp.where(named, jnp.maximum(preact[cell] + biases[part], 0.0), 0.0).astype(BF)
     lat = lat_out[...]
     for j in range(ns):
         recon = jnp.dot(lat, wc[:, j * fw : (j + 1) * fw], preferred_element_type=F32)
@@ -151,25 +181,23 @@
 def sum_kernel(terms, meta, *refs):
     w_refs, b_refs = refs[:terms], refs[terms : 2 * terms]
     w_out, b_out = refs[2 * terms :]
-    j, k = pl.program_id(0), pl.program_id(1)
     w_out[...] = jnp.zeros_like(w_out)
     for i in range(terms):
-
-        @pl.when(meta[i] == k)
-        def _(i=i):
-            w_out[0] += w_refs[i][...].astype(F32)
-
-    @pl.when((j == 0) & (k == 0))
+        block = meta[i]
+
+        @pl.when(block >= 0)
+        def _(i=i, block=block):
+            w_out[block] += w_refs[i][...].astype(F32)
+
+    @pl.when((pl.program_id(0) == 0) & (pl.program_id(1) == 0))
     def _():
         b_out[...] = jnp.zeros_like(b_out)
-
-    @pl.when(j == 0)
-    def _():
         for i in range(terms):
-
-            @pl.when(meta[i] == k)
-            def _(i=i):
-                b_out[pl.ds(k, 1)] += b_refs[i][0:1].astype(F32)[None]
+            block = meta[i]
+
+            @pl.when(block >= 0)
+            def _(i=i, block=block):
+                b_out[block] += b_refs[i][0:1].astype(F32)
 
 
 def shards(activations, dictionary, enc_bias, dec_bias, block_codes):
@@ -184,19 +212,22 @@
     aligned = share % SPAN == 0
     ns, fw = (nd, share) if aligned else (1, width)
 
-    mine = lax.dynamic_index_in_dim(block_codes, s, axis=1, keepdims=False)
-    codes = lax.all_gather(mine, "dp", axis=0, tiled=False)
+    ring_x = [activations]
+    for t in range(1, nz):
+        ring_x.append(along_ring(ring_x[-1]))
+    codes = [lax.dynamic_index_in_dim(block_codes, s, axis=1, keepdims=False)]
+    for t in range(1, nz):
+        codes.append(along_ring(codes[-1]))
+    codes = jnp.stack(codes)
+    codes = jnp.concatenate([codes, to_sibling(codes)])
     filled = codes >= 0
     local = codes - s * shard_blocks
     owner = jnp.where(filled, local // own_blocks, -1)
     inner = jnp.where(filled, local % own_blocks, -1)
-
-    def pick(holder):
-        match = owner == holder
-        return jnp.max(jnp.where(match, inner, -1), axis=(1, 2)), jnp.any(match, axis=2).astype(jnp.int32)
-
-    own_pick, own_named = pick(d)
-    sib_pick, sib_named = pick(d ^ 1)
+    holders = jnp.stack([d, d ^ 1])[:, None, None, None]
+    match = owner == holders
+    picked = jnp.max(jnp.where(match, inner, -1), axis=(2, 3))
+    named = jnp.any(match, axis=3).astype(jnp.int32)
 
     order = s ^ jnp.arange(nd, dtype=jnp.int32)
     dec_rel = dec_bias.reshape(nd, share)[order].reshape(1, width)
@@ -205,17 +236,19 @@
         table = table.reshape(-1, nd, share)[:, order].reshape(-1, width)
     own_w = table.reshape(own_blocks, SPAN, width)
     sib_w = to_sibling(own_w)
-    own_b = enc_bias.reshape(own_blocks, SPAN)
+    own_b = enc_bias.reshape(own_blocks, 1, SPAN)
     sib_b = to_sibling(own_b)
     place = order if aligned else jnp.zeros((1,), jnp.int32)
 
-    def meta_of(t):
-        g = (d + 2 * (nz - t)) % npar
-        safe = jnp.maximum(jnp.stack([own_pick[g], sib_pick[g]]), 0)
-        named = jnp.stack([own_named[g], sib_named[g]], axis=1).reshape(-1)
-        bias = jnp.concatenate([own_b[safe[0]], sib_b[safe[1]]]).astype(F32).reshape(1, 2 * SPAN)
-        return jnp.concatenate([safe, named, place]), bias
-
+    metas = jnp.concatenate(
+        [
+            jnp.maximum(picked[:, :nz], 0).T,
+            named[:, :nz].transpose(1, 2, 0).reshape(nz, 2 * ntb),
+            jnp.broadcast_to(place, (nz, place.shape[0])),
+        ],
+        axis=1,
+    )
+    metas = [metas[t] for t in range(nz)]
     base = 2 + 2 * ntb
 
     def w_specs():
@@ -223,6 +256,11 @@
             pl.BlockSpec((1, SPAN, fw), lambda i, m, part=part, j=j: (m[part], 0, m[base + j]))
             for part in range(2)
             for j in range(ns)
+        ]
+
+    def b_specs():
+        return [
+            pl.BlockSpec((1, 1, SPAN), lambda i, m, part=part: (m[part], 0, 0)) for part in range(2)
         ]
 
     def whole(shape):
@@ -243,15 +281,17 @@
 
     half = tokens // 2
 
-    def forward(slots, meta, bias):
+    def forward(slots, meta):
         pieces, layout = flatten(slots)
         if aligned:
-            out_layout = [(j, h * half, half) for j in range(ns) for h in (0, 1)]
-            dtypes = []
-            for j in range(ns):
-                for h in (0, 1):
-                    fed = any(k & j == j and k.bit_count() == j.bit_count() + 1 and k ^ hop_bit(k, h) == j for k in range(1, nd))
-                    dtypes.append(F32 if fed else BF)
+            out_layout, dtypes = [], []
+            for j in range(nd):
+                if j.bit_count() < 2:
+                    out_layout.append((j, 0, tokens))
+                    dtypes.append(F32)
+                else:
+                    out_layout += [(j, 0, half), (j, half, half)]
+                    dtypes += [BF if j == nd - 1 else F32] * 2
         else:
             out_layout, dtypes = [(0, 0, tokens)], [F32]
         res = pl.pallas_call(
@@ -261,7 +301,8 @@
                 grid=(1,),
                 in_specs=[whole(p.shape) for p in pieces]
                 + w_specs()
-                + [whole((1, width)), whole((1, 2 * SPAN))],
+                + [whole((1, width))]
+                + b_specs(),
                 out_specs=[whole((tokens, 2 * SPAN))] + [whole((c, fw)) for _, _, c in out_layout],
                 scratch_shapes=[pltpu.VMEM((tokens, width), BF), pltpu.VMEM((2 * SPAN, width), BF)],
             ),
@@ -271,12 +312,16 @@
             cost_estimate=pl.CostEstimate(
                 flops=8 * tokens * SPAN * width, bytes_accessed=8 * tokens * width, transcendentals=0
             ),
-        )(meta, *pieces, *([own_w] * ns), *([sib_w] * ns), dec_rel, bias)
+        )(meta, *pieces, *([own_w] * ns), *([sib_w] * ns), dec_rel, own_b, sib_b)
         lat, outs = res[0], res[1:]
         if aligned:
-            return lat, [[outs[2 * j], outs[2 * j + 1]] for j in range(nd)]
-        full = outs[0].reshape(2, half, nd, share)
-        return lat, [[full[h, :, j] for h in (0, 1)] for j in range(nd)]
+            acc = {}
+            for out, (j, _, _) in zip(outs, out_layout):
+                acc.setdefault(j, []).append(out)
+            return lat, acc
+        full = outs[0].reshape(tokens, nd, share)
+        split = {j: [full[:, j]] if j.bit_count() < 2 else [full[:half, j], full[half:, j]] for j in range(nd)}
+        return lat, split
 
     def backward(x_slots, e_slots, lat, meta):
         xp, xl = flatten(x_slots)
@@ -304,36 +349,111 @@
             ),
         )(meta, *xp, *ep, *([own_w] * ns), *([sib_w] * ns), dec_rel, lat)
 
-    metas = [meta_of(t) for t in range(nz)]
-    own_x = [activations]
-    for t in range(1, nz):
-        own_x.append(along_ring(own_x[-1]))
-    x_slots, lats, parts = [], [], []
-    for t in range(nz):
-        x_slots.append(gather_slots(own_x[t]))
-        lat, part = forward(x_slots[t], *metas[t])
-        lats.append(lat)
-        parts.append(part)
+    levels = nd.bit_length() - 1
+    paired = nd == 4 and nz == 4
+    steps = Steps()
+    x_slots = [{0: [x]} for x in ring_x]
+    x_left = {}
+
+    def x_step(*jobs):
+        items, spans = [], []
+        for t, count, mode in jobs:
+            more, keys = gather_level(x_slots[t], count, mode)
+            spans.append((t, keys, len(items)))
+            items += more
+        got = steps.send(items)
+        for t, keys, at in spans:
+            gather_store(x_slots[t], keys, got[at : at + len(keys)])
+
+    lats, accs = {}, {}
+
+    def encode(t):
+        lats[t], accs[t] = forward([x_slots[t][j] for j in range(nd)], metas[t])
+
+    def r_step(t, count):
+        items, keys = scatter_level(accs[t], count)
+        scatter_store(accs[t], keys, steps.send(items))
+
+    if paired:
+        x_step((0, 1, 0))
+        x_step((1, 1, 0))
+        x_step((0, 2, 0), (1, 2, 1))
+        encode(1)
+        encode(0)
+        x_step((2, 1, 0))
+        r_step(1, 2)
+        x_step((3, 1, 0))
+        x_step((2, 2, 0), (3, 2, 1))
+        r_step(1, 1)
+        encode(2)
+        r_step(2, 2)
+        encode(3)
+        r_step(3, 2)
+        r_step(2, 1)
+        r_step(0, 2)
+        r_step(3, 1)
+        r_step(0, 1)
+    else:
+        for t in range(nz):
+            for count in range(1, levels + 1):
+                x_step((t, count, 2))
+            encode(t)
+        for t in list(range(1, nz)) + [0]:
+            for count in range(levels, 0, -1):
+                r_step(t, count)
     carry = None
     for t in list(range(1, nz)) + [0]:
-        total = scatter_sum(parts[t])
+        total = accs[t][0][0]
         if carry is not None:
             total = total + along_ring(carry.astype(BF)).astype(F32)
         carry = total
     dec_own = lax.dynamic_slice_in_dim(dec_bias, s * share, share)
     error = (carry + dec_own - activations.astype(F32)).astype(BF)
 
-    own_e = error
-    own_terms, sib_terms = [], []
-    for t in range(nz):
-        if t:
-            own_e = along_ring(own_e)
-        mine_t, theirs = backward(x_slots[t], gather_slots(own_e), lats[t], metas[t][0])
-        own_terms.append(mine_t)
-        sib_terms.append(to_sibling(theirs))
-
-    here = [(d + 2 * (nz - t)) % npar for t in range(nz)]
-    which = jnp.stack([own_pick[g] for g in here] + [own_pick[g ^ 1] for g in here])
+    ring_e = [error]
+    for t in range(1, nz):
+        ring_e.append(along_ring(ring_e[-1]))
+    e_slots = [{0: [e]} for e in ring_e]
+    own_terms, sib_terms = {}, {}
+    steps = Steps()
+
+    def e_step(*jobs, after=()):
+        items, spans = [], []
+        for t, count, mode in jobs:
+            more, keys = gather_level(e_slots[t], count, mode)
+            spans.append((t, keys, len(items)))
+            items += more
+        got = steps.send(items, after)
+        for t, keys, at in spans:
+            gather_store(e_slots[t], keys, got[at : at + len(keys)])
+
+    def decode(t):
+        own_terms[t], theirs = backward(
+            [x_slots[t][j] for j in range(nd)], [e_slots[t][j] for j in range(nd)], lats[t], metas[t]
+        )
+        sib_terms[t] = to_sibling(theirs)
+
+    if paired:
+        e_step((0, 1, 0))
+        e_step((1, 1, 0))
+        e_step((0, 2, 0), (1, 2, 1))
+        e_step((2, 1, 0))
+        decode(0)
+        decode(1)
+        e_step((2, 2, 2))
+        e_step((3, 1, 0), after=[own_terms[0]])
+        e_step((3, 2, 2), after=[own_terms[1]])
+        decode(2)
+        decode(3)
+    else:
+        for t in range(nz):
+            for count in range(1, levels + 1):
+                e_step((t, count, 2))
+            decode(t)
+    own_terms = [own_terms[t] for t in range(nz)]
+    sib_terms = [sib_terms[t] for t in range(nz)]
+
+    which = picked[0]
     terms = own_terms + sib_terms
     nt = len(terms)
     meta = jnp.concatenate([which, place])
@@ -341,11 +461,11 @@
         functools.partial(sum_kernel, nt),
         grid_spec=pltpu.PrefetchScalarGridSpec(
             num_scalar_prefetch=1,
-            grid=(ns, own_blocks),
-            in_specs=[pl.BlockSpec((SPAN, fw), lambda j, k, m: (0, j))] * nt
+            grid=(ns, 2),
+            in_specs=[pl.BlockSpec((SPAN // 2, fw), lambda j, k, m: (k, j))] * nt
             + [pl.BlockSpec((EXTRA, SPAN), lambda j, k, m: (SPAN // EXTRA, 0))] * nt,
             out_specs=[
-                pl.BlockSpec((1, SPAN, fw), lambda j, k, m: (k, 0, m[nt + j])),
+                pl.BlockSpec((own_blocks, SPAN // 2, fw), lambda j, k, m: (0, k, m[nt + j])),
                 pl.BlockSpec((own_blocks, 1, SPAN), lambda j, k, m: (0, 0, 0)),
             ],
         ),

time: 329 us -> 245 us (0.74)
  Pallas kernels: 62.1 us -> 45 us
  between operations: 17.1 us -> 1.31 us
  starting transfers between devices: 71.9 us -> 57 us
  blocking collectives: 14.6 us -> 0 us
  waiting for transfers between devices: 133 us -> 119 us
  other arithmetic: 10.4 us -> 6.12 us
    ppermute x9 -> x12, waiting for transfers between devices: 70.5 us -> 45.2 us  [along_ring(): return lax.ppermute(x, 'dp', [(i, (i + 2) % n) for i in range(n)])]
    ppermute x56 -> x42, starting transfers between devices: 67.5 us -> 50.6 us  [over_dict(): return lax.ppermute(x, 'dict', [(i, i ^ bit) for i in range(n)])]
    all_gather x1 -> x0, blocking collectives: 14.6 us -> none  [shards(): codes = lax.all_gather(mine, 'dp', axis=0, tiled=False)]
    pallas_call x1, Pallas kernels: 19.2 us -> 8.83 us  [shards(): pl.pallas_call(functools.partial(sum_kernel, nt), grid_spec=pltpu.Prefetc...]
    ppermute x56 -> x42, waiting for transfers between devices: 62.8 us -> 71.9 us  [over_dict(): return lax.ppermute(x, 'dict', [(i, i ^ bit) for i in range(n)])]
    unnamed x45 -> x95, local copies, waits for them, and re-layouts: 4.52 us -> 12.3 us
    pallas_call x4, Pallas kernels: 24.8 us -> 19.5 us  [backward(): pl.pallas_call(functools.partial(bwd_kernel, xl, el, ns, fw), grid_spec=p...]
    max x3 -> x0, other arithmetic: 5.21 us -> none  [meta_of(): safe = jnp.maximum(jnp.stack([own_pick[g], sib_pick[g]]), 0)]
  transfers between devices with their start and end apart: 71 -> 61, of which waited for: 22 -> 30; matrix products, arithmetic and copies ran while one was open for 7% -> 3% of each run, Pallas kernels for 13% -> 15%
where the time goes in v2:
time: 245 us; the launch traced here: 244 us
  waiting for transfers between devices  119 us (49%)
  starting transfers between devices  57 us (23%)
  Pallas kernels  45 us (18%)
  local copies, waits for them, and re-layouts  15.6 us (6%)
  other arithmetic  6.12 us (2%)
    ppermute x42, waiting for transfers between devices, over_dict(): return lax.ppermute(x, 'dict', [(i, i ^ bit) for i in range(n)])  71.9 us
    ppermute x42, starting transfers between devices, over_dict(): return lax.ppermute(x, 'dict', [(i, i ^ bit) for i in range(n)])  50.6 us
    ppermute x12, waiting for transfers between devices, along_ring(): return lax.ppermute(x, 'dp', [(i, (i + 2) % n) for i in range(n)])  45.2 us
    pallas_call x4, Pallas kernels, backward(): pl.pallas_call(functools.partial(bwd_kernel, xl, el, ns, fw), grid_spec=p...  19.5 us
    pallas_call x4, Pallas kernels, forward(): pl.pallas_call(functools.partial(fwd_kernel, layout, ns, fw, out_layout),...  16.7 us
    unnamed x95, local copies, waits for them, and re-layouts  12.3 us
    pallas_call x1, Pallas kernels, shards(): pl.pallas_call(functools.partial(sum_kernel, nt), grid_spec=pltpu.Prefetc...  8.83 us
  transfers between devices with their start and end apart: 61, of which 30 were waited for; matrix products, arithmetic and copies ran while one was open for 3% of the time, Pallas kernels for 15%

profile of v2, /device:TPU:0, one launch (start us, length us, event | category | flops | bytes accessed | tf_op | source)
XLA Modules:
  0.0 244.3 jit_solution(55042626060212505)
XLA Ops:
  1.2 2.6 %collective-permute-start.9 = (bf16[256,896]{1,0:T(8,128)(2,1)}, bf16[256,896]{1,0:T(8,128)(2,1)S(1)}, u32[]{:S(2)}, u32[]{:S(2)}) collective-permute-start(bf16[256,896]{1,0:T(8,128)(2,1)} %refs_0_.3), channel_id=1, source_target_pairs={{0,2},{1,3},{2,4},{3,5},{4,6},{5,7},{6,0},{7,1},{8,10},{9,11},{10,... | collective-permute-start | bytes 1376264 | tf_op jit(solution)/shard_map/ppermute | solution.py:48
  10.6 6.6 %collective-permute-done = s32[2,8]{1,0:T(2,128)S(1)} collective-permute-done((s32[2,8]{1,0:T(2,128)S(1)}, s32[2,8]{1,0:T(2,128)S(1)}, u32[]{:S(2)}, u32[]{:S(2)}) %collective-permute-start) | collective-permute-done | bytes 96 | tf_op jit(solution)/shard_map/ppermute | solution.py:48
  17.2 5.4 %collective-permute-done.1 = s32[2,8]{1,0:T(2,128)S(1)} collective-permute-done((s32[2,8]{1,0:T(2,128)S(1)}, s32[2,8]{1,0:T(2,128)S(1)}, u32[]{:S(2)}, u32[]{:S(2)}) %collective-permute-start.1) | collective-permute-done | bytes 96 | tf_op jit(solution)/shard_map/ppermute | solution.py:48
  22.6 5.4 %collective-permute-done.2 = s32[2,8]{1,0:T(2,128)S(1)} collective-permute-done((s32[2,8]{1,0:T(2,128)S(1)}, s32[2,8]{1,0:T(2,128)S(1)}, u32[]{:S(2)}, u32[]{:S(2)}) %collective-permute-start.2) | collective-permute-done | bytes 96 | tf_op jit(solution)/shard_map/ppermute | solution.py:48
  31.6 9.3 %collective-permute-done.13.refs_2_ = bf16[256,896]{1,0:T(8,128)(2,1)S(1)} collective-permute-done((bf16[256,896]{1,0:T(8,128)(2,1)S(1)}, bf16[256,896]{1,0:T(8,128)(2,1)S(1)}, u32[]{:S(2)}, u32[]{:S(2)}) %collective-permute-start.13) | collective-permute-done | bytes 458784 | tf_op jit(solution)/shard_map/ppermute | solution.py:38
  47.5 6.9 %collective-permute-done.18.refs_3_ = bf16[256,896]{1,0:T(8,128)(2,1)S(1)} collective-permute-done((bf16[256,896]{1,0:T(8,128)(2,1)S(1)}, bf16[256,896]{1,0:T(8,128)(2,1)S(1)}, u32[]{:S(2)}, u32[]{:S(2)}) %collective-permute-start.18) | collective-permute-done | bytes 458784 | tf_op jit(solution)/shard_map/ppermute | solution.py:38
  54.4 3.2 %copy-done.2 = bf16[1024,3584]{1,0:T(8,128)(2,1)S(1)} copy-done((bf16[1024,3584]{1,0:T(8,128)(2,1)S(1)}, bf16[1024,3584]{1,0:T(8,128)(2,1)}, u32[]{:S(2)}) %copy-start.2) | copy-done | bytes 7340056
  57.6 4.3 %shard_map.77 = (bf16[256,256]{1,0:T(8,128)(2,1)S(1)}, f32[256,896]{1,0:T(8,128)S(1)}, f32[256,896]{1,0:T(8,128)S(1)}, f32[256,896]{1,0:T(8,128)S(1)}, bf16[128,...) custom-call(s32[10]{0:T(128)S(1)} %get-tuple-element.135.meta, bf16[256,896]{1,0:T(8,128)(2,1)S(1)} %collective-permute-done.9.refs_0_, ...), custom_call_target="tpu_custom_call" | custom-call | flops 939524096 | bytes 7340032 | tf_op jit(solution)/shard_map/pallas_call | solution.py:297
  73.8 4.2 %collective-permute-done.16.refs_1_ = bf16[256,896]{1,0:T(8,128)(2,1)S(1)} collective-permute-done((bf16[256,896]{1,0:T(8,128)(2,1)S(1)}, bf16[256,896]{1,0:T(8,128)(2,1)S(1)}, u32[]{:S(2)}, u32[]{:S(2)}) %collective-permute-start.16) | collective-permute-done | bytes 458784 | tf_op jit(solution)/shard_map/ppermute | solution.py:38
  77.9 4.0 %collective-permute-done.17.refs_2_ = bf16[256,896]{1,0:T(8,128)(2,1)S(1)} collective-permute-done((bf16[256,896]{1,0:T(8,128)(2,1)S(1)}, bf16[256,896]{1,0:T(8,128)(2,1)S(1)}, u32[]{:S(2)}, u32[]{:S(2)}) %collective-permute-start.17) | collective-permute-done | bytes 458784 | tf_op jit(solution)/shard_map/ppermute | solution.py:38
  85.5 4.1 %shard_map.76 = (bf16[256,256]{1,0:T(8,128)(2,1)S(1)}, f32[256,896]{1,0:T(8,128)S(1)}, f32[256,896]{1,0:T(8,128)S(1)}, f32[256,896]{1,0:T(8,128)S(1)}, bf16[128,...) custom-call(s32[10]{0:T(128)S(1)} %get-tuple-element.133.meta, bf16[256,896]{1,0:T(8,128)(2,1)S(1)} %copy-done.5, ...), custom_call_target="tpu_custom_call" | custom-call | flops 939524096 | bytes 7340032 | tf_op jit(solution)/shard_map/pallas_call | solution.py:297
  91.8 4.1 %shard_map.79 = (bf16[256,256]{1,0:T(8,128)(2,1)S(1)}, f32[256,896]{1,0:T(8,128)S(1)}, f32[256,896]{1,0:T(8,128)S(1)}, f32[256,896]{1,0:T(8,128)S(1)}, bf16[128,...) custom-call(s32[10]{0:T(128)S(1)} %get-tuple-element.134.meta, bf16[256,896]{1,0:T(8,128)(2,1)S(1)} %collective-permute-done.10.refs_0_, ...), custom_call_target="tpu_custom_call" | custom-call | flops 939524096 | bytes 7340032 | tf_op jit(solution)/shard_map/pallas_call | solution.py:297
  96.6 2.5 %collective-permute-done.23 = bf16[256,896]{1,0:T(8,128)(2,1)S(1)} collective-permute-done((bf16[256,896]{1,0:T(8,128)(2,1)S(1)}, bf16[256,896]{1,0:T(8,128)(2,1)S(1)}, u32[]{:S(2)}, u32[]{:S(2)}) %collective-permute-start.23) | collective-permute-done | bytes 458784 | tf_op jit(solution)/shard_map/ppermute | solution.py:38
  99.1 3.3 %collective-permute-done.22 = bf16[256,896]{1,0:T(8,128)(2,1)S(1)} collective-permute-done((bf16[256,896]{1,0:T(8,128)(2,1)S(1)}, bf16[256,896]{1,0:T(8,128)(2,1)S(1)}, u32[]{:S(2)}, u32[]{:S(2)}) %collective-permute-start.22) | collective-permute-done | bytes 458784 | tf_op jit(solution)/shard_map/ppermute | solution.py:38
  103.5 4.1 %shard_map.78 = (bf16[256,256]{1,0:T(8,128)(2,1)S(1)}, f32[256,896]{1,0:T(8,128)S(1)}, f32[256,896]{1,0:T(8,128)S(1)}, f32[256,896]{1,0:T(8,128)S(1)}, bf16[128,...) custom-call(s32[10]{0:T(128)S(1)} %get-tuple-element.136.meta, bf16[256,896]{1,0:T(8,128)(2,1)S(1)} %collective-permute-done.11.refs_0_, ...), custom_call_target="tpu_custom_call" | custom-call | flops 939524096 | bytes 7340032 | tf_op jit(solution)/shard_map/pallas_call | solution.py:297
  111.7 2.1 collective-permute-start.33
  113.8 2.5 %collective-permute-done.25 = bf16[128,896]{1,0:T(8,128)(2,1)S(1)} collective-permute-done((bf16[128,896]{1,0:T(8,128)(2,1)S(1)}, bf16[128,896]{1,0:T(8,128)(2,1)S(1)}, u32[]{:S(2)}, u32[]{:S(2)}) %collective-permute-start.25) | collective-permute-done | bytes 229408 | tf_op jit(solution)/shard_map/ppermute | solution.py:38
  119.8 8.0 %collective-permute-done.34 = bf16[256,896]{1,0:T(8,128)(2,1)S(1)} collective-permute-done((bf16[256,896]{1,0:T(8,128)(2,1)S(1)}, bf16[256,896]{1,0:T(8,128)(2,1)S(1)}, u32[]{:S(2)}, u32[]{:S(2)}) %collective-permute-start.34) | collective-permute-done | bytes 458784 | tf_op jit(solution)/shard_map/ppermute | solution.py:38
  135.3 3.1 %collective-permute-done.38 = bf16[256,896]{1,0:T(8,128)(2,1)S(1)} collective-permute-done((bf16[256,896]{1,0:T(8,128)(2,1)S(1)}, bf16[256,896]{1,0:T(8,128)(2,1)S(1)}, u32[]{:S(2)}, u32[]{:S(2)}) %collective-permute-start.38) | collective-permute-done | bytes 458784 | tf_op jit(solution)/shard_map/ppermute | solution.py:48
  138.4 4.2 %collective-permute-done.36 = bf16[256,896]{1,0:T(8,128)(2,1)S(1)} collective-permute-done((bf16[256,896]{1,0:T(8,128)(2,1)S(1)}, bf16[256,896]{1,0:T(8,128)(2,1)S(1)}, u32[]{:S(2)}, u32[]{:S(2)}) %collective-permute-start.36) | collective-permute-done | bytes 458784 | tf_op jit(solution)/shard_map/ppermute | solution.py:38
  144.4 3.9 %collective-permute-done.29 = bf16[256,896]{1,0:T(8,128)(2,1)} collective-permute-done((bf16[256,896]{1,0:T(8,128)(2,1)}, bf16[256,896]{1,0:T(8,128)(2,1)}, u32[]{:S(2)}, u32[]{:S(2)}) %collective-permute-start.29) | collective-permute-done | bytes 458784 | tf_op jit(solution)/shard_map/ppermute | solution.py:38
  148.3 8.6 %collective-permute-done.39 = bf16[256,896]{1,0:T(8,128)(2,1)} collective-permute-done((bf16[256,896]{1,0:T(8,128)(2,1)}, bf16[256,896]{1,0:T(8,128)(2,1)}, u32[]{:S(2)}, u32[]{:S(2)}) %collective-permute-start.39) | collective-permute-done | bytes 458784 | tf_op jit(solution)/shard_map/ppermute | solution.py:48
  159.2 2.7 %collective-permute-start.41 = (bf16[256,896]{1,0:T(8,128)(2,1)S(1)}, bf16[256,896]{1,0:T(8,128)(2,1)S(1)}, u32[]{:S(2)}, u32[]{:S(2)}) collective-permute-start(bf16[256,896]{1,0:T(8,128)(2,1)S(1)} %subtract_convert_fusion.refs_4_), channel_id=1, source_target_pairs={{0,16},{8,24},{16,0},{24,8},{1,17},{9,25},{17,1},{25,9},{2,18},{10... | collective-permute-start | bytes 1376264 | tf_op jit(solution)/shard_map/ppermute | solution.py:38
  161.9 12.2 %collective-permute-done.43.refs_4_ = bf16[256,896]{1,0:T(8,128)(2,1)S(1)} collective-permute-done((bf16[256,896]{1,0:T(8,128)(2,1)S(1)}, bf16[256,896]{1,0:T(8,128)(2,1)S(1)}, u32[]{:S(2)}, u32[]{:S(2)}) %collective-permute-start.43) | collective-permute-done | bytes 458784 | tf_op jit(solution)/shard_map/ppermute | solution.py:48
  176.2 11.3 %collective-permute-done.44.refs_5_ = bf16[256,896]{1,0:T(8,128)(2,1)S(1)} collective-permute-done((bf16[256,896]{1,0:T(8,128)(2,1)S(1)}, bf16[256,896]{1,0:T(8,128)(2,1)S(1)}, u32[]{:S(2)}, u32[]{:S(2)}) %collective-permute-start.44) | collective-permute-done | bytes 458784 | tf_op jit(solution)/shard_map/ppermute | solution.py:38
  192.2 3.1 %copy-done.4 = bf16[1024,3584]{1,0:T(8,128)(2,1)S(1)} copy-done((bf16[1024,3584]{1,0:T(8,128)(2,1)S(1)}, bf16[1024,3584]{1,0:T(8,128)(2,1)}, u32[]{:S(2)}) %copy-start.4) | copy-done | bytes 7340056
  200.3 5.1 %shard_map.80 = (bf16[144,3584]{1,0:T(8,128)(2,1)S(1)}, bf16[144,3584]{1,0:T(8,128)(2,1)S(1)}) custom-call(s32[10]{0:T(128)S(1)} %get-tuple-element.133.meta, bf16[256,896]{1,0:T(8,128)(2,1)S(1)} %copy-done.6, bf16[256,896]{1,0:T(8,128)(2,1)S(1)} %copy-done.10, bf16[256,896]{1,0:T(8,128)(2,1)S(1)} %copy-done.12, bf16[256,896]{1,0:T(8,128)(2,1)S(1)} %copy-done.36, ...), custom_call_target="tpu_custom_call" | custom-call | flops 1409286144 | bytes 9175040 | tf_op jit(solution)/shard_map/pallas_call | solution.py:330
  212.6 4.8 %shard_map.81 = (bf16[144,3584]{1,0:T(8,128)(2,1)S(1)}, bf16[144,3584]{1,0:T(8,128)(2,1)S(1)}) custom-call(s32[10]{0:T(128)S(1)} %get-tuple-element.135.meta, bf16[256,896]{1,0:T(8,128)(2,1)S(1)} %copy-done.8, bf16[256,896]{1,0:T(8,128)(2,1)S(1)} %copy-done.24, bf16[256,896]{1,0:T(8,128)(2,1)S(1)} %copy-done.16, bf16[256,896]{1,0:T(8,128)(2,1)S(1)} %copy-done.26, ...), custom_call_target="tpu_custom_call" | custom-call | flops 1409286144 | bytes 9175040 | tf_op jit(solution)/shard_map/pallas_call | solution.py:330
  222.9 4.8 %shard_map.82 = (bf16[144,3584]{1,0:T(8,128)(2,1)S(1)}, bf16[144,3584]{1,0:T(8,128)(2,1)S(1)}) custom-call(s32[10]{0:T(128)S(1)} %get-tuple-element.134.meta, bf16[256,896]{1,0:T(8,128)(2,1)S(1)} %copy-done.14, bf16[256,896]{1,0:T(8,128)(2,1)S(1)} %copy-done.20, bf16[256,896]{1,0:T(8,128)(2,1)S(1)} %copy-done.22, bf16[256,896]{1,0:T(8,128)(2,1)S(1)} %copy-done.34, ...), custom_call_target="tpu_custom_call" | custom-call | flops 1409286144 | bytes 9175040 | tf_op jit(solution)/shard_map/pallas_call | solution.py:330
  227.9 4.8 %shard_map.83 = (bf16[144,3584]{1,0:T(8,128)(2,1)S(1)}, bf16[144,3584]{1,0:T(8,128)(2,1)S(1)}) custom-call(s32[10]{0:T(128)S(1)} %get-tuple-element.136.meta, bf16[256,896]{1,0:T(8,128)(2,1)S(1)} %copy-done.18, bf16[256,896]{1,0:T(8,128)(2,1)S(1)} %copy-done.28, bf16[256,896]{1,0:T(8,128)(2,1)S(1)} %copy-done.30, bf16[256,896]{1,0:T(8,128)(2,1)S(1)} %copy-done.32, ...), custom_call_target="tpu_custom_call" | custom-call | flops 1409286144 | bytes 9175040 | tf_op jit(solution)/shard_map/pallas_call | solution.py:330
  233.3 2.2 collective-permute-done.60.refs_7_.refs_15_
  235.5 8.8 %shard_map.84 = (f32[8,128,3584]{2,1,0:T(8,128)}, f32[8,1,128]{2,1,0:T(1,128)}) custom-call(s32[12]{0:T(128)S(1)} %pad_add_fusion.2.meta, bf16[144,3584]{1,0:T(8,128)(2,1)S(1)} %get-tuple-element.111.refs_0_.refs_8_, bf16[144,3584]{1,0:T(8,128)(2,1)S(1)} %get-tuple-element.114.refs_1_.refs_9_, bf16[144,3584]{1,0:T(8,128)(2,1)S(1)} %get-tuple-element.119.refs_2_.refs_10_, ...), custom_call_target="tpu_custom_call" | custom-call | flops 3670016 | bytes 22020096 | tf_op jit(solution)/shard_map/pallas_call | solution.py:460
  (236 shorter events, 80.9 us)
Async XLA Ops:
  0.6 53.8 %collective-permute-start.7 = (bf16[8,128,3584]{2,1,0:T(8,128)(2,1)}, bf16[8,128,3584]{2,1,0:T(8,128)(2,1)}, u32[]{:S(2)}, u32[]{:S(2)}) collective-permute-start(bf16[8,128,3584]{2,1,0:T(8,128)(2,1)} %bitcast.34), channel_id=1, source_target_pairs={{0,1},{1,0},{2,3},{3,2},{4,5},{5,4},{6,7},{7,6},{8,9},{9,8},{10,11... | collective-permute-start | bytes 22020104 | tf_op jit(solution)/shard_map/ppermute | solution.py:43
  1.2 26.8 %collective-permute-start.9 = (bf16[256,896]{1,0:T(8,128)(2,1)}, bf16[256,896]{1,0:T(8,128)(2,1)S(1)}, u32[]{:S(2)}, u32[]{:S(2)}) collective-permute-start(bf16[256,896]{1,0:T(8,128)(2,1)} %refs_0_.3), channel_id=1, source_target_pairs={{0,2},{1,3},{2,4},{3,5},{4,6},{5,7},{6,0},{7,1},{8,10},{9,11},{10,... | collective-permute-start | bytes 1376264 | tf_op jit(solution)/shard_map/ppermute | solution.py:48
  3.8 26.2 %collective-permute-start.4 = (bf16[256,896]{1,0:T(8,128)(2,1)}, bf16[256,896]{1,0:T(8,128)(2,1)S(1)}, u32[]{:S(2)}, u32[]{:S(2)}) collective-permute-start(bf16[256,896]{1,0:T(8,128)(2,1)} %refs_0_.3), channel_id=1, source_target_pairs={{0,8},{8,0},{16,24},{24,16},{1,9},{9,1},{17,25},{25,17},{2,10},{10... | collective-permute-start | bytes 1376264 | tf_op jit(solution)/shard_map/ppermute | solution.py:38
  5.3 26.3 %collective-permute-start.5 = (bf16[256,896]{1,0:T(8,128)(2,1)}, bf16[256,896]{1,0:T(8,128)(2,1)S(1)}, u32[]{:S(2)}, u32[]{:S(2)}) collective-permute-start(bf16[256,896]{1,0:T(8,128)(2,1)} %refs_0_.3), channel_id=1, source_target_pairs={{0,16},{8,24},{16,0},{24,8},{1,17},{9,25},{17,1},{25,9},{2,18},{10... | collective-permute-start | bytes 1376264 | tf_op jit(solution)/shard_map/ppermute | solution.py:38
  29.6 16.8 %collective-permute-start.8 = (bf16[8,1,128]{2,1,0:T(2,128)(2,1)S(1)}, bf16[8,1,128]{2,1,0:T(2,128)(2,1)S(1)}, u32[]{:S(2)}, u32[]{:S(2)}) collective-permute-start(bf16[8,1,128]{2,1,0:T(2,128)(2,1)S(1)} %copy.31.refs_13_), channel_id=1, source_target_pairs={{0,1},{1,0},{2,3},{3,2},{4,5},{5,4},{6,7},{7,6},{8,9},{9,8},{10,11... | collective-permute-start | bytes 6152 | tf_op jit(solution)/shard_map/ppermute | solution.py:43
  31.6 14.3 %collective-permute-start.10 = (bf16[256,896]{1,0:T(8,128)(2,1)S(1)}, bf16[256,896]{1,0:T(8,128)(2,1)S(1)}, u32[]{:S(2)}, u32[]{:S(2)}) collective-permute-start(bf16[256,896]{1,0:T(8,128)(2,1)S(1)} %collective-permute-done.9.refs_0_), channel_id=1, source_target_pairs={{0,2},{1,3},{2,4},{3,5},{4,6},{5,7},{6,0},{7,1},{8,10},{9,11},{10,... | collective-permute-start | bytes 1376264 | tf_op jit(solution)/shard_map/ppermute | solution.py:48
  40.9 13.4 %collective-permute-start.18 = (bf16[256,896]{1,0:T(8,128)(2,1)S(1)}, bf16[256,896]{1,0:T(8,128)(2,1)S(1)}, u32[]{:S(2)}, u32[]{:S(2)}) collective-permute-start(bf16[256,896]{1,0:T(8,128)(2,1)S(1)} %collective-permute-done.13.refs_2_), channel_id=1, source_target_pairs={{0,8},{8,0},{16,24},{24,16},{1,9},{9,1},{17,25},{25,17},{2,10},{10... | collective-permute-start | bytes 1376264 | tf_op jit(solution)/shard_map/ppermute | solution.py:38
  42.9 19.1 %collective-permute-start.6 = (bf16[256,896]{1,0:T(8,128)(2,1)S(1)}, bf16[256,896]{1,0:T(8,128)(2,1)S(1)}, u32[]{:S(2)}, u32[]{:S(2)}) collective-permute-start(bf16[256,896]{1,0:T(8,128)(2,1)S(1)} %collective-permute-done.4.refs_1_), channel_id=1, source_target_pairs={{0,16},{8,24},{16,0},{24,8},{1,17},{9,25},{17,1},{25,9},{2,18},{10... | collective-permute-start | bytes 1376264 | tf_op jit(solution)/shard_map/ppermute | solution.py:38
  45.9 20.1 %collective-permute-start.14 = (bf16[256,896]{1,0:T(8,128)(2,1)S(1)}, bf16[256,896]{1,0:T(8,128)(2,1)S(1)}, u32[]{:S(2)}, u32[]{:S(2)}) collective-permute-start(bf16[256,896]{1,0:T(8,128)(2,1)S(1)} %collective-permute-done.10.refs_0_), channel_id=1, source_target_pairs={{0,8},{8,0},{16,24},{24,16},{1,9},{9,1},{17,25},{25,17},{2,10},{10... | collective-permute-start | bytes 1376264 | tf_op jit(solution)/shard_map/ppermute | solution.py:38
  46.4 19.6 %collective-permute-start.15 = (bf16[256,896]{1,0:T(8,128)(2,1)S(1)}, bf16[256,896]{1,0:T(8,128)(2,1)S(1)}, u32[]{:S(2)}, u32[]{:S(2)}) collective-permute-start(bf16[256,896]{1,0:T(8,128)(2,1)S(1)} %collective-permute-done.10.refs_0_), channel_id=1, source_target_pairs={{0,16},{8,24},{16,0},{24,8},{1,17},{9,25},{17,1},{25,9},{2,18},{10... | collective-permute-start | bytes 1376264 | tf_op jit(solution)/shard_map/ppermute | solution.py:38
  67.6 14.3 %collective-permute-start.17 = (bf16[256,896]{1,0:T(8,128)(2,1)S(1)}, bf16[256,896]{1,0:T(8,128)(2,1)S(1)}, u32[]{:S(2)}, u32[]{:S(2)}) collective-permute-start(bf16[256,896]{1,0:T(8,128)(2,1)S(1)} %collective-permute-done.11.refs_0_), channel_id=1, source_target_pairs={{0,16},{8,24},{16,0},{24,8},{1,17},{9,25},{17,1},{25,9},{2,18},{10... | collective-permute-start | bytes 1376264 | tf_op jit(solution)/shard_map/ppermute | solution.py:38
  72.1 19.7 %collective-permute-start.30 = (bf16[256,896]{1,0:T(8,128)(2,1)S(1)}, bf16[256,896]{1,0:T(8,128)(2,1)S(1)}, u32[]{:S(2)}, u32[]{:S(2)}) collective-permute-start(bf16[256,896]{1,0:T(8,128)(2,1)S(1)} %collective-permute-done.14.refs_1_), channel_id=1, source_target_pairs={{0,16},{8,24},{16,0},{24,8},{1,17},{9,25},{17,1},{25,9},{2,18},{10... | collective-permute-start | bytes 1376264 | tf_op jit(solution)/shard_map/ppermute | solution.py:38
  82.0 14.0 %collective-permute-start.21 = (bf16[256,896]{1,0:T(8,128)(2,1)S(1)}, bf16[256,896]{1,0:T(8,128)(2,1)S(1)}, u32[]{:S(2)}, u32[]{:S(2)}) collective-permute-start(bf16[256,896]{1,0:T(8,128)(2,1)S(1)} %collective-permute-done.17.refs_2_), channel_id=1, source_target_pairs={{0,8},{8,0},{16,24},{24,16},{1,9},{9,1},{17,25},{25,17},{2,10},{10... | collective-permute-start | bytes 1376264 | tf_op jit(solution)/shard_map/ppermute | solution.py:38
  82.5 16.6 %collective-permute-start.23 = (bf16[256,896]{1,0:T(8,128)(2,1)S(1)}, bf16[256,896]{1,0:T(8,128)(2,1)S(1)}, u32[]{:S(2)}, u32[]{:S(2)}) collective-permute-start(bf16[256,896]{1,0:T(8,128)(2,1)S(1)} %get-tuple-element.83), channel_id=1, source_target_pairs={{0,16},{8,24},{16,0},{24,8},{1,17},{9,25},{17,1},{25,9},{2,18},{10... | collective-permute-start | bytes 1376264 | tf_op jit(solution)/shard_map/ppermute | solution.py:38
  84.0 18.4 %collective-permute-start.22 = (bf16[256,896]{1,0:T(8,128)(2,1)S(1)}, bf16[256,896]{1,0:T(8,128)(2,1)S(1)}, u32[]{:S(2)}, u32[]{:S(2)}) collective-permute-start(bf16[256,896]{1,0:T(8,128)(2,1)S(1)} %get-tuple-element.81), channel_id=1, source_target_pairs={{0,8},{8,0},{16,24},{24,16},{1,9},{9,1},{17,25},{25,17},{2,10},{10... | collective-permute-start | bytes 1376264 | tf_op jit(solution)/shard_map/ppermute | solution.py:38
  96.0 14.9 %collective-permute-start.32 = (bf16[128,896]{1,0:T(8,128)(2,1)S(1)}, bf16[128,896]{1,0:T(8,128)(2,1)S(1)}, u32[]{:S(2)}, u32[]{:S(2)}) collective-permute-start(bf16[128,896]{1,0:T(8,128)(2,1)S(1)} %get-tuple-element.100), channel_id=1, source_target_pairs={{0,8},{8,0},{16,24},{24,16},{1,9},{9,1},{17,25},{25,17},{2,10},{10... | collective-permute-start | bytes 688136 | tf_op jit(solution)/shard_map/ppermute | solution.py:38
  102.6 17.3 %collective-permute-start.37 = (bf16[256,896]{1,0:T(8,128)(2,1)S(1)}, bf16[256,896]{1,0:T(8,128)(2,1)S(1)}, u32[]{:S(2)}, u32[]{:S(2)}) collective-permute-start(bf16[256,896]{1,0:T(8,128)(2,1)S(1)} %add_convert_fusion.2), channel_id=1, source_target_pairs={{0,2},{1,3},{2,4},{3,5},{4,6},{5,7},{6,0},{7,1},{8,10},{9,11},{10,... | collective-permute-start | bytes 1376264 | tf_op jit(solution)/shard_map/ppermute | solution.py:48
  111.4 16.4 %collective-permute-start.34 = (bf16[256,896]{1,0:T(8,128)(2,1)S(1)}, bf16[256,896]{1,0:T(8,128)(2,1)S(1)}, u32[]{:S(2)}, u32[]{:S(2)}) collective-permute-start(bf16[256,896]{1,0:T(8,128)(2,1)S(1)} %add_convert_fusion.4), channel_id=1, source_target_pairs={{0,16},{8,24},{16,0},{24,8},{1,17},{9,25},{17,1},{25,9},{2,18},{10... | collective-permute-start | bytes 1376264 | tf_op jit(solution)/shard_map/ppermute | solution.py:38
  111.7 16.1 %collective-permute-start.33 = (bf16[256,896]{1,0:T(8,128)(2,1)S(1)}, bf16[256,896]{1,0:T(8,128)(2,1)S(1)}, u32[]{:S(2)}, u32[]{:S(2)}) collective-permute-start(bf16[256,896]{1,0:T(8,128)(2,1)S(1)} %add_convert_fusion.5), channel_id=1, source_target_pairs={{0,8},{8,0},{16,24},{24,16},{1,9},{9,1},{17,25},{25,17},{2,10},{10... | collective-permute-start | bytes 1376264 | tf_op jit(solution)/shard_map/ppermute | solution.py:38
  118.2 14.5 %collective-permute-start.26 = (bf16[128,896]{1,0:T(8,128)(2,1)S(1)}, bf16[128,896]{1,0:T(8,128)(2,1)S(1)}, u32[]{:S(2)}, u32[]{:S(2)}) collective-permute-start(bf16[128,896]{1,0:T(8,128)(2,1)S(1)} %get-tuple-element.87), channel_id=1, source_target_pairs={{0,16},{8,24},{16,0},{24,8},{1,17},{9,25},{17,1},{25,9},{2,18},{10... | collective-permute-start | bytes 688136 | tf_op jit(solution)/shard_map/ppermute | solution.py:38
  128.1 14.4 %collective-permute-start.36 = (bf16[256,896]{1,0:T(8,128)(2,1)S(1)}, bf16[256,896]{1,0:T(8,128)(2,1)S(1)}, u32[]{:S(2)}, u32[]{:S(2)}) collective-permute-start(bf16[256,896]{1,0:T(8,128)(2,1)S(1)} %add_convert_fusion.3), channel_id=1, source_target_pairs={{0,16},{8,24},{16,0},{24,8},{1,17},{9,25},{17,1},{25,9},{2,18},{10... | collective-permute-start | bytes 1376264 | tf_op jit(solution)/shard_map/ppermute | solution.py:38
  132.7 15.6 %collective-permute-start.29 = (bf16[256,896]{1,0:T(8,128)(2,1)}, bf16[256,896]{1,0:T(8,128)(2,1)}, u32[]{:S(2)}, u32[]{:S(2)}) collective-permute-start(bf16[256,896]{1,0:T(8,128)(2,1)} %add_convert_fusion.7), channel_id=1, source_target_pairs={{0,16},{8,24},{16,0},{24,8},{1,17},{9,25},{17,1},{25,9},{2,18},{10... | collective-permute-start | bytes 1376264 | tf_op jit(solution)/shard_map/ppermute | solution.py:38
  143.5 13.4 %collective-permute-start.39 = (bf16[256,896]{1,0:T(8,128)(2,1)}, bf16[256,896]{1,0:T(8,128)(2,1)}, u32[]{:S(2)}, u32[]{:S(2)}) collective-permute-start(bf16[256,896]{1,0:T(8,128)(2,1)} %add_convert_fusion), channel_id=1, source_target_pairs={{0,2},{1,3},{2,4},{3,5},{4,6},{5,7},{6,0},{7,1},{8,10},{9,11},{10,... | collective-permute-start | bytes 1376264 | tf_op jit(solution)/shard_map/ppermute | solution.py:48
  158.9 15.2 %collective-permute-start.43 = (bf16[256,896]{1,0:T(8,128)(2,1)S(1)}, bf16[256,896]{1,0:T(8,128)(2,1)S(1)}, u32[]{:S(2)}, u32[]{:S(2)}) collective-permute-start(bf16[256,896]{1,0:T(8,128)(2,1)S(1)} %subtract_convert_fusion.refs_4_), channel_id=1, source_target_pairs={{0,2},{1,3},{2,4},{3,5},{4,6},{5,7},{6,0},{7,1},{8,10},{9,11},{10,... | collective-permute-start | bytes 1376264 | tf_op jit(solution)/shard_map/ppermute | solution.py:48
  159.0 15.9 %collective-permute-start.40 = (bf16[256,896]{1,0:T(8,128)(2,1)S(1)}, bf16[256,896]{1,0:T(8,128)(2,1)S(1)}, u32[]{:S(2)}, u32[]{:S(2)}) collective-permute-start(bf16[256,896]{1,0:T(8,128)(2,1)S(1)} %subtract_convert_fusion.refs_4_), channel_id=1, source_target_pairs={{0,8},{8,0},{16,24},{24,16},{1,9},{9,1},{17,25},{25,17},{2,10},{10... | collective-permute-start | bytes 1376264 | tf_op jit(solution)/shard_map/ppermute | solution.py:38
  159.2 15.7 %collective-permute-start.41 = (bf16[256,896]{1,0:T(8,128)(2,1)S(1)}, bf16[256,896]{1,0:T(8,128)(2,1)S(1)}, u32[]{:S(2)}, u32[]{:S(2)}) collective-permute-start(bf16[256,896]{1,0:T(8,128)(2,1)S(1)} %subtract_convert_fusion.refs_4_), channel_id=1, source_target_pairs={{0,16},{8,24},{16,0},{24,8},{1,17},{9,25},{17,1},{25,9},{2,18},{10... | collective-permute-start | bytes 1376264 | tf_op jit(solution)/shard_map/ppermute | solution.py:38
  174.9 14.2 %collective-permute-start.47 = (bf16[256,896]{1,0:T(8,128)(2,1)S(1)}, bf16[256,896]{1,0:T(8,128)(2,1)S(1)}, u32[]{:S(2)}, u32[]{:S(2)}) collective-permute-start(bf16[256,896]{1,0:T(8,128)(2,1)S(1)} %collective-permute-done.43.refs_4_), channel_id=1, source_target_pairs={{0,2},{1,3},{2,4},{3,5},{4,6},{5,7},{6,0},{7,1},{8,10},{9,11},{10,... | collective-permute-start | bytes 1376264 | tf_op jit(solution)/shard_map/ppermute | solution.py:48
  174.9 17.3 %collective-permute-start.42 = (bf16[256,896]{1,0:T(8,128)(2,1)S(1)}, bf16[256,896]{1,0:T(8,128)(2,1)S(1)}, u32[]{:S(2)}, u32[]{:S(2)}) collective-permute-start(bf16[256,896]{1,0:T(8,128)(2,1)S(1)} %collective-permute-done.40.refs_5_), channel_id=1, source_target_pairs={{0,16},{8,24},{16,0},{24,8},{1,17},{9,25},{17,1},{25,9},{2,18},{10... | collective-permute-start | bytes 1376264 | tf_op jit(solution)/shard_map/ppermute | solution.py:38
  189.1 16.3 %collective-permute-start.48 = (bf16[256,896]{1,0:T(8,128)(2,1)S(1)}, bf16[256,896]{1,0:T(8,128)(2,1)S(1)}, u32[]{:S(2)}, u32[]{:S(2)}) collective-permute-start(bf16[256,896]{1,0:T(8,128)(2,1)S(1)} %collective-permute-done.47.refs_4_), channel_id=1, source_target_pairs={{0,8},{8,0},{16,24},{24,16},{1,9},{9,1},{17,25},{25,17},{2,10},{10... | collective-permute-start | bytes 1376264 | tf_op jit(solution)/shard_map/ppermute | solution.py:38
  190.2 15.3 %collective-permute-start.49 = (bf16[256,896]{1,0:T(8,128)(2,1)S(1)}, bf16[256,896]{1,0:T(8,128)(2,1)S(1)}, u32[]{:S(2)}, u32[]{:S(2)}) collective-permute-start(bf16[256,896]{1,0:T(8,128)(2,1)S(1)} %collective-permute-done.47.refs_4_), channel_id=1, source_target_pairs={{0,16},{8,24},{16,0},{24,8},{1,17},{9,25},{17,1},{25,9},{2,18},{10... | collective-permute-start | bytes 1376264 | tf_op jit(solution)/shard_map/ppermute | solution.py:38
  192.0 13.5 %collective-permute-start.52 = (bf16[256,896]{1,0:T(8,128)(2,1)S(1)}, bf16[256,896]{1,0:T(8,128)(2,1)S(1)}, u32[]{:S(2)}, u32[]{:S(2)}) collective-permute-start(bf16[256,896]{1,0:T(8,128)(2,1)S(1)} %collective-permute-done.47.refs_4_), channel_id=1, source_target_pairs={{0,2},{1,3},{2,4},{3,5},{4,6},{5,7},{6,0},{7,1},{8,10},{9,11},{10,... | collective-permute-start | bytes 1376264 | tf_op jit(solution)/shard_map/ppermute | solution.py:48
  192.0 17.3 %collective-permute-start.46 = (bf16[256,896]{1,0:T(8,128)(2,1)S(1)}, bf16[256,896]{1,0:T(8,128)(2,1)S(1)}, u32[]{:S(2)}, u32[]{:S(2)}) collective-permute-start(bf16[256,896]{1,0:T(8,128)(2,1)S(1)} %collective-permute-done.45.refs_6_), channel_id=1, source_target_pairs={{0,8},{8,0},{16,24},{24,16},{1,9},{9,1},{17,25},{25,17},{2,10},{10... | collective-permute-start | bytes 1376264 | tf_op jit(solution)/shard_map/ppermute | solution.py:38
  (74 other events, 1063.7 us)

commit v3 on v2

--- a/solution.py
+++ b/solution.py
@@ -10,6 +10,14 @@
 SPAN = 128
 EXTRA = 16
 VMEM_LIMIT = 30 * 1024 * 1024
+PLAN_X = (
+    "a010", "a110 S0", "a020 a121", "k1", "k0", "a210", "r12", "a310", "a220 a321", "r11",
+    "k2", "r22", "k3", "r32", "r21", "r31", "r02", "r01",
+)
+PLAN_E = (
+    "a010", "a110", "a020 a121", "a210", "d0", "d1", "a222", "a310 D0", "a322 D1", "d2", "d3",
+)
+DEPTH = 2
 BF = jnp.bfloat16
 F32 = jnp.float32
 
@@ -22,8 +30,8 @@
     def __init__(self):
         self.done = []
 
-    def send(self, items, after=()):
-        held = list(after) + (self.done[-2] if len(self.done) > 1 else [])
+    def send(self, items, after=(), depth=DEPTH):
+        held = list(after) + (self.done[-depth] if len(self.done) >= depth > 0 else [])
         out = []
         for x, bit in items:
             if held:
@@ -212,22 +220,21 @@
     aligned = share % SPAN == 0
     ns, fw = (nd, share) if aligned else (1, width)
 
+    mine = lax.dynamic_index_in_dim(block_codes, s, axis=1, keepdims=False)
+    everyone = lax.all_to_all(jnp.broadcast_to(mine, (npar, *mine.shape)), "dp", 0, 0)
+    codes = [everyone[(d + 2 * (nz - t)) % npar] for t in range(nz)]
     ring_x = [activations]
     for t in range(1, nz):
         ring_x.append(along_ring(ring_x[-1]))
-    codes = [lax.dynamic_index_in_dim(block_codes, s, axis=1, keepdims=False)]
-    for t in range(1, nz):
-        codes.append(along_ring(codes[-1]))
-    codes = jnp.stack(codes)
-    codes = jnp.concatenate([codes, to_sibling(codes)])
-    filled = codes >= 0
-    local = codes - s * shard_blocks
-    owner = jnp.where(filled, local // own_blocks, -1)
-    inner = jnp.where(filled, local % own_blocks, -1)
-    holders = jnp.stack([d, d ^ 1])[:, None, None, None]
-    match = owner == holders
-    picked = jnp.max(jnp.where(match, inner, -1), axis=(2, 3))
-    named = jnp.any(match, axis=3).astype(jnp.int32)
+
+    def pick(codes):
+        filled = codes >= 0
+        local = codes - s * shard_blocks
+        owner = jnp.where(filled, local // own_blocks, -1)
+        inner = jnp.where(filled, local % own_blocks, -1)
+        match = owner == jnp.stack([d, d ^ 1])[:, None, None, None]
+        picked = jnp.max(jnp.where(match, inner, -1), axis=(2, 3))
+        return picked, jnp.any(match, axis=3).astype(jnp.int32)
 
     order = s ^ jnp.arange(nd, dtype=jnp.int32)
     dec_rel = dec_bias.reshape(nd, share)[order].reshape(1, width)
@@ -240,15 +247,20 @@
     sib_b = to_sibling(own_b)
     place = order if aligned else jnp.zeros((1,), jnp.int32)
 
-    metas = jnp.concatenate(
-        [
-            jnp.maximum(picked[:, :nz], 0).T,
-            named[:, :nz].transpose(1, 2, 0).reshape(nz, 2 * ntb),
-            jnp.broadcast_to(place, (nz, place.shape[0])),
-        ],
-        axis=1,
-    )
-    metas = [metas[t] for t in range(nz)]
+    def metas_of(codes):
+        picked, named = pick(jnp.stack(codes))
+        n = len(codes)
+        metas = jnp.concatenate(
+            [
+                jnp.maximum(picked, 0).T,
+                named.transpose(1, 2, 0).reshape(n, 2 * ntb),
+                jnp.broadcast_to(place, (n, place.shape[0])),
+            ],
+            axis=1,
+        )
+        return [metas[t] for t in range(n)]
+
+    metas = metas_of(codes)
     base = 2 + 2 * ntb
 
     def w_specs():
@@ -281,7 +293,7 @@
 
     half = tokens // 2
 
-    def forward(slots, meta):
+    def forward(slots, meta, last):
         pieces, layout = flatten(slots)
         if aligned:
             out_layout, dtypes = [], []
@@ -291,7 +303,7 @@
                     dtypes.append(F32)
                 else:
                     out_layout += [(j, 0, half), (j, half, half)]
-                    dtypes += [BF if j == nd - 1 else F32] * 2
+                    dtypes += [last if j == nd - 1 else F32] * 2
         else:
             out_layout, dtypes = [(0, 0, tokens)], [F32]
         res = pl.pallas_call(
@@ -351,58 +363,71 @@
 
     levels = nd.bit_length() - 1
     paired = nd == 4 and nz == 4
-    steps = Steps()
+    results = {"K": {}, "D": {}, "C": {t: c for t, c in enumerate(codes)}}
+    accs, sib_terms = {}, {}
+
+    def run(plan, slots):
+        steps = Steps()
+        fed = {int(w[1]) for line in plan for w in line.split() if w[0] == "h"}
+        for line in plan:
+            words = line.split()
+            after, depth = [], DEPTH if paired else 0
+            for w in words:
+                if w[0] == "S":
+                    after += steps.done[int(w[1:])]
+                elif w[0] in results:
+                    after.append(results[w[0]][int(w[1:])])
+                elif w[0] == "/":
+                    depth = int(w[1:])
+            hold = lambda x: lax.optimization_barrier((x, *after))[0] if after else x
+            items, stores = [], []
+            for w in words:
+                if w[0] not in "arkdgh":
+                    continue
+                t = int(w[1])
+                if w[0] == "a":
+                    more, keys = gather_level(slots[t], int(w[2]), int(w[3]))
+                    stores.append((gather_store, slots[t], keys, len(items)))
+                    items += more
+                elif w[0] == "r":
+                    more, keys = scatter_level(accs[t], int(w[2]))
+                    stores.append((scatter_store, accs[t], keys, len(items)))
+                    items += more
+                elif w[0] == "k":
+                    last = F32 if t - 1 in fed else BF
+                    lat, accs[t] = forward([slots[t][j] for j in range(nd)], hold(metas[t]), last)
+                    results["K"][t] = lat
+                elif w[0] == "d":
+                    results["D"][t], theirs = backward(
+                        [x_slots[t][j] for j in range(nd)],
+                        [slots[t][j] for j in range(nd)],
+                        results["K"][t],
+                        hold(metas[t]),
+                    )
+                    sib_terms[t] = to_sibling(theirs)
+                elif w[0] == "g":
+                    slots[t][nd - 1] = [along_ring(hold(x)) for x in slots[t - 1][nd - 1]]
+                elif w[0] == "h":
+                    moved = [along_ring(hold(x.astype(BF))) for x in accs[t].pop(nd - 1)]
+                    accs[t + 1][nd - 1] = [x + y.astype(F32) for x, y in zip(accs[t + 1][nd - 1], moved)]
+            if items:
+                got = steps.send(items, after, depth)
+                for store, where, keys, at in stores:
+                    store(where, keys, got[at : at + len(keys)])
+
+    ring_order = list(range(1, nz)) + [0]
+    plan_x, plan_e = PLAN_X, PLAN_E
+    if not paired:
+        plan_x, plan_e = [], []
+        for t in range(nz):
+            gather = [f"a{t}{c}2" for c in range(1, levels + 1)]
+            plan_x += gather + [f"k{t}"]
+            plan_e += gather + [f"d{t}"]
+        plan_x += [f"r{t}{c}" for t in ring_order for c in range(levels, 0, -1)]
     x_slots = [{0: [x]} for x in ring_x]
-    x_left = {}
-
-    def x_step(*jobs):
-        items, spans = [], []
-        for t, count, mode in jobs:
-            more, keys = gather_level(x_slots[t], count, mode)
-            spans.append((t, keys, len(items)))
-            items += more
-        got = steps.send(items)
-        for t, keys, at in spans:
-            gather_store(x_slots[t], keys, got[at : at + len(keys)])
-
-    lats, accs = {}, {}
-
-    def encode(t):
-        lats[t], accs[t] = forward([x_slots[t][j] for j in range(nd)], metas[t])
-
-    def r_step(t, count):
-        items, keys = scatter_level(accs[t], count)
-        scatter_store(accs[t], keys, steps.send(items))
-
-    if paired:
-        x_step((0, 1, 0))
-        x_step((1, 1, 0))
-        x_step((0, 2, 0), (1, 2, 1))
-        encode(1)
-        encode(0)
-        x_step((2, 1, 0))
-        r_step(1, 2)
-        x_step((3, 1, 0))
-        x_step((2, 2, 0), (3, 2, 1))
-        r_step(1, 1)
-        encode(2)
-        r_step(2, 2)
-        encode(3)
-        r_step(3, 2)
-        r_step(2, 1)
-        r_step(0, 2)
-        r_step(3, 1)
-        r_step(0, 1)
-    else:
-        for t in range(nz):
-            for count in range(1, levels + 1):
-                x_step((t, count, 2))
-            encode(t)
-        for t in list(range(1, nz)) + [0]:
-            for count in range(levels, 0, -1):
-                r_step(t, count)
+    run(plan_x, x_slots)
     carry = None
-    for t in list(range(1, nz)) + [0]:
+    for t in ring_order:
         total = accs[t][0][0]
         if carry is not None:
             total = total + along_ring(carry.astype(BF)).astype(F32)
@@ -413,47 +438,12 @@
     ring_e = [error]
     for t in range(1, nz):
         ring_e.append(along_ring(ring_e[-1]))
-    e_slots = [{0: [e]} for e in ring_e]
-    own_terms, sib_terms = {}, {}
-    steps = Steps()
-
-    def e_step(*jobs, after=()):
-        items, spans = [], []
-        for t, count, mode in jobs:
-            more, keys = gather_level(e_slots[t], count, mode)
-            spans.append((t, keys, len(items)))
-            items += more
-        got = steps.send(items, after)
-        for t, keys, at in spans:
-            gather_store(e_slots[t], keys, got[at : at + len(keys)])
-
-    def decode(t):
-        own_terms[t], theirs = backward(
-            [x_slots[t][j] for j in range(nd)], [e_slots[t][j] for j in range(nd)], lats[t], metas[t]
-        )
-        sib_terms[t] = to_sibling(theirs)
-
-    if paired:
-        e_step((0, 1, 0))
-        e_step((1, 1, 0))
-        e_step((0, 2, 0), (1, 2, 1))
-        e_step((2, 1, 0))
-        decode(0)
-        decode(1)
-        e_step((2, 2, 2))
-        e_step((3, 1, 0), after=[own_terms[0]])
-        e_step((3, 2, 2), after=[own_terms[1]])
-        decode(2)
-        decode(3)
-    else:
-        for t in range(nz):
-            for count in range(1, levels + 1):
-                e_step((t, count, 2))
-            decode(t)
-    own_terms = [own_terms[t] for t in range(nz)]
+    run(plan_e, [{0: [e]} for e in ring_e])
+    own_terms = [results["D"][t] for t in range(nz)]
     sib_terms = [sib_terms[t] for t in range(nz)]
 
-    which = picked[0]
+    codes = jnp.stack(codes)
+    which = pick(jnp.concatenate([codes, to_sibling(codes)]))[0][0]
     terms = own_terms + sib_terms
     nt = len(terms)
     meta = jnp.concatenate([which, place])

time: 245 us -> 229 us (0.935)
  waiting for transfers between devices: 119 us -> 98.7 us
  starting transfers between devices: 57 us -> 61.3 us
    ppermute x12 -> x9, waiting for transfers between devices: 45.2 us -> 15.7 us  [along_ring(): return lax.ppermute(x, 'dp', [(i, (i + 2) % n) for i in range(n)])]
    ppermute x42, waiting for transfers between devices: 71.9 us -> 77.5 us  [over_dict(): return lax.ppermute(x, 'dict', [(i, i ^ bit) for i in range(n)])]
    all_to_all x0 -> x1, starting transfers between devices: none -> 3.87 us  [shards(): lax.all_to_all(jnp.broadcast_to(mine, (npar, *mine.shape)), 'dp', 0, 0)]
    all_to_all x0 -> x1, waiting for transfers between devices: none -> 3.35 us  [shards(): lax.all_to_all(jnp.broadcast_to(mine, (npar, *mine.shape)), 'dp', 0, 0)]
    ppermute x12 -> x9, starting transfers between devices: 4.64 us -> 7.03 us  [along_ring(): return lax.ppermute(x, 'dp', [(i, (i + 2) % n) for i in range(n)])]
    unnamed x95 -> x97, local copies, waits for them, and re-layouts: 12.3 us -> 12.3 us
  transfers between devices with their start and end apart: 61 -> 59, of which waited for: 30 -> 31; matrix products, arithmetic and copies ran while one was open for 3% -> 3% of each run, Pallas kernels for 15% -> 16%
where the time goes in v3:
time: 229 us; the launch traced here: 228 us
  waiting for transfers between devices  98.7 us (43%)
  starting transfers between devices  61.3 us (27%)
  Pallas kernels  45.4 us (20%)
  local copies, waits for them, and re-layouts  16 us (7%)
  other arithmetic  5.66 us (2%)
    ppermute x42, waiting for transfers between devices, over_dict(): return lax.ppermute(x, 'dict', [(i, i ^ bit) for i in range(n)])  77.5 us
    ppermute x42, starting transfers between devices, over_dict(): return lax.ppermute(x, 'dict', [(i, i ^ bit) for i in range(n)])  48.3 us
    pallas_call x4, Pallas kernels, backward(): pl.pallas_call(functools.partial(bwd_kernel, xl, el, ns, fw), grid_spec=p...  19.6 us
    pallas_call x4, Pallas kernels, forward(): pl.pallas_call(functools.partial(fwd_kernel, layout, ns, fw, out_layout),...  16.9 us
    ppermute x9, waiting for transfers between devices, along_ring(): return lax.ppermute(x, 'dp', [(i, (i + 2) % n) for i in range(n)])  15.7 us
    unnamed x97, local copies, waits for them, and re-layouts  12.3 us
    pallas_call x1, Pallas kernels, shards(): pl.pallas_call(functools.partial(sum_kernel, nt), grid_spec=pltpu.Prefetc...  8.86 us
    ppermute x9, starting transfers between devices, along_ring(): return lax.ppermute(x, 'dp', [(i, (i + 2) % n) for i in range(n)])  7.03 us
  transfers between devices with their start and end apart: 59, of which 31 were waited for; matrix products, arithmetic and copies ran while one was open for 3% of the time, Pallas kernels for 16%

profile of v3, /device:TPU:0, one launch (start us, length us, event | category | flops | bytes accessed | tf_op | source)
XLA Modules:
  0.0 228.4 jit_solution(3866379866604510052)
XLA Ops:
  1.2 2.6 %collective-permute-start.5 = (bf16[256,896]{1,0:T(8,128)(2,1)}, bf16[256,896]{1,0:T(8,128)(2,1)S(1)}, u32[]{:S(2)}, u32[]{:S(2)}) collective-permute-start(bf16[256,896]{1,0:T(8,128)(2,1)} %refs_0_.3), channel_id=1, source_target_pairs={{0,2},{1,3},{2,4},{3,5},{4,6},{5,7},{6,0},{7,1},{8,10},{9,11},{10,... | collective-permute-start | bytes 1376264 | tf_op jit(solution)/shard_map/ppermute | solution.py:56
  7.4 3.9 %all-to-all-start = ((s32[8,2,8]{2,1,0:T(2,128)}), s32[8,2,8]{2,1,0:T(2,128)S(1)}, u32[]{:S(2)}, u32[]{:S(2)}) async-start(s32[8,2,8]{2,1,0:T(2,128)} %broadcast_in_dim.34), calls=%async_computation | async-start | bytes 16384 | tf_op jit(solution)/shard_map/all_to_all | solution.py:224
  14.0 3.4 %all-to-all-done = s32[8,2,8]{2,1,0:T(2,128)S(1)} async-done(((s32[8,2,8]{2,1,0:T(2,128)}), s32[8,2,8]{2,1,0:T(2,128)S(1)}, u32[]{:S(2)}, u32[]{:S(2)}) %all-to-all-start) | async-done | bytes 544 | tf_op jit(solution)/shard_map/all_to_all | solution.py:224
  21.8 8.1 %collective-permute-done.8.refs_2_ = bf16[256,896]{1,0:T(8,128)(2,1)S(1)} collective-permute-done((bf16[256,896]{1,0:T(8,128)(2,1)S(1)}, bf16[256,896]{1,0:T(8,128)(2,1)S(1)}, u32[]{:S(2)}, u32[]{:S(2)}) %collective-permute-start.8) | collective-permute-done | bytes 458784 | tf_op jit(solution)/shard_map/ppermute | solution.py:46
  35.5 7.8 %collective-permute-done.11.refs_3_ = bf16[256,896]{1,0:T(8,128)(2,1)S(1)} collective-permute-done((bf16[256,896]{1,0:T(8,128)(2,1)S(1)}, bf16[256,896]{1,0:T(8,128)(2,1)S(1)}, u32[]{:S(2)}, u32[]{:S(2)}) %collective-permute-start.11) | collective-permute-done | bytes 458784 | tf_op jit(solution)/shard_map/ppermute | solution.py:46
  44.4 3.1 %copy-done.2 = bf16[1024,3584]{1,0:T(8,128)(2,1)S(1)} copy-done((bf16[1024,3584]{1,0:T(8,128)(2,1)S(1)}, bf16[1024,3584]{1,0:T(8,128)(2,1)}, u32[]{:S(2)}) %copy-start.2) | copy-done | bytes 7340056
  47.5 4.4 %shard_map.77 = (bf16[256,256]{1,0:T(8,128)(2,1)S(1)}, f32[256,896]{1,0:T(8,128)S(1)}, f32[256,896]{1,0:T(8,128)S(1)}, f32[256,896]{1,0:T(8,128)S(1)}, bf16[128,...) custom-call(s32[10]{0:T(128)S(1)} %get-tuple-element.147.meta, bf16[256,896]{1,0:T(8,128)(2,1)S(1)} %collective-permute-done.5.refs_0_, ...), custom_call_target="tpu_custom_call" | custom-call | flops 939524096 | bytes 7340032 | tf_op jit(solution)/shard_map/pallas_call | solution.py:309
  57.1 3.4 %collective-permute-done.13 = bf16[128,896]{1,0:T(8,128)(2,1)S(1)} collective-permute-done((bf16[128,896]{1,0:T(8,128)(2,1)S(1)}, bf16[128,896]{1,0:T(8,128)(2,1)S(1)}, u32[]{:S(2)}, u32[]{:S(2)}) %collective-permute-start.13) | collective-permute-done | bytes 229408 | tf_op jit(solution)/shard_map/ppermute | solution.py:46
  63.1 2.8 %collective-permute-done.23.refs_1_ = bf16[256,896]{1,0:T(8,128)(2,1)S(1)} collective-permute-done((bf16[256,896]{1,0:T(8,128)(2,1)S(1)}, bf16[256,896]{1,0:T(8,128)(2,1)S(1)}, u32[]{:S(2)}, u32[]{:S(2)}) %collective-permute-start.23) | collective-permute-done | bytes 458784 | tf_op jit(solution)/shard_map/ppermute | solution.py:46
  65.9 5.4 %collective-permute-done.16.refs_2_ = bf16[256,896]{1,0:T(8,128)(2,1)S(1)} collective-permute-done((bf16[256,896]{1,0:T(8,128)(2,1)S(1)}, bf16[256,896]{1,0:T(8,128)(2,1)S(1)}, u32[]{:S(2)}, u32[]{:S(2)}) %collective-permute-start.16) | collective-permute-done | bytes 458784 | tf_op jit(solution)/shard_map/ppermute | solution.py:46
  74.9 4.2 %shard_map.76 = (bf16[256,256]{1,0:T(8,128)(2,1)S(1)}, f32[256,896]{1,0:T(8,128)S(1)}, f32[256,896]{1,0:T(8,128)S(1)}, f32[256,896]{1,0:T(8,128)S(1)}, bf16[128,...) custom-call(s32[10]{0:T(128)S(1)} %get-tuple-element.145.meta, bf16[256,896]{1,0:T(8,128)(2,1)S(1)} %copy-done.5, ...), custom_call_target="tpu_custom_call" | custom-call | flops 939524096 | bytes 7340032 | tf_op jit(solution)/shard_map/pallas_call | solution.py:309
  79.1 2.1 collective-permute-done.14.refs_3_
  81.2 4.2 %shard_map.78 = (bf16[256,256]{1,0:T(8,128)(2,1)S(1)}, f32[256,896]{1,0:T(8,128)S(1)}, f32[256,896]{1,0:T(8,128)S(1)}, f32[256,896]{1,0:T(8,128)S(1)}, bf16[128,...) custom-call(s32[10]{0:T(128)S(1)} %get-tuple-element.148.meta, bf16[256,896]{1,0:T(8,128)(2,1)S(1)} %collective-permute-done.6.refs_0_, ...), custom_call_target="tpu_custom_call" | custom-call | flops 939524096 | bytes 7340032 | tf_op jit(solution)/shard_map/pallas_call | solution.py:309
  91.1 4.2 %shard_map.79 = (bf16[256,256]{1,0:T(8,128)(2,1)S(1)}, f32[256,896]{1,0:T(8,128)S(1)}, f32[256,896]{1,0:T(8,128)S(1)}, f32[256,896]{1,0:T(8,128)S(1)}, bf16[128,...) custom-call(s32[10]{0:T(128)S(1)} %get-tuple-element.146.meta, bf16[256,896]{1,0:T(8,128)(2,1)S(1)} %collective-permute-done.15.refs_0_, ...), custom_call_target="tpu_custom_call" | custom-call | flops 939524096 | bytes 7340032 | tf_op jit(solution)/shard_map/pallas_call | solution.py:309
  100.2 3.7 %collective-permute-done.27 = bf16[128,896]{1,0:T(8,128)(2,1)S(1)} collective-permute-done((bf16[128,896]{1,0:T(8,128)(2,1)S(1)}, bf16[128,896]{1,0:T(8,128)(2,1)S(1)}, u32[]{:S(2)}, u32[]{:S(2)}) %collective-permute-start.27) | collective-permute-done | bytes 229408 | tf_op jit(solution)/shard_map/ppermute | solution.py:46
  106.6 7.8 %collective-permute-done.21 = bf16[256,896]{1,0:T(8,128)(2,1)S(1)} collective-permute-done((bf16[256,896]{1,0:T(8,128)(2,1)S(1)}, bf16[256,896]{1,0:T(8,128)(2,1)S(1)}, u32[]{:S(2)}, u32[]{:S(2)}) %collective-permute-start.21) | collective-permute-done | bytes 458784 | tf_op jit(solution)/shard_map/ppermute | solution.py:46
  117.8 4.3 %collective-permute-done.31 = bf16[128,896]{1,0:T(8,128)(2,1)S(1)} collective-permute-done((bf16[128,896]{1,0:T(8,128)(2,1)S(1)}, bf16[128,896]{1,0:T(8,128)(2,1)S(1)}, u32[]{:S(2)}, u32[]{:S(2)}) %collective-permute-start.31) | collective-permute-done | bytes 229408 | tf_op jit(solution)/shard_map/ppermute | solution.py:46
  122.1 2.9 %collective-permute-done.22 = bf16[128,896]{1,0:T(8,128)(2,1)S(1)} collective-permute-done((bf16[128,896]{1,0:T(8,128)(2,1)S(1)}, bf16[128,896]{1,0:T(8,128)(2,1)S(1)}, u32[]{:S(2)}, u32[]{:S(2)}) %collective-permute-start.22) | collective-permute-done | bytes 229408 | tf_op jit(solution)/shard_map/ppermute | solution.py:46
  130.6 4.3 %collective-permute-done.32 = bf16[256,896]{1,0:T(8,128)(2,1)} collective-permute-done((bf16[256,896]{1,0:T(8,128)(2,1)}, bf16[256,896]{1,0:T(8,128)(2,1)}, u32[]{:S(2)}, u32[]{:S(2)}) %collective-permute-start.32) | collective-permute-done | bytes 458784 | tf_op jit(solution)/shard_map/ppermute | solution.py:46
  135.8 3.8 %collective-permute-done.35 = bf16[256,896]{1,0:T(8,128)(2,1)} collective-permute-done((bf16[256,896]{1,0:T(8,128)(2,1)}, bf16[256,896]{1,0:T(8,128)(2,1)}, u32[]{:S(2)}, u32[]{:S(2)}) %collective-permute-start.35) | collective-permute-done | bytes 458784 | tf_op jit(solution)/shard_map/ppermute | solution.py:56
  139.6 2.0 subtract_convert_fusion.refs_4_
  144.1 9.3 %collective-permute-done.40.refs_4_ = bf16[256,896]{1,0:T(8,128)(2,1)S(1)} collective-permute-done((bf16[256,896]{1,0:T(8,128)(2,1)S(1)}, bf16[256,896]{1,0:T(8,128)(2,1)S(1)}, u32[]{:S(2)}, u32[]{:S(2)}) %collective-permute-start.40) | collective-permute-done | bytes 458784 | tf_op jit(solution)/shard_map/ppermute | solution.py:56
  156.9 7.5 %collective-permute-done.41.refs_5_ = bf16[256,896]{1,0:T(8,128)(2,1)S(1)} collective-permute-done((bf16[256,896]{1,0:T(8,128)(2,1)S(1)}, bf16[256,896]{1,0:T(8,128)(2,1)S(1)}, u32[]{:S(2)}, u32[]{:S(2)}) %collective-permute-start.41) | collective-permute-done | bytes 458784 | tf_op jit(solution)/shard_map/ppermute | solution.py:46
  164.5 2.9 %collective-permute-done.42.refs_6_ = bf16[256,896]{1,0:T(8,128)(2,1)S(1)} collective-permute-done((bf16[256,896]{1,0:T(8,128)(2,1)S(1)}, bf16[256,896]{1,0:T(8,128)(2,1)S(1)}, u32[]{:S(2)}, u32[]{:S(2)}) %collective-permute-start.42) | collective-permute-done | bytes 458784 | tf_op jit(solution)/shard_map/ppermute | solution.py:46
  172.1 4.0 %collective-permute-done.39.refs_7_ = bf16[256,896]{1,0:T(8,128)(2,1)S(1)} collective-permute-done((bf16[256,896]{1,0:T(8,128)(2,1)S(1)}, bf16[256,896]{1,0:T(8,128)(2,1)S(1)}, u32[]{:S(2)}, u32[]{:S(2)}) %collective-permute-start.39) | collective-permute-done | bytes 458784 | tf_op jit(solution)/shard_map/ppermute | solution.py:46
  176.2 3.1 %copy-done.4 = bf16[1024,3584]{1,0:T(8,128)(2,1)S(1)} copy-done((bf16[1024,3584]{1,0:T(8,128)(2,1)S(1)}, bf16[1024,3584]{1,0:T(8,128)(2,1)}, u32[]{:S(2)}) %copy-start.4) | copy-done | bytes 7340056
  184.3 5.1 %shard_map.80 = (bf16[144,3584]{1,0:T(8,128)(2,1)S(1)}, bf16[144,3584]{1,0:T(8,128)(2,1)S(1)}) custom-call(s32[10]{0:T(128)S(1)} %get-tuple-element.145.meta, bf16[256,896]{1,0:T(8,128)(2,1)S(1)} %copy-done.6, bf16[256,896]{1,0:T(8,128)(2,1)S(1)} %copy-done.10, bf16[256,896]{1,0:T(8,128)(2,1)S(1)} %copy-done.12, bf16[256,896]{1,0:T(8,128)(2,1)S(1)} %copy-done.36, ...), custom_call_target="tpu_custom_call" | custom-call | flops 1409286144 | bytes 9175040 | tf_op jit(solution)/shard_map/pallas_call | solution.py:342
  193.8 4.8 %shard_map.81 = (bf16[144,3584]{1,0:T(8,128)(2,1)S(1)}, bf16[144,3584]{1,0:T(8,128)(2,1)S(1)}) custom-call(s32[10]{0:T(128)S(1)} %get-tuple-element.147.meta, bf16[256,896]{1,0:T(8,128)(2,1)S(1)} %copy-done.8, bf16[256,896]{1,0:T(8,128)(2,1)S(1)} %copy-done.24, bf16[256,896]{1,0:T(8,128)(2,1)S(1)} %copy-done.16, bf16[256,896]{1,0:T(8,128)(2,1)S(1)} %copy-done.26, ...), custom_call_target="tpu_custom_call" | custom-call | flops 1409286144 | bytes 9175040 | tf_op jit(solution)/shard_map/pallas_call | solution.py:342
  205.7 4.8 %shard_map.82 = (bf16[144,3584]{1,0:T(8,128)(2,1)S(1)}, bf16[144,3584]{1,0:T(8,128)(2,1)S(1)}) custom-call(s32[10]{0:T(128)S(1)} %get-tuple-element.148.meta, bf16[256,896]{1,0:T(8,128)(2,1)S(1)} %copy-done.14, bf16[256,896]{1,0:T(8,128)(2,1)S(1)} %copy-done.20, bf16[256,896]{1,0:T(8,128)(2,1)S(1)} %copy-done.22, bf16[256,896]{1,0:T(8,128)(2,1)S(1)} %copy-done.34, ...), custom_call_target="tpu_custom_call" | custom-call | flops 1409286144 | bytes 9175040 | tf_op jit(solution)/shard_map/pallas_call | solution.py:342
  210.7 4.8 %shard_map.83 = (bf16[144,3584]{1,0:T(8,128)(2,1)S(1)}, bf16[144,3584]{1,0:T(8,128)(2,1)S(1)}) custom-call(s32[10]{0:T(128)S(1)} %get-tuple-element.146.meta, bf16[256,896]{1,0:T(8,128)(2,1)S(1)} %copy-done.18, bf16[256,896]{1,0:T(8,128)(2,1)S(1)} %copy-done.28, bf16[256,896]{1,0:T(8,128)(2,1)S(1)} %copy-done.30, bf16[256,896]{1,0:T(8,128)(2,1)S(1)} %copy-done.32, ...), custom_call_target="tpu_custom_call" | custom-call | flops 1409286144 | bytes 9175040 | tf_op jit(solution)/shard_map/pallas_call | solution.py:342
  217.0 2.1 collective-permute-done.36
  219.5 8.9 %shard_map.84 = (f32[8,128,3584]{2,1,0:T(8,128)}, f32[8,1,128]{2,1,0:T(1,128)}) custom-call(s32[12]{0:T(128)S(1)} %pad_add_fusion.2.meta, bf16[144,3584]{1,0:T(8,128)(2,1)S(1)} %get-tuple-element.113.refs_0_.refs_8_, bf16[144,3584]{1,0:T(8,128)(2,1)S(1)} %get-tuple-element.116.refs_1_.refs_9_, bf16[144,3584]{1,0:T(8,128)(2,1)S(1)} %get-tuple-element.121.refs_2_.refs_10_, ...), custom_call_target="tpu_custom_call" | custom-call | flops 3670016 | bytes 22020096 | tf_op jit(solution)/shard_map/pallas_call | solution.py:450
  (238 shorter events, 81.5 us)
Async XLA Ops:
  0.6 43.7 %collective-permute-start.3 = (bf16[8,128,3584]{2,1,0:T(8,128)(2,1)}, bf16[8,128,3584]{2,1,0:T(8,128)(2,1)}, u32[]{:S(2)}, u32[]{:S(2)}) collective-permute-start(bf16[8,128,3584]{2,1,0:T(8,128)(2,1)} %bitcast.27), channel_id=1, source_target_pairs={{0,1},{1,0},{2,3},{3,2},{4,5},{5,4},{6,7},{7,6},{8,9},{9,8},{10,11... | collective-permute-start | bytes 22020104 | tf_op jit(solution)/shard_map/ppermute | solution.py:51
  1.2 16.2 %collective-permute-start.5 = (bf16[256,896]{1,0:T(8,128)(2,1)}, bf16[256,896]{1,0:T(8,128)(2,1)S(1)}, u32[]{:S(2)}, u32[]{:S(2)}) collective-permute-start(bf16[256,896]{1,0:T(8,128)(2,1)} %refs_0_.3), channel_id=1, source_target_pairs={{0,2},{1,3},{2,4},{3,5},{4,6},{5,7},{6,0},{7,1},{8,10},{9,11},{10,... | collective-permute-start | bytes 1376264 | tf_op jit(solution)/shard_map/ppermute | solution.py:56
  3.8 13.6 %collective-permute-start = (bf16[256,896]{1,0:T(8,128)(2,1)}, bf16[256,896]{1,0:T(8,128)(2,1)S(1)}, u32[]{:S(2)}, u32[]{:S(2)}) collective-permute-start(bf16[256,896]{1,0:T(8,128)(2,1)} %refs_0_.3), channel_id=1, source_target_pairs={{0,8},{8,0},{16,24},{24,16},{1,9},{9,1},{17,25},{25,17},{2,10},{10... | collective-permute-start | bytes 1376264 | tf_op jit(solution)/shard_map/ppermute | solution.py:46
  5.3 12.5 %collective-permute-start.1 = (bf16[256,896]{1,0:T(8,128)(2,1)}, bf16[256,896]{1,0:T(8,128)(2,1)S(1)}, u32[]{:S(2)}, u32[]{:S(2)}) collective-permute-start(bf16[256,896]{1,0:T(8,128)(2,1)} %refs_0_.3), channel_id=1, source_target_pairs={{0,16},{8,24},{16,0},{24,8},{1,17},{9,25},{17,1},{25,9},{2,18},{10... | collective-permute-start | bytes 1376264 | tf_op jit(solution)/shard_map/ppermute | solution.py:46
  12.0 23.1 %collective-permute-start.4 = (bf16[8,1,128]{2,1,0:T(2,128)(2,1)S(1)}, bf16[8,1,128]{2,1,0:T(2,128)(2,1)S(1)}, u32[]{:S(2)}, u32[]{:S(2)}) collective-permute-start(bf16[8,1,128]{2,1,0:T(2,128)(2,1)S(1)} %copy.33.refs_13_), channel_id=1, source_target_pairs={{0,1},{1,0},{2,3},{3,2},{4,5},{5,4},{6,7},{7,6},{8,9},{9,8},{10,11... | collective-permute-start | bytes 6152 | tf_op jit(solution)/shard_map/ppermute | solution.py:51
  19.6 12.3 %collective-permute-start.7 = (bf16[256,896]{1,0:T(8,128)(2,1)S(1)}, bf16[256,896]{1,0:T(8,128)(2,1)S(1)}, u32[]{:S(2)}, u32[]{:S(2)}) collective-permute-start(bf16[256,896]{1,0:T(8,128)(2,1)S(1)} %collective-permute-done.5.refs_0_), channel_id=1, source_target_pairs={{0,8},{8,0},{16,24},{24,16},{1,9},{9,1},{17,25},{25,17},{2,10},{10... | collective-permute-start | bytes 1376264 | tf_op jit(solution)/shard_map/ppermute | solution.py:46
  20.8 13.7 %collective-permute-start.6 = (bf16[256,896]{1,0:T(8,128)(2,1)S(1)}, bf16[256,896]{1,0:T(8,128)(2,1)S(1)}, u32[]{:S(2)}, u32[]{:S(2)}) collective-permute-start(bf16[256,896]{1,0:T(8,128)(2,1)S(1)} %collective-permute-done.5.refs_0_), channel_id=1, source_target_pairs={{0,2},{1,3},{2,4},{3,5},{4,6},{5,7},{6,0},{7,1},{8,10},{9,11},{10,... | collective-permute-start | bytes 1376264 | tf_op jit(solution)/shard_map/ppermute | solution.py:56
  29.9 13.5 %collective-permute-start.11 = (bf16[256,896]{1,0:T(8,128)(2,1)S(1)}, bf16[256,896]{1,0:T(8,128)(2,1)S(1)}, u32[]{:S(2)}, u32[]{:S(2)}) collective-permute-start(bf16[256,896]{1,0:T(8,128)(2,1)S(1)} %collective-permute-done.8.refs_2_), channel_id=1, source_target_pairs={{0,8},{8,0},{16,24},{24,16},{1,9},{9,1},{17,25},{25,17},{2,10},{10... | collective-permute-start | bytes 1376264 | tf_op jit(solution)/shard_map/ppermute | solution.py:46
  31.9 20.0 %collective-permute-start.2 = (bf16[256,896]{1,0:T(8,128)(2,1)S(1)}, bf16[256,896]{1,0:T(8,128)(2,1)S(1)}, u32[]{:S(2)}, u32[]{:S(2)}) collective-permute-start(bf16[256,896]{1,0:T(8,128)(2,1)S(1)} %collective-permute-done.refs_1_), channel_id=1, source_target_pairs={{0,16},{8,24},{16,0},{24,8},{1,17},{9,25},{17,1},{25,9},{2,18},{10... | collective-permute-start | bytes 1376264 | tf_op jit(solution)/shard_map/ppermute | solution.py:46
  34.5 19.9 %collective-permute-start.9 = (bf16[256,896]{1,0:T(8,128)(2,1)S(1)}, bf16[256,896]{1,0:T(8,128)(2,1)S(1)}, u32[]{:S(2)}, u32[]{:S(2)}) collective-permute-start(bf16[256,896]{1,0:T(8,128)(2,1)S(1)} %collective-permute-done.6.refs_0_), channel_id=1, source_target_pairs={{0,8},{8,0},{16,24},{24,16},{1,9},{9,1},{17,25},{25,17},{2,10},{10... | collective-permute-start | bytes 1376264 | tf_op jit(solution)/shard_map/ppermute | solution.py:46
  35.1 19.6 %collective-permute-start.10 = (bf16[256,896]{1,0:T(8,128)(2,1)S(1)}, bf16[256,896]{1,0:T(8,128)(2,1)S(1)}, u32[]{:S(2)}, u32[]{:S(2)}) collective-permute-start(bf16[256,896]{1,0:T(8,128)(2,1)S(1)} %collective-permute-done.6.refs_0_), channel_id=1, source_target_pairs={{0,16},{8,24},{16,0},{24,8},{1,17},{9,25},{17,1},{25,9},{2,18},{10... | collective-permute-start | bytes 1376264 | tf_op jit(solution)/shard_map/ppermute | solution.py:46
  56.1 15.2 %collective-permute-start.16 = (bf16[256,896]{1,0:T(8,128)(2,1)S(1)}, bf16[256,896]{1,0:T(8,128)(2,1)S(1)}, u32[]{:S(2)}, u32[]{:S(2)}) collective-permute-start(bf16[256,896]{1,0:T(8,128)(2,1)S(1)} %collective-permute-done.15.refs_0_), channel_id=1, source_target_pairs={{0,16},{8,24},{16,0},{24,8},{1,17},{9,25},{17,1},{25,9},{2,18},{10... | collective-permute-start | bytes 1376264 | tf_op jit(solution)/shard_map/ppermute | solution.py:46
  61.5 19.7 %collective-permute-start.14 = (bf16[256,896]{1,0:T(8,128)(2,1)S(1)}, bf16[256,896]{1,0:T(8,128)(2,1)S(1)}, u32[]{:S(2)}, u32[]{:S(2)}) collective-permute-start(bf16[256,896]{1,0:T(8,128)(2,1)S(1)} %collective-permute-done.9.refs_1_), channel_id=1, source_target_pairs={{0,16},{8,24},{16,0},{24,8},{1,17},{9,25},{17,1},{25,9},{2,18},{10... | collective-permute-start | bytes 1376264 | tf_op jit(solution)/shard_map/ppermute | solution.py:46
  71.3 14.1 %collective-permute-start.17 = (bf16[256,896]{1,0:T(8,128)(2,1)S(1)}, bf16[256,896]{1,0:T(8,128)(2,1)S(1)}, u32[]{:S(2)}, u32[]{:S(2)}) collective-permute-start(bf16[256,896]{1,0:T(8,128)(2,1)S(1)} %collective-permute-done.16.refs_2_), channel_id=1, source_target_pairs={{0,8},{8,0},{16,24},{24,16},{1,9},{9,1},{17,25},{25,17},{2,10},{10... | collective-permute-start | bytes 1376264 | tf_op jit(solution)/shard_map/ppermute | solution.py:46
  72.4 15.3 %collective-permute-start.25 = (bf16[256,896]{1,0:T(8,128)(2,1)S(1)}, bf16[256,896]{1,0:T(8,128)(2,1)S(1)}, u32[]{:S(2)}, u32[]{:S(2)}) collective-permute-start(bf16[256,896]{1,0:T(8,128)(2,1)S(1)} %get-tuple-element.96), channel_id=1, source_target_pairs={{0,16},{8,24},{16,0},{24,8},{1,17},{9,25},{17,1},{25,9},{2,18},{10... | collective-permute-start | bytes 1376264 | tf_op jit(solution)/shard_map/ppermute | solution.py:46
  73.9 15.2 %collective-permute-start.24 = (bf16[256,896]{1,0:T(8,128)(2,1)S(1)}, bf16[256,896]{1,0:T(8,128)(2,1)S(1)}, u32[]{:S(2)}, u32[]{:S(2)}) collective-permute-start(bf16[256,896]{1,0:T(8,128)(2,1)S(1)} %get-tuple-element.94), channel_id=1, source_target_pairs={{0,8},{8,0},{16,24},{24,16},{1,9},{9,1},{17,25},{25,17},{2,10},{10... | collective-permute-start | bytes 1376264 | tf_op jit(solution)/shard_map/ppermute | solution.py:46
  89.3 27.0 %collective-permute-start.33 = (bf16[256,896]{1,0:T(8,128)(2,1)S(1)}, bf16[256,896]{1,0:T(8,128)(2,1)S(1)}, u32[]{:S(2)}, u32[]{:S(2)}) collective-permute-start(bf16[256,896]{1,0:T(8,128)(2,1)S(1)} %add_convert_fusion.2), channel_id=1, source_target_pairs={{0,2},{1,3},{2,4},{3,5},{4,6},{5,7},{6,0},{7,1},{8,10},{9,11},{10,... | collective-permute-start | bytes 1376264 | tf_op jit(solution)/shard_map/ppermute | solution.py:56
  98.0 16.4 %collective-permute-start.21 = (bf16[256,896]{1,0:T(8,128)(2,1)S(1)}, bf16[256,896]{1,0:T(8,128)(2,1)S(1)}, u32[]{:S(2)}, u32[]{:S(2)}) collective-permute-start(bf16[256,896]{1,0:T(8,128)(2,1)S(1)} %add_convert_fusion.9), channel_id=1, source_target_pairs={{0,16},{8,24},{16,0},{24,8},{1,17},{9,25},{17,1},{25,9},{2,18},{10... | collective-permute-start | bytes 1376264 | tf_op jit(solution)/shard_map/ppermute | solution.py:46
  99.6 14.8 %collective-permute-start.20 = (bf16[256,896]{1,0:T(8,128)(2,1)S(1)}, bf16[256,896]{1,0:T(8,128)(2,1)S(1)}, u32[]{:S(2)}, u32[]{:S(2)}) collective-permute-start(bf16[256,896]{1,0:T(8,128)(2,1)S(1)} %add_convert_fusion.10), channel_id=1, source_target_pairs={{0,8},{8,0},{16,24},{24,16},{1,9},{9,1},{17,25},{25,17},{2,10},{10... | collective-permute-start | bytes 1376264 | tf_op jit(solution)/shard_map/ppermute | solution.py:46
  104.5 21.5 %collective-permute-start.29 = (bf16[256,896]{1,0:T(8,128)(2,1)S(1)}, bf16[256,896]{1,0:T(8,128)(2,1)S(1)}, u32[]{:S(2)}, u32[]{:S(2)}) collective-permute-start(bf16[256,896]{1,0:T(8,128)(2,1)S(1)} %add_convert_fusion.4), channel_id=1, source_target_pairs={{0,16},{8,24},{16,0},{24,8},{1,17},{9,25},{17,1},{25,9},{2,18},{10... | collective-permute-start | bytes 1376264 | tf_op jit(solution)/shard_map/ppermute | solution.py:46
  105.5 20.6 %collective-permute-start.28 = (bf16[256,896]{1,0:T(8,128)(2,1)S(1)}, bf16[256,896]{1,0:T(8,128)(2,1)S(1)}, u32[]{:S(2)}, u32[]{:S(2)}) collective-permute-start(bf16[256,896]{1,0:T(8,128)(2,1)S(1)} %add_convert_fusion.5), channel_id=1, source_target_pairs={{0,8},{8,0},{16,24},{24,16},{1,9},{9,1},{17,25},{25,17},{2,10},{10... | collective-permute-start | bytes 1376264 | tf_op jit(solution)/shard_map/ppermute | solution.py:46
  141.7 13.6 %collective-permute-start.37 = (bf16[256,896]{1,0:T(8,128)(2,1)S(1)}, bf16[256,896]{1,0:T(8,128)(2,1)S(1)}, u32[]{:S(2)}, u32[]{:S(2)}) collective-permute-start(bf16[256,896]{1,0:T(8,128)(2,1)S(1)} %subtract_convert_fusion.refs_4_), channel_id=1, source_target_pairs={{0,8},{8,0},{16,24},{24,16},{1,9},{9,1},{17,25},{25,17},{2,10},{10... | collective-permute-start | bytes 1376264 | tf_op jit(solution)/shard_map/ppermute | solution.py:46
  153.9 13.5 %collective-permute-start.42 = (bf16[256,896]{1,0:T(8,128)(2,1)S(1)}, bf16[256,896]{1,0:T(8,128)(2,1)S(1)}, u32[]{:S(2)}, u32[]{:S(2)}) collective-permute-start(bf16[256,896]{1,0:T(8,128)(2,1)S(1)} %collective-permute-done.40.refs_4_), channel_id=1, source_target_pairs={{0,16},{8,24},{16,0},{24,8},{1,17},{9,25},{17,1},{25,9},{2,18},{10... | collective-permute-start | bytes 1376264 | tf_op jit(solution)/shard_map/ppermute | solution.py:46
  155.3 13.6 %collective-permute-start.44 = (bf16[256,896]{1,0:T(8,128)(2,1)S(1)}, bf16[256,896]{1,0:T(8,128)(2,1)S(1)}, u32[]{:S(2)}, u32[]{:S(2)}) collective-permute-start(bf16[256,896]{1,0:T(8,128)(2,1)S(1)} %collective-permute-done.40.refs_4_), channel_id=1, source_target_pairs={{0,2},{1,3},{2,4},{3,5},{4,6},{5,7},{6,0},{7,1},{8,10},{9,11},{10,... | collective-permute-start | bytes 1376264 | tf_op jit(solution)/shard_map/ppermute | solution.py:56
  155.3 20.9 %collective-permute-start.39 = (bf16[256,896]{1,0:T(8,128)(2,1)S(1)}, bf16[256,896]{1,0:T(8,128)(2,1)S(1)}, u32[]{:S(2)}, u32[]{:S(2)}) collective-permute-start(bf16[256,896]{1,0:T(8,128)(2,1)S(1)} %collective-permute-done.37.refs_5_), channel_id=1, source_target_pairs={{0,16},{8,24},{16,0},{24,8},{1,17},{9,25},{17,1},{25,9},{2,18},{10... | collective-permute-start | bytes 1376264 | tf_op jit(solution)/shard_map/ppermute | solution.py:46
  168.9 20.5 %collective-permute-start.45 = (bf16[256,896]{1,0:T(8,128)(2,1)S(1)}, bf16[256,896]{1,0:T(8,128)(2,1)S(1)}, u32[]{:S(2)}, u32[]{:S(2)}) collective-permute-start(bf16[256,896]{1,0:T(8,128)(2,1)S(1)} %collective-permute-done.44.refs_4_), channel_id=1, source_target_pairs={{0,8},{8,0},{16,24},{24,16},{1,9},{9,1},{17,25},{25,17},{2,10},{10... | collective-permute-start | bytes 1376264 | tf_op jit(solution)/shard_map/ppermute | solution.py:46
  170.6 18.9 %collective-permute-start.46 = (bf16[256,896]{1,0:T(8,128)(2,1)S(1)}, bf16[256,896]{1,0:T(8,128)(2,1)S(1)}, u32[]{:S(2)}, u32[]{:S(2)}) collective-permute-start(bf16[256,896]{1,0:T(8,128)(2,1)S(1)} %collective-permute-done.44.refs_4_), channel_id=1, source_target_pairs={{0,16},{8,24},{16,0},{24,8},{1,17},{9,25},{17,1},{25,9},{2,18},{10... | collective-permute-start | bytes 1376264 | tf_op jit(solution)/shard_map/ppermute | solution.py:46
  170.9 18.6 %collective-permute-start.49 = (bf16[256,896]{1,0:T(8,128)(2,1)S(1)}, bf16[256,896]{1,0:T(8,128)(2,1)S(1)}, u32[]{:S(2)}, u32[]{:S(2)}) collective-permute-start(bf16[256,896]{1,0:T(8,128)(2,1)S(1)} %collective-permute-done.44.refs_4_), channel_id=1, source_target_pairs={{0,2},{1,3},{2,4},{3,5},{4,6},{5,7},{6,0},{7,1},{8,10},{9,11},{10,... | collective-permute-start | bytes 1376264 | tf_op jit(solution)/shard_map/ppermute | solution.py:56
  170.9 20.8 %collective-permute-start.43 = (bf16[256,896]{1,0:T(8,128)(2,1)S(1)}, bf16[256,896]{1,0:T(8,128)(2,1)S(1)}, u32[]{:S(2)}, u32[]{:S(2)}) collective-permute-start(bf16[256,896]{1,0:T(8,128)(2,1)S(1)} %collective-permute-done.42.refs_6_), channel_id=1, source_target_pairs={{0,8},{8,0},{16,24},{24,16},{1,9},{9,1},{17,25},{25,17},{2,10},{10... | collective-permute-start | bytes 1376264 | tf_op jit(solution)/shard_map/ppermute | solution.py:46
  190.2 13.6 %collective-permute-start.51 = (bf16[256,896]{1,0:T(8,128)(2,1)S(1)}, bf16[256,896]{1,0:T(8,128)(2,1)S(1)}, u32[]{:S(2)}, u32[]{:S(2)}) collective-permute-start(bf16[256,896]{1,0:T(8,128)(2,1)S(1)} %collective-permute-done.49.refs_4_), channel_id=1, source_target_pairs={{0,16},{8,24},{16,0},{24,8},{1,17},{9,25},{17,1},{25,9},{2,18},{10... | collective-permute-start | bytes 1376264 | tf_op jit(solution)/shard_map/ppermute | solution.py:46
  205.2 14.3 %collective-permute-start.54 = (bf16[144,3584]{1,0:T(8,128)(2,1)S(1)}, bf16[144,3584]{1,0:T(8,128)(2,1)S(1)}, u32[]{:S(2)}, u32[]{:S(2)}) collective-permute-start(bf16[144,3584]{1,0:T(8,128)(2,1)S(1)} %get-tuple-element.127), channel_id=1, source_target_pairs={{0,1},{1,0},{2,3},{3,2},{4,5},{5,4},{6,7},{7,6},{8,9},{9,8},{10,11... | collective-permute-start | bytes 3096584 | tf_op jit(solution)/shard_map/ppermute | solution.py:51
  205.2 14.3 %collective-permute-start.55 = (bf16[144,3584]{1,0:T(8,128)(2,1)S(1)}, bf16[144,3584]{1,0:T(8,128)(2,1)S(1)}, u32[]{:S(2)}, u32[]{:S(2)}) collective-permute-start(bf16[144,3584]{1,0:T(8,128)(2,1)S(1)} %get-tuple-element.128), channel_id=1, source_target_pairs={{0,1},{1,0},{2,3},{3,2},{4,5},{5,4},{6,7},{7,6},{8,9},{9,8},{10,11... | collective-permute-start | bytes 3096584 | tf_op jit(solution)/shard_map/ppermute | solution.py:51
  (73 other events, 1030.5 us)

commit v4 on v3

--- a/solution.py
+++ b/solution.py
@@ -11,11 +11,11 @@
 EXTRA = 16
 VMEM_LIMIT = 30 * 1024 * 1024
 PLAN_X = (
-    "a010", "a110 S0", "a020 a121", "k1", "k0", "a210", "r12", "a310", "a220 a321", "r11",
-    "k2", "r22", "k3", "r32", "r21", "r31", "r02", "r01",
+    "a010", "a110 S0", "a020 a121", "k1", "k0", "a210", "r11", "a310", "a220 a321",
+    "k2", "h1", "r22", "k3", "r32", "r21", "r31", "r02", "r01",
 )
 PLAN_E = (
-    "a010", "a110", "a020 a121", "a210", "d0", "d1", "a222", "a310 D0", "a322 D1", "d2", "d3",
+    "a010", "a022", "a110", "g1", "a310", "d0", "a210 D0", "d1", "a322", "a222 D1", "d3", "d2",
 )
 DEPTH = 2
 BF = jnp.bfloat16
@@ -51,9 +51,9 @@
     return lax.ppermute(x, "dp", [(i, i ^ 1) for i in range(n)])
 
 
-def along_ring(x):
+def along_ring(x, hops=1):
     n = lax.axis_size("dp")
-    return lax.ppermute(x, "dp", [(i, (i + 2) % n) for i in range(n)])
+    return lax.ppermute(x, "dp", [(i, (i + 2 * hops) % n) for i in range(n)])
 
 
 def gather_level(slots, count, mode):
@@ -437,13 +437,17 @@
 
     ring_e = [error]
     for t in range(1, nz):
-        ring_e.append(along_ring(ring_e[-1]))
+        if t == nz - 1 > 1:
+            ring_e.append(along_ring(error, nz - 1))
+        else:
+            ring_e.append(along_ring(ring_e[-1]))
+    codes = jnp.stack(codes)
+    which = pick(jnp.concatenate([codes, to_sibling(codes)]))[0][0]
+    metas[0], which = lax.optimization_barrier((metas[0], which))
     run(plan_e, [{0: [e]} for e in ring_e])
     own_terms = [results["D"][t] for t in range(nz)]
     sib_terms = [sib_terms[t] for t in range(nz)]
 
-    codes = jnp.stack(codes)
-    which = pick(jnp.concatenate([codes, to_sibling(codes)]))[0][0]
     terms = own_terms + sib_terms
     nt = len(terms)
     meta = jnp.concatenate([which, place])

time: 229 us -> 224 us (0.978)
  waiting for transfers between devices: 98.7 us -> 78.2 us
  starting transfers between devices: 61.3 us -> 69.9 us
  other arithmetic: 5.66 us -> 9.06 us
  local copies, waits for them, and re-layouts: 16 us -> 19.2 us
    ppermute x42 -> x40, waiting for transfers between devices: 77.5 us -> 55.8 us  [over_dict(): return lax.ppermute(x, 'dict', [(i, i ^ bit) for i in range(n)])]
    ppermute x9 -> x13, starting transfers between devices: 7.03 us -> 17.8 us  [along_ring(): return lax.ppermute(x, 'dp', [(i, (i + 2 * hops) % n) for i in range(n)])]
    unnamed x97 -> x119, local copies, waits for them, and re-layouts: 12.3 us -> 14.9 us
    ppermute x42 -> x40, starting transfers between devices: 48.3 us -> 46.6 us  [over_dict(): return lax.ppermute(x, 'dict', [(i, i ^ bit) for i in range(n)])]
    ppermute x9 -> x13, waiting for transfers between devices: 15.7 us -> 16.3 us  [along_ring(): return lax.ppermute(x, 'dp', [(i, (i + 2 * hops) % n) for i in range(n)])]
  transfers between devices with their start and end apart: 59 -> 61, of which waited for: 31 -> 20; matrix products, arithmetic and copies ran while one was open for 3% -> 5% of each run, Pallas kernels for 16% -> 16%
where the time goes in v4:
time: 224 us; the launch traced here: 223 us
  waiting for transfers between devices  78.2 us (35%)
  starting transfers between devices  69.9 us (31%)
  Pallas kernels  44.9 us (20%)
  local copies, waits for them, and re-layouts  19.2 us (9%)
  other arithmetic  9.06 us (4%)
    ppermute x40, waiting for transfers between devices, over_dict(): return lax.ppermute(x, 'dict', [(i, i ^ bit) for i in range(n)])  55.8 us
    ppermute x40, starting transfers between devices, over_dict(): return lax.ppermute(x, 'dict', [(i, i ^ bit) for i in range(n)])  46.6 us
    pallas_call x4, Pallas kernels, backward(): pl.pallas_call(functools.partial(bwd_kernel, xl, el, ns, fw), grid_spec=p...  19.4 us
    ppermute x13, starting transfers between devices, along_ring(): return lax.ppermute(x, 'dp', [(i, (i + 2 * hops) % n) for i in range(n)])  17.8 us
    pallas_call x4, Pallas kernels, forward(): pl.pallas_call(functools.partial(fwd_kernel, layout, ns, fw, out_layout),...  16.7 us
    ppermute x13, waiting for transfers between devices, along_ring(): return lax.ppermute(x, 'dp', [(i, (i + 2 * hops) % n) for i in range(n)])  16.3 us
    unnamed x119, local copies, waits for them, and re-layouts  14.9 us
    pallas_call x1, Pallas kernels, shards(): pl.pallas_call(functools.partial(sum_kernel, nt), grid_spec=pltpu.Prefetc...  8.83 us
  transfers between devices with their start and end apart: 61, of which 20 were waited for; matrix products, arithmetic and copies ran while one was open for 5% of the time, Pallas kernels for 16%

profile of v4, /device:TPU:0, one launch (start us, length us, event | category | flops | bytes accessed | tf_op | source)
XLA Modules:
  0.0 222.8 jit_solution(6326004558576843907)
XLA Ops:
  1.2 2.6 %collective-permute-start.5 = (bf16[256,896]{1,0:T(8,128)(2,1)}, bf16[256,896]{1,0:T(8,128)(2,1)S(1)}, u32[]{:S(2)}, u32[]{:S(2)}) collective-permute-start(bf16[256,896]{1,0:T(8,128)(2,1)} %refs_0_.3), channel_id=1, source_target_pairs={{0,2},{1,3},{2,4},{3,5},{4,6},{5,7},{6,0},{7,1},{8,10},{9,11},{10,... | collective-permute-start | bytes 1376264 | tf_op jit(solution)/shard_map/ppermute | solution.py:56
  7.4 3.9 %all-to-all-start = ((s32[8,2,8]{2,1,0:T(2,128)}), s32[8,2,8]{2,1,0:T(2,128)S(1)}, u32[]{:S(2)}, u32[]{:S(2)}) async-start(s32[8,2,8]{2,1,0:T(2,128)} %broadcast_in_dim.34), calls=%async_computation | async-start | bytes 16384 | tf_op jit(solution)/shard_map/all_to_all | solution.py:224
  13.5 3.9 %all-to-all-done = s32[8,2,8]{2,1,0:T(2,128)S(1)} async-done(((s32[8,2,8]{2,1,0:T(2,128)}), s32[8,2,8]{2,1,0:T(2,128)S(1)}, u32[]{:S(2)}, u32[]{:S(2)}) %all-to-all-start) | async-done | bytes 544 | tf_op jit(solution)/shard_map/all_to_all | solution.py:224
  23.5 7.6 %collective-permute-done.8.refs_2_ = bf16[256,896]{1,0:T(8,128)(2,1)S(1)} collective-permute-done((bf16[256,896]{1,0:T(8,128)(2,1)S(1)}, bf16[256,896]{1,0:T(8,128)(2,1)S(1)}, u32[]{:S(2)}, u32[]{:S(2)}) %collective-permute-start.8) | collective-permute-done | bytes 458784 | tf_op jit(solution)/shard_map/ppermute | solution.py:46
  34.5 2.1 collective-permute-done.6.refs_0_
  37.7 6.9 %collective-permute-done.11.refs_3_ = bf16[256,896]{1,0:T(8,128)(2,1)S(1)} collective-permute-done((bf16[256,896]{1,0:T(8,128)(2,1)S(1)}, bf16[256,896]{1,0:T(8,128)(2,1)S(1)}, u32[]{:S(2)}, u32[]{:S(2)}) %collective-permute-start.11) | collective-permute-done | bytes 458784 | tf_op jit(solution)/shard_map/ppermute | solution.py:46
  44.9 3.1 %copy-done.2 = bf16[1024,3584]{1,0:T(8,128)(2,1)S(1)} copy-done((bf16[1024,3584]{1,0:T(8,128)(2,1)S(1)}, bf16[1024,3584]{1,0:T(8,128)(2,1)}, u32[]{:S(2)}) %copy-start.2) | copy-done | bytes 7340056
  48.0 4.3 %shard_map.77 = (bf16[256,256]{1,0:T(8,128)(2,1)S(1)}, f32[256,896]{1,0:T(8,128)S(1)}, f32[256,896]{1,0:T(8,128)S(1)}, f32[256,896]{1,0:T(8,128)S(1)}, bf16[128,...) custom-call(s32[10]{0:T(128)S(1)} %get-tuple-element.145.meta, bf16[256,896]{1,0:T(8,128)(2,1)S(1)} %collective-permute-done.5.refs_0_, ...), custom_call_target="tpu_custom_call" | custom-call | flops 939524096 | bytes 7340032 | tf_op jit(solution)/shard_map/pallas_call | solution.py:309
  57.7 8.3 %collective-permute-done.13 = bf16[256,896]{1,0:T(8,128)(2,1)S(1)} collective-permute-done((bf16[256,896]{1,0:T(8,128)(2,1)S(1)}, bf16[256,896]{1,0:T(8,128)(2,1)S(1)}, u32[]{:S(2)}, u32[]{:S(2)}) %collective-permute-start.13) | collective-permute-done | bytes 458784 | tf_op jit(solution)/shard_map/ppermute | solution.py:46
  71.6 4.1 %shard_map.76 = (bf16[256,256]{1,0:T(8,128)(2,1)S(1)}, f32[256,896]{1,0:T(8,128)S(1)}, f32[256,896]{1,0:T(8,128)S(1)}, f32[256,896]{1,0:T(8,128)S(1)}, bf16[128,...) custom-call(s32[10]{0:T(128)S(1)} %get-tuple-element.109.meta, bf16[256,896]{1,0:T(8,128)(2,1)S(1)} %copy-done.5, ...), custom_call_target="tpu_custom_call" | custom-call | flops 939524096 | bytes 7340032 | tf_op jit(solution)/shard_map/pallas_call | solution.py:309
  77.9 5.6 %collective-permute-done.14.refs_3_ = bf16[256,896]{1,0:T(8,128)(2,1)S(1)} collective-permute-done((bf16[256,896]{1,0:T(8,128)(2,1)S(1)}, bf16[256,896]{1,0:T(8,128)(2,1)S(1)}, u32[]{:S(2)}, u32[]{:S(2)}) %collective-permute-start.14) | collective-permute-done | bytes 458784 | tf_op jit(solution)/shard_map/ppermute | solution.py:46
  83.5 4.1 %shard_map.78 = (bf16[256,256]{1,0:T(8,128)(2,1)S(1)}, f32[256,896]{1,0:T(8,128)S(1)}, f32[256,896]{1,0:T(8,128)S(1)}, f32[256,896]{1,0:T(8,128)S(1)}, f32[128,896]{1,0:T(8,128)S(1)}, /*index=5*/f32[128,896]{1,0:T(8,128)S(1)}) custom-call(s32[10]{0:T(128)S(1)} %get-tuple-element.146.meta, bf16[256,896]{1,0:T(8,128)(2,1)S(1)} %collective-permute-done.6.refs_0_, ...), custom_call_target="tpu_custom_call" | custom-call | flops 939524096 | bytes 7340032 | tf_op jit(solution)/shard_map/pallas_call | solution.py:309
  91.1 4.1 %shard_map.79 = (bf16[256,256]{1,0:T(8,128)(2,1)S(1)}, f32[256,896]{1,0:T(8,128)S(1)}, f32[256,896]{1,0:T(8,128)S(1)}, f32[256,896]{1,0:T(8,128)S(1)}, bf16[128,...) custom-call(s32[10]{0:T(128)S(1)} %get-tuple-element.144.meta, bf16[256,896]{1,0:T(8,128)(2,1)S(1)} %collective-permute-done.16.refs_0_, ...), custom_call_target="tpu_custom_call" | custom-call | flops 939524096 | bytes 7340032 | tf_op jit(solution)/shard_map/pallas_call | solution.py:309
  99.7 4.1 %collective-permute-done.27 = bf16[128,896]{1,0:T(8,128)(2,1)S(1)} collective-permute-done((bf16[128,896]{1,0:T(8,128)(2,1)S(1)}, bf16[128,896]{1,0:T(8,128)(2,1)S(1)}, u32[]{:S(2)}, u32[]{:S(2)}) %collective-permute-start.27) | collective-permute-done | bytes 229408 | tf_op jit(solution)/shard_map/ppermute | solution.py:46
  106.7 8.5 %collective-permute-done.23 = bf16[256,896]{1,0:T(8,128)(2,1)S(1)} collective-permute-done((bf16[256,896]{1,0:T(8,128)(2,1)S(1)}, bf16[256,896]{1,0:T(8,128)(2,1)S(1)}, u32[]{:S(2)}, u32[]{:S(2)}) %collective-permute-start.23) | collective-permute-done | bytes 458784 | tf_op jit(solution)/shard_map/ppermute | solution.py:46
  118.2 7.0 %collective-permute-done.31 = bf16[128,896]{1,0:T(8,128)(2,1)S(1)} collective-permute-done((bf16[128,896]{1,0:T(8,128)(2,1)S(1)}, bf16[128,896]{1,0:T(8,128)(2,1)S(1)}, u32[]{:S(2)}, u32[]{:S(2)}) %collective-permute-start.31) | collective-permute-done | bytes 229408 | tf_op jit(solution)/shard_map/ppermute | solution.py:46
  129.4 2.1 collective-permute-start.35
  132.3 3.6 %collective-permute-done.32 = bf16[256,896]{1,0:T(8,128)(2,1)} collective-permute-done((bf16[256,896]{1,0:T(8,128)(2,1)}, bf16[256,896]{1,0:T(8,128)(2,1)}, u32[]{:S(2)}, u32[]{:S(2)}) %collective-permute-start.32) | collective-permute-done | bytes 458784 | tf_op jit(solution)/shard_map/ppermute | solution.py:46
  136.8 3.2 %collective-permute-done.35 = bf16[256,896]{1,0:T(8,128)(2,1)} collective-permute-done((bf16[256,896]{1,0:T(8,128)(2,1)}, bf16[256,896]{1,0:T(8,128)(2,1)}, u32[]{:S(2)}, u32[]{:S(2)}) %collective-permute-start.35) | collective-permute-done | bytes 458784 | tf_op jit(solution)/shard_map/ppermute | solution.py:56
  140.0 2.0 subtract_convert_fusion.refs_4_
  146.3 2.6 %collective-permute-start.51 = (bf16[256,896]{1,0:T(8,128)(2,1)S(1)}, bf16[256,896]{1,0:T(8,128)(2,1)S(1)}, u32[]{:S(2)}, u32[]{:S(2)}) collective-permute-start(bf16[256,896]{1,0:T(8,128)(2,1)S(1)} %subtract_convert_fusion.refs_4_), channel_id=1, source_target_pairs={{0,6},{1,7},{2,0},{3,1},{4,2},{5,3},{6,4},{7,5},{8,14},{9,15},{10,... | collective-permute-start | bytes 1376264 | tf_op jit(solution)/shard_map/ppermute | solution.py:56
  155.1 4.3 %collective-permute-done.41.refs_4_ = bf16[256,896]{1,0:T(8,128)(2,1)S(1)} collective-permute-done((bf16[256,896]{1,0:T(8,128)(2,1)S(1)}, bf16[256,896]{1,0:T(8,128)(2,1)S(1)}, u32[]{:S(2)}, u32[]{:S(2)}) %collective-permute-start.41) | collective-permute-done | bytes 458784 | tf_op jit(solution)/shard_map/ppermute | solution.py:56
  160.1 2.2 collective-permute-done.51.refs_4_
  165.2 2.1 collective-permute-start.53
  167.3 3.1 %copy-done.4 = bf16[1024,3584]{1,0:T(8,128)(2,1)S(1)} copy-done((bf16[1024,3584]{1,0:T(8,128)(2,1)S(1)}, bf16[1024,3584]{1,0:T(8,128)(2,1)}, u32[]{:S(2)}) %copy-start.4) | copy-done | bytes 7340056
  176.0 5.1 %shard_map.80 = (bf16[144,3584]{1,0:T(8,128)(2,1)S(1)}, bf16[144,3584]{1,0:T(8,128)(2,1)S(1)}) custom-call(s32[10]{0:T(128)S(1)} %copy-done.50, bf16[256,896]{1,0:T(8,128)(2,1)S(1)} %copy-done.6, bf16[256,896]{1,0:T(8,128)(2,1)S(1)} %copy-done.10, bf16[256,896]{1,0:T(8,128)(2,1)S(1)} %copy-done.12, bf16[256,896]{1,0:T(8,128)(2,1)S(1)} %copy-done.34, ...), custom_call_target="tpu_custom_call" | custom-call | flops 1409286144 | bytes 9175040 | tf_op jit(solution)/shard_map/pallas_call | solution.py:342
  181.4 3.7 %collective-permute-start.44 = (bf16[128,896]{1,0:T(8,128)(2,1)S(1)}, bf16[128,896]{1,0:T(8,128)(2,1)S(1)}, u32[]{:S(2)}, u32[]{:S(2)}) collective-permute-start(bf16[128,896]{1,0:T(8,128)(2,1)S(1)} %collective-permute-done.39.refs_7_), channel_id=1, source_target_pairs={{0,2},{1,3},{2,4},{3,5},{4,6},{5,7},{6,0},{7,1},{8,10},{9,11},{10,... | collective-permute-start | bytes 688136 | tf_op jit(solution)/shard_map/ppermute | solution.py:56
  193.0 4.8 %shard_map.81 = (bf16[144,3584]{1,0:T(8,128)(2,1)S(1)}, bf16[144,3584]{1,0:T(8,128)(2,1)S(1)}) custom-call(s32[10]{0:T(128)S(1)} %copy-done.48, bf16[256,896]{1,0:T(8,128)(2,1)S(1)} %copy-done.8, bf16[256,896]{1,0:T(8,128)(2,1)S(1)} %copy-done.22, bf16[256,896]{1,0:T(8,128)(2,1)S(1)} %copy-done.20, bf16[256,896]{1,0:T(8,128)(2,1)S(1)} %copy-done.24, ...), custom_call_target="tpu_custom_call" | custom-call | flops 1409286144 | bytes 9175040 | tf_op jit(solution)/shard_map/pallas_call | solution.py:342
  201.4 4.8 %shard_map.83 = (bf16[144,3584]{1,0:T(8,128)(2,1)S(1)}, bf16[144,3584]{1,0:T(8,128)(2,1)S(1)}) custom-call(s32[10]{0:T(128)S(1)} %copy-done.46, bf16[256,896]{1,0:T(8,128)(2,1)S(1)} %copy-done.26, bf16[256,896]{1,0:T(8,128)(2,1)S(1)} %copy-done.32, bf16[256,896]{1,0:T(8,128)(2,1)S(1)} %copy-done.30, bf16[256,896]{1,0:T(8,128)(2,1)S(1)} %copy-done.36, ...), custom_call_target="tpu_custom_call" | custom-call | flops 1409286144 | bytes 9175040 | tf_op jit(solution)/shard_map/pallas_call | solution.py:342
  206.3 4.8 %shard_map.82 = (bf16[144,3584]{1,0:T(8,128)(2,1)S(1)}, bf16[144,3584]{1,0:T(8,128)(2,1)S(1)}) custom-call(s32[10]{0:T(128)S(1)} %copy-done.44, bf16[256,896]{1,0:T(8,128)(2,1)S(1)} %copy-done.14, bf16[256,896]{1,0:T(8,128)(2,1)S(1)} %copy-done.16, bf16[256,896]{1,0:T(8,128)(2,1)S(1)} %copy-done.18, bf16[256,896]{1,0:T(8,128)(2,1)S(1)} %copy-done.28, ...), custom_call_target="tpu_custom_call" | custom-call | flops 1409286144 | bytes 9175040 | tf_op jit(solution)/shard_map/pallas_call | solution.py:342
  211.8 2.2 collective-permute-done.58.refs_6_.refs_14_
  213.9 8.8 %shard_map.84 = (f32[8,128,3584]{2,1,0:T(8,128)}, f32[8,1,128]{2,1,0:T(1,128)}) custom-call(s32[12]{0:T(128)S(1)} %pad_add_fusion.2.meta, bf16[144,3584]{1,0:T(8,128)(2,1)S(1)} %get-tuple-element.111.refs_0_.refs_8_, bf16[144,3584]{1,0:T(8,128)(2,1)S(1)} %get-tuple-element.114.refs_1_.refs_9_, bf16[144,3584]{1,0:T(8,128)(2,1)S(1)} %get-tuple-element.119.refs_2_.refs_10_, ...), custom_call_target="tpu_custom_call" | custom-call | flops 3670016 | bytes 22020096 | tf_op jit(solution)/shard_map/pallas_call | solution.py:454
  (269 shorter events, 81.6 us)
Async XLA Ops:
  0.6 44.3 %collective-permute-start.3 = (bf16[8,128,3584]{2,1,0:T(8,128)(2,1)}, bf16[8,128,3584]{2,1,0:T(8,128)(2,1)}, u32[]{:S(2)}, u32[]{:S(2)}) collective-permute-start(bf16[8,128,3584]{2,1,0:T(8,128)(2,1)} %bitcast.27), channel_id=1, source_target_pairs={{0,1},{1,0},{2,3},{3,2},{4,5},{5,4},{6,7},{7,6},{8,9},{9,8},{10,11... | collective-permute-start | bytes 22020104 | tf_op jit(solution)/shard_map/ppermute | solution.py:51
  1.2 17.4 %collective-permute-start.5 = (bf16[256,896]{1,0:T(8,128)(2,1)}, bf16[256,896]{1,0:T(8,128)(2,1)S(1)}, u32[]{:S(2)}, u32[]{:S(2)}) collective-permute-start(bf16[256,896]{1,0:T(8,128)(2,1)} %refs_0_.3), channel_id=1, source_target_pairs={{0,2},{1,3},{2,4},{3,5},{4,6},{5,7},{6,0},{7,1},{8,10},{9,11},{10,... | collective-permute-start | bytes 1376264 | tf_op jit(solution)/shard_map/ppermute | solution.py:56
  3.8 14.8 %collective-permute-start = (bf16[256,896]{1,0:T(8,128)(2,1)}, bf16[256,896]{1,0:T(8,128)(2,1)S(1)}, u32[]{:S(2)}, u32[]{:S(2)}) collective-permute-start(bf16[256,896]{1,0:T(8,128)(2,1)} %refs_0_.3), channel_id=1, source_target_pairs={{0,8},{8,0},{16,24},{24,16},{1,9},{9,1},{17,25},{25,17},{2,10},{10... | collective-permute-start | bytes 1376264 | tf_op jit(solution)/shard_map/ppermute | solution.py:46
  5.3 13.3 %collective-permute-start.1 = (bf16[256,896]{1,0:T(8,128)(2,1)}, bf16[256,896]{1,0:T(8,128)(2,1)S(1)}, u32[]{:S(2)}, u32[]{:S(2)}) collective-permute-start(bf16[256,896]{1,0:T(8,128)(2,1)} %refs_0_.3), channel_id=1, source_target_pairs={{0,16},{8,24},{16,0},{24,8},{1,17},{9,25},{17,1},{25,9},{2,18},{10... | collective-permute-start | bytes 1376264 | tf_op jit(solution)/shard_map/ppermute | solution.py:46
  21.2 13.3 %collective-permute-start.7 = (bf16[256,896]{1,0:T(8,128)(2,1)S(1)}, bf16[256,896]{1,0:T(8,128)(2,1)S(1)}, u32[]{:S(2)}, u32[]{:S(2)}) collective-permute-start(bf16[256,896]{1,0:T(8,128)(2,1)S(1)} %collective-permute-done.5.refs_0_), channel_id=1, source_target_pairs={{0,8},{8,0},{16,24},{24,16},{1,9},{9,1},{17,25},{25,17},{2,10},{10... | collective-permute-start | bytes 1376264 | tf_op jit(solution)/shard_map/ppermute | solution.py:46
  22.9 13.7 %collective-permute-start.6 = (bf16[256,896]{1,0:T(8,128)(2,1)S(1)}, bf16[256,896]{1,0:T(8,128)(2,1)S(1)}, u32[]{:S(2)}, u32[]{:S(2)}) collective-permute-start(bf16[256,896]{1,0:T(8,128)(2,1)S(1)} %collective-permute-done.5.refs_0_), channel_id=1, source_target_pairs={{0,2},{1,3},{2,4},{3,5},{4,6},{5,7},{6,0},{7,1},{8,10},{9,11},{10,... | collective-permute-start | bytes 1376264 | tf_op jit(solution)/shard_map/ppermute | solution.py:56
  31.1 13.5 %collective-permute-start.11 = (bf16[256,896]{1,0:T(8,128)(2,1)S(1)}, bf16[256,896]{1,0:T(8,128)(2,1)S(1)}, u32[]{:S(2)}, u32[]{:S(2)}) collective-permute-start(bf16[256,896]{1,0:T(8,128)(2,1)S(1)} %collective-permute-done.8.refs_2_), channel_id=1, source_target_pairs={{0,8},{8,0},{16,24},{24,16},{1,9},{9,1},{17,25},{25,17},{2,10},{10... | collective-permute-start | bytes 1376264 | tf_op jit(solution)/shard_map/ppermute | solution.py:46
  32.8 19.7 %collective-permute-start.2 = (bf16[256,896]{1,0:T(8,128)(2,1)S(1)}, bf16[256,896]{1,0:T(8,128)(2,1)S(1)}, u32[]{:S(2)}, u32[]{:S(2)}) collective-permute-start(bf16[256,896]{1,0:T(8,128)(2,1)S(1)} %collective-permute-done.refs_1_), channel_id=1, source_target_pairs={{0,16},{8,24},{16,0},{24,8},{1,17},{9,25},{17,1},{25,9},{2,18},{10... | collective-permute-start | bytes 1376264 | tf_op jit(solution)/shard_map/ppermute | solution.py:46
  36.7 19.1 %collective-permute-start.9 = (bf16[256,896]{1,0:T(8,128)(2,1)S(1)}, bf16[256,896]{1,0:T(8,128)(2,1)S(1)}, u32[]{:S(2)}, u32[]{:S(2)}) collective-permute-start(bf16[256,896]{1,0:T(8,128)(2,1)S(1)} %collective-permute-done.6.refs_0_), channel_id=1, source_target_pairs={{0,8},{8,0},{16,24},{24,16},{1,9},{9,1},{17,25},{25,17},{2,10},{10... | collective-permute-start | bytes 1376264 | tf_op jit(solution)/shard_map/ppermute | solution.py:46
  37.2 18.5 %collective-permute-start.10 = (bf16[256,896]{1,0:T(8,128)(2,1)S(1)}, bf16[256,896]{1,0:T(8,128)(2,1)S(1)}, u32[]{:S(2)}, u32[]{:S(2)}) collective-permute-start(bf16[256,896]{1,0:T(8,128)(2,1)S(1)} %collective-permute-done.6.refs_0_), channel_id=1, source_target_pairs={{0,16},{8,24},{16,0},{24,8},{1,17},{9,25},{17,1},{25,9},{2,18},{10... | collective-permute-start | bytes 1376264 | tf_op jit(solution)/shard_map/ppermute | solution.py:46
  52.5 13.5 %collective-permute-start.13 = (bf16[256,896]{1,0:T(8,128)(2,1)S(1)}, bf16[256,896]{1,0:T(8,128)(2,1)S(1)}, u32[]{:S(2)}, u32[]{:S(2)}) collective-permute-start(bf16[256,896]{1,0:T(8,128)(2,1)S(1)} %convert_element_type.105), channel_id=1, source_target_pairs={{0,16},{8,24},{16,0},{24,8},{1,17},{9,25},{17,1},{25,9},{2,18},{10... | collective-permute-start | bytes 1376264 | tf_op jit(solution)/shard_map/ppermute | solution.py:46
  56.2 21.1 %collective-permute-start.18 = (bf16[256,896]{1,0:T(8,128)(2,1)S(1)}, bf16[256,896]{1,0:T(8,128)(2,1)S(1)}, u32[]{:S(2)}, u32[]{:S(2)}) collective-permute-start(bf16[256,896]{1,0:T(8,128)(2,1)S(1)} %collective-permute-done.16.refs_0_), channel_id=1, source_target_pairs={{0,16},{8,24},{16,0},{24,8},{1,17},{9,25},{17,1},{25,9},{2,18},{10... | collective-permute-start | bytes 1376264 | tf_op jit(solution)/shard_map/ppermute | solution.py:46
  66.0 17.4 %collective-permute-start.14 = (bf16[256,896]{1,0:T(8,128)(2,1)S(1)}, bf16[256,896]{1,0:T(8,128)(2,1)S(1)}, u32[]{:S(2)}, u32[]{:S(2)}) collective-permute-start(bf16[256,896]{1,0:T(8,128)(2,1)S(1)} %collective-permute-done.9.refs_1_), channel_id=1, source_target_pairs={{0,16},{8,24},{16,0},{24,8},{1,17},{9,25},{17,1},{25,9},{2,18},{10... | collective-permute-start | bytes 1376264 | tf_op jit(solution)/shard_map/ppermute | solution.py:46
  67.6 20.1 %collective-permute-start.20 = (bf16[128,896]{1,0:T(8,128)(2,1)S(1)}, bf16[128,896]{1,0:T(8,128)(2,1)S(1)}, u32[]{:S(2)}, u32[]{:S(2)}) collective-permute-start(bf16[128,896]{1,0:T(8,128)(2,1)S(1)} %get-tuple-element.85), channel_id=1, source_target_pairs={{0,2},{1,3},{2,4},{3,5},{4,6},{5,7},{6,0},{7,1},{8,10},{9,11},{10,... | collective-permute-start | bytes 688136 | tf_op jit(solution)/shard_map/ppermute | solution.py:56
  68.6 19.1 %collective-permute-start.15 = (bf16[128,896]{1,0:T(8,128)(2,1)S(1)}, bf16[128,896]{1,0:T(8,128)(2,1)S(1)}, u32[]{:S(2)}, u32[]{:S(2)}) collective-permute-start(bf16[128,896]{1,0:T(8,128)(2,1)S(1)} %get-tuple-element.81), channel_id=1, source_target_pairs={{0,2},{1,3},{2,4},{3,5},{4,6},{5,7},{6,0},{7,1},{8,10},{9,11},{10,... | collective-permute-start | bytes 688136 | tf_op jit(solution)/shard_map/ppermute | solution.py:56
  70.1 17.7 %collective-permute-start.17 = (bf16[256,896]{1,0:T(8,128)(2,1)S(1)}, bf16[256,896]{1,0:T(8,128)(2,1)S(1)}, u32[]{:S(2)}, u32[]{:S(2)}) collective-permute-start(bf16[256,896]{1,0:T(8,128)(2,1)S(1)} %collective-permute-done.16.refs_0_), channel_id=1, source_target_pairs={{0,8},{8,0},{16,24},{24,16},{1,9},{9,1},{17,25},{25,17},{2,10},{10... | collective-permute-start | bytes 1376264 | tf_op jit(solution)/shard_map/ppermute | solution.py:46
  77.3 13.0 %collective-permute-start.25 = (bf16[256,896]{1,0:T(8,128)(2,1)S(1)}, bf16[256,896]{1,0:T(8,128)(2,1)S(1)}, u32[]{:S(2)}, u32[]{:S(2)}) collective-permute-start(bf16[256,896]{1,0:T(8,128)(2,1)S(1)} %collective-permute-done.18.refs_2_), channel_id=1, source_target_pairs={{0,8},{8,0},{16,24},{24,16},{1,9},{9,1},{17,25},{25,17},{2,10},{10... | collective-permute-start | bytes 1376264 | tf_op jit(solution)/shard_map/ppermute | solution.py:46
  88.5 27.2 %collective-permute-start.33 = (bf16[256,896]{1,0:T(8,128)(2,1)S(1)}, bf16[256,896]{1,0:T(8,128)(2,1)S(1)}, u32[]{:S(2)}, u32[]{:S(2)}) collective-permute-start(bf16[256,896]{1,0:T(8,128)(2,1)S(1)} %add_convert_fusion.2), channel_id=1, source_target_pairs={{0,2},{1,3},{2,4},{3,5},{4,6},{5,7},{6,0},{7,1},{8,10},{9,11},{10,... | collective-permute-start | bytes 1376264 | tf_op jit(solution)/shard_map/ppermute | solution.py:56
  97.4 17.8 %collective-permute-start.23 = (bf16[256,896]{1,0:T(8,128)(2,1)S(1)}, bf16[256,896]{1,0:T(8,128)(2,1)S(1)}, u32[]{:S(2)}, u32[]{:S(2)}) collective-permute-start(bf16[256,896]{1,0:T(8,128)(2,1)S(1)} %add_convert_fusion.7), channel_id=1, source_target_pairs={{0,16},{8,24},{16,0},{24,8},{1,17},{9,25},{17,1},{25,9},{2,18},{10... | collective-permute-start | bytes 1376264 | tf_op jit(solution)/shard_map/ppermute | solution.py:46
  99.1 16.1 %collective-permute-start.22 = (bf16[256,896]{1,0:T(8,128)(2,1)S(1)}, bf16[256,896]{1,0:T(8,128)(2,1)S(1)}, u32[]{:S(2)}, u32[]{:S(2)}) collective-permute-start(bf16[256,896]{1,0:T(8,128)(2,1)S(1)} %add_convert_fusion.8), channel_id=1, source_target_pairs={{0,8},{8,0},{16,24},{24,16},{1,9},{9,1},{17,25},{25,17},{2,10},{10... | collective-permute-start | bytes 1376264 | tf_op jit(solution)/shard_map/ppermute | solution.py:46
  105.4 20.7 %collective-permute-start.29 = (bf16[256,896]{1,0:T(8,128)(2,1)S(1)}, bf16[256,896]{1,0:T(8,128)(2,1)S(1)}, u32[]{:S(2)}, u32[]{:S(2)}) collective-permute-start(bf16[256,896]{1,0:T(8,128)(2,1)S(1)} %add_convert_fusion.4), channel_id=1, source_target_pairs={{0,16},{8,24},{16,0},{24,8},{1,17},{9,25},{17,1},{25,9},{2,18},{10... | collective-permute-start | bytes 1376264 | tf_op jit(solution)/shard_map/ppermute | solution.py:46
  105.9 20.2 %collective-permute-start.28 = (bf16[256,896]{1,0:T(8,128)(2,1)S(1)}, bf16[256,896]{1,0:T(8,128)(2,1)S(1)}, u32[]{:S(2)}, u32[]{:S(2)}) collective-permute-start(bf16[256,896]{1,0:T(8,128)(2,1)S(1)} %add_convert_fusion.5), channel_id=1, source_target_pairs={{0,8},{8,0},{16,24},{24,16},{1,9},{9,1},{17,25},{25,17},{2,10},{10... | collective-permute-start | bytes 1376264 | tf_op jit(solution)/shard_map/ppermute | solution.py:46
  145.1 14.3 %collective-permute-start.41 = (bf16[256,896]{1,0:T(8,128)(2,1)S(1)}, bf16[256,896]{1,0:T(8,128)(2,1)S(1)}, u32[]{:S(2)}, u32[]{:S(2)}) collective-permute-start(bf16[256,896]{1,0:T(8,128)(2,1)S(1)} %subtract_convert_fusion.refs_4_), channel_id=1, source_target_pairs={{0,2},{1,3},{2,4},{3,5},{4,6},{5,7},{6,0},{7,1},{8,10},{9,11},{10,... | collective-permute-start | bytes 1376264 | tf_op jit(solution)/shard_map/ppermute | solution.py:56
  146.3 16.1 %collective-permute-start.51 = (bf16[256,896]{1,0:T(8,128)(2,1)S(1)}, bf16[256,896]{1,0:T(8,128)(2,1)S(1)}, u32[]{:S(2)}, u32[]{:S(2)}) collective-permute-start(bf16[256,896]{1,0:T(8,128)(2,1)S(1)} %subtract_convert_fusion.refs_4_), channel_id=1, source_target_pairs={{0,6},{1,7},{2,0},{3,1},{4,2},{5,3},{6,4},{7,5},{8,14},{9,15},{10,... | collective-permute-start | bytes 1376264 | tf_op jit(solution)/shard_map/ppermute | solution.py:56
  159.4 21.7 %collective-permute-start.42 = (bf16[256,896]{1,0:T(8,128)(2,1)S(1)}, bf16[256,896]{1,0:T(8,128)(2,1)S(1)}, u32[]{:S(2)}, u32[]{:S(2)}) collective-permute-start(bf16[256,896]{1,0:T(8,128)(2,1)S(1)} %collective-permute-done.41.refs_4_), channel_id=1, source_target_pairs={{0,8},{8,0},{16,24},{24,16},{1,9},{9,1},{17,25},{25,17},{2,10},{10... | collective-permute-start | bytes 1376264 | tf_op jit(solution)/shard_map/ppermute | solution.py:46
  159.8 21.3 %collective-permute-start.43 = (bf16[256,896]{1,0:T(8,128)(2,1)S(1)}, bf16[256,896]{1,0:T(8,128)(2,1)S(1)}, u32[]{:S(2)}, u32[]{:S(2)}) collective-permute-start(bf16[256,896]{1,0:T(8,128)(2,1)S(1)} %collective-permute-done.41.refs_4_), channel_id=1, source_target_pairs={{0,16},{8,24},{16,0},{24,8},{1,17},{9,25},{17,1},{25,9},{2,18},{10... | collective-permute-start | bytes 1376264 | tf_op jit(solution)/shard_map/ppermute | solution.py:46
  162.4 18.8 %collective-permute-start.46 = (bf16[256,896]{1,0:T(8,128)(2,1)S(1)}, bf16[256,896]{1,0:T(8,128)(2,1)S(1)}, u32[]{:S(2)}, u32[]{:S(2)}) collective-permute-start(bf16[256,896]{1,0:T(8,128)(2,1)S(1)} %collective-permute-done.41.refs_4_), channel_id=1, source_target_pairs={{0,2},{1,3},{2,4},{3,5},{4,6},{5,7},{6,0},{7,1},{8,10},{9,11},{10,... | collective-permute-start | bytes 1376264 | tf_op jit(solution)/shard_map/ppermute | solution.py:56
  162.5 22.6 %collective-permute-start.52 = (bf16[256,896]{1,0:T(8,128)(2,1)S(1)}, bf16[256,896]{1,0:T(8,128)(2,1)S(1)}, u32[]{:S(2)}, u32[]{:S(2)}) collective-permute-start(bf16[256,896]{1,0:T(8,128)(2,1)S(1)} %collective-permute-done.51.refs_4_), channel_id=1, source_target_pairs={{0,8},{8,0},{16,24},{24,16},{1,9},{9,1},{17,25},{25,17},{2,10},{10... | collective-permute-start | bytes 1376264 | tf_op jit(solution)/shard_map/ppermute | solution.py:46
  165.2 20.3 %collective-permute-start.53 = (bf16[256,896]{1,0:T(8,128)(2,1)S(1)}, bf16[256,896]{1,0:T(8,128)(2,1)S(1)}, u32[]{:S(2)}, u32[]{:S(2)}) collective-permute-start(bf16[256,896]{1,0:T(8,128)(2,1)S(1)} %collective-permute-done.51.refs_4_), channel_id=1, source_target_pairs={{0,16},{8,24},{16,0},{24,8},{1,17},{9,25},{17,1},{25,9},{2,18},{10... | collective-permute-start | bytes 1376264 | tf_op jit(solution)/shard_map/ppermute | solution.py:46
  181.1 16.7 %collective-permute-start.47 = (bf16[256,896]{1,0:T(8,128)(2,1)S(1)}, bf16[256,896]{1,0:T(8,128)(2,1)S(1)}, u32[]{:S(2)}, u32[]{:S(2)}) collective-permute-start(bf16[256,896]{1,0:T(8,128)(2,1)S(1)} %collective-permute-done.46.refs_4_), channel_id=1, source_target_pairs={{0,8},{8,0},{16,24},{24,16},{1,9},{9,1},{17,25},{25,17},{2,10},{10... | collective-permute-start | bytes 1376264 | tf_op jit(solution)/shard_map/ppermute | solution.py:46
  181.2 16.7 %collective-permute-start.48 = (bf16[256,896]{1,0:T(8,128)(2,1)S(1)}, bf16[256,896]{1,0:T(8,128)(2,1)S(1)}, u32[]{:S(2)}, u32[]{:S(2)}) collective-permute-start(bf16[256,896]{1,0:T(8,128)(2,1)S(1)} %collective-permute-done.46.refs_4_), channel_id=1, source_target_pairs={{0,16},{8,24},{16,0},{24,8},{1,17},{9,25},{17,1},{25,9},{2,18},{10... | collective-permute-start | bytes 1376264 | tf_op jit(solution)/shard_map/ppermute | solution.py:46
  185.4 15.4 %collective-permute-start.54 = (bf16[128,896]{1,0:T(8,128)(2,1)S(1)}, bf16[128,896]{1,0:T(8,128)(2,1)S(1)}, u32[]{:S(2)}, u32[]{:S(2)}) collective-permute-start(bf16[128,896]{1,0:T(8,128)(2,1)S(1)} %slice.50), channel_id=1, source_target_pairs={{0,16},{8,24},{16,0},{24,8},{1,17},{9,25},{17,1},{25,9},{2,18},{10... | collective-permute-start | bytes 688136 | tf_op jit(solution)/shard_map/ppermute | solution.py:46
  (86 other events, 1252.7 us)
